TPU v7x, 32 devices: a whole 2x2x4 slice. The times are simulated.
32 devices in a mesh: seq: 4 (over x, core), fsdp: 8 (over z, y).
Axes of the slice: x: 2, y: 2, z: 4, core: 2. Of those that a mesh axis runs over, the one named last changes fastest.
Arguments:
- patches: bfloat16 [2, 32, 1536, 768], P(None, ('seq', 'fsdp')), may hold values from -6 to 6
- positions: int32 [2, 2, 32, 1536], P(None, None, ('seq', 'fsdp')), may hold values from 0 to 63
- lengths: int32 [2, 32, 2], P(None, ('seq', 'fsdp')), may hold values from 128 to 1152, as said below
- res_weights: int32 [2, 32, 2], P(None, ('seq', 'fsdp')), may hold values from 1 to 6
- labels: int32 [2, 32, 2], P(None, ('seq', 'fsdp')), may hold values from 0 to 999
- block_slot: int32 [13], replicated, may hold values from 0 to 15, as said below
- blocks: float32 [13, 768, 768], P(None, 'fsdp')
- pos_table: float32 [2, 64, 768], P(None, None, 'fsdp'), may hold values from -3 to 3
- gains: float32 [5, 768], P(None, 'fsdp')
- head: float32 [768, 1000], P('fsdp'), may hold values from -0.21875 to 0.21875
- left_stats: float32 [16, 768, 768], P('fsdp')
- right_stats: float32 [16, 768, 768], P('fsdp')
- left_roots: float32 [16, 768, 768], P('fsdp')
- right_roots: float32 [16, 768, 768], P('fsdp')
- pos_first: float32 [2, 64, 768], P(None, None, 'fsdp'), may hold values from -5.722046e-06 to 5.722046e-06
- pos_second: float32 [2, 64, 768], P(None, None, 'fsdp'), may hold values from 6.207647e-13 to 2.4596338e-12
- gain_first: float32 [5, 768], P(None, 'fsdp'), may hold values from -2.670288e-05 to 2.670288e-05
- gain_second: float32 [5, 768], P(None, 'fsdp'), may hold values from 1.5226305e-11 to 6.2076476e-11
- head_first: float32 [768, 1000], P('fsdp'), may hold values from -5.722046e-06 to 5.722046e-06
- head_second: float32 [768, 1000], P('fsdp'), may hold values from 6.207647e-13 to 2.4596338e-12
Outputs:
- blocks_new: float32 [13, 768, 768], P(None, 'fsdp')
- block_grads: float32 [13, 768, 768], P(None, 'fsdp')
- left_new: float32 [16, 768, 768], P('fsdp')
- right_new: float32 [16, 768, 768], P('fsdp')
- pos_new: float32 [2, 64, 768], P(None, None, 'fsdp')
- pos_first_new: float32 [2, 64, 768], P(None, None, 'fsdp')
- pos_second_new: float32 [2, 64, 768], P(None, None, 'fsdp')
- gains_new: float32 [5, 768], P(None, 'fsdp')
- gain_first_new: float32 [5, 768], P(None, 'fsdp')
- gain_second_new: float32 [5, 768], P(None, 'fsdp')
- head_new: float32 [768, 1000], P('fsdp')
- head_first_new: float32 [768, 1000], P('fsdp')
- head_second_new: float32 [768, 1000], P('fsdp')
- clip_norm: float32 [], replicated
- loss_sum: float32 [], replicated
- weight_sum: float32 [], replicated
Inputs may be any that keep to these rules, and one draw needn't show every extreme that they name: `lengths`: slot 0 of every pack holds a sequence of exactly 1152 patches, slot 1 one of 128 to 256; the remaining slots of the pack are padding. `block_slot`: distinct slots, one a block; slot s is owned by fsdp index s // 2; slots that no block names stay empty.
All inputs are finite; a program needn't handle non-finite values.
Results may differ from a plain program's by a relative error of at most 0.0095.
Values may be sent and summed in bfloat16 or wider, within the bound.
No kernel may reach another device: no remote copies, remote signals or barrier semaphores. Data moves between devices by JAX's collectives and lax.ppermute only.
A program may use at most 576 MiB of HBM per device.

v0:
```python
import jax
import jax.numpy as jnp
from jax import lax
from jax.sharding import PartitionSpec as P

HEADS = 12
HEAD = 64
PACK = 1536
MB = 2
STEP = 10


highest = lax.Precision.HIGHEST
norm_eps = 1e-06
clip_bound = 0.01
stat_decay = 0.95
shampoo_rate = 0.1
decay_rate = 0.01
first_decay = 0.9
second_decay = 0.95
adam_rate = 0.04
table_rate = 0.5
gain_rate = 0.25
adam_eps = 1e-10
narrow = jnp.bfloat16
wide = jnp.float32


def layer_norm(values, gain):
    centred = values - jnp.mean(values, axis=-1, keepdims=True)
    inverse = lax.rsqrt(jnp.mean(centred * centred, axis=-1, keepdims=True) + norm_eps)
    unit = centred * inverse
    return (unit * gain, unit, inverse)


def norm_back(unit, inverse, gain, grad_out):
    scaled = grad_out * gain
    gain_grad = jnp.sum(grad_out * unit, axis=0)
    grad_in = inverse * (
        scaled
        - jnp.mean(scaled, axis=-1, keepdims=True)
        - unit * jnp.mean(scaled * unit, axis=-1, keepdims=True)
    )
    return (grad_in, gain_grad)


def gelu_exact(inner):
    return jax.nn.gelu(inner, approximate=False)


def segments(pack_lengths):
    tokens = jnp.arange(PACK)
    return (tokens >= pack_lengths[0]).astype(jnp.int32) + (
        tokens >= pack_lengths[0] + pack_lengths[1]
    ).astype(jnp.int32)


def masked_scores(query_block, keys, segment_block, segment):
    scores = jnp.einsum("qhd,khd->hqk", query_block, keys, preferred_element_type=wide) * HEAD ** (
        -0.5
    )
    same = segment_block[:, None] == segment[None, :]
    return jnp.where(same[None], scores, -1e30)


def attend(query, keys, values, segment):
    block_rows = min(512, PACK)
    count = PACK // block_rows

    def one_block(inputs):
        query_block, segment_block = inputs
        scores = masked_scores(query_block, keys, segment_block, segment)
        peak = jnp.max(scores, axis=-1, keepdims=True)
        expo = jnp.exp(scores - peak)
        total = jnp.sum(expo, axis=-1, keepdims=True)
        probs = (expo / total).astype(narrow)
        mixed = jnp.einsum("hqk,khd->qhd", probs, values, preferred_element_type=wide)
        return (mixed, (peak + jnp.log(total))[:, :, 0])

    mixed, log_total = lax.map(
        one_block,
        (query.reshape(count, block_rows, HEADS, HEAD), segment.reshape(count, block_rows)),
    )
    return (mixed.reshape(PACK, HEADS, HEAD), log_total)


def attend_back(query, keys, values, segment, log_total, grad_mixed):
    block_rows = min(512, PACK)
    count = PACK // block_rows
    scale = HEAD ** (-0.5)

    def one_block(carry, inputs):
        key_grad, value_grad = carry
        query_block, segment_block, lse_block, grad_block = inputs
        scores = masked_scores(query_block, keys, segment_block, segment)
        probs = jnp.exp(scores - lse_block[:, :, None])
        value_grad = value_grad + jnp.einsum(
            "hqk,qhd->khd", probs.astype(narrow), grad_block, preferred_element_type=wide
        )
        prob_grad = jnp.einsum("qhd,khd->hqk", grad_block, values, preferred_element_type=wide)
        score_grad = (
            probs * (prob_grad - jnp.sum(probs * prob_grad, axis=-1, keepdims=True))
        ).astype(narrow)
        query_grad = scale * jnp.einsum(
            "hqk,khd->qhd", score_grad, keys, preferred_element_type=wide
        )
        key_grad = key_grad + scale * jnp.einsum(
            "hqk,qhd->khd", score_grad, query_block, preferred_element_type=wide
        )
        return ((key_grad, value_grad), query_grad)

    zeros = jnp.zeros((PACK, HEADS, HEAD), wide)
    inputs = (
        query.reshape(count, block_rows, HEADS, HEAD),
        segment.reshape(count, block_rows),
        log_total,
        grad_mixed.reshape(count, block_rows, HEADS, HEAD),
    )
    (key_grad, value_grad), query_grad = lax.scan(one_block, (zeros, zeros), inputs)
    return (query_grad.reshape(PACK, HEADS, HEAD), key_grad, value_grad)


def layer_forward(full, patch_rows, places, pack_lengths, pack_weights, pack_labels):
    weights, table, gain_rows, head_weight = full
    gains = gain_rows.astype(wide)
    width = weights.shape[2]
    segment = segments(pack_lengths)
    grid = jnp.arange(table.shape[1])
    row_hot = (places[0][:, None] == grid[None, :]).astype(narrow)
    col_hot = (places[1][:, None] == grid[None, :]).astype(narrow)
    embed = (
        jnp.dot(patch_rows, weights[0], preferred_element_type=wide)
        + jnp.dot(row_hot, table[0], preferred_element_type=wide)
        + jnp.dot(col_hot, table[1], preferred_element_type=wide)
    )
    normed, unit_one, inverse_one = layer_norm(embed, gains[0])
    first = normed.astype(narrow)
    projected = jnp.einsum("pd,kde->kpe", first, weights[1:4], preferred_element_type=wide)
    query_normed, query_unit, query_inverse = layer_norm(
        projected[0].reshape(PACK, HEADS, HEAD), gains[1].reshape(HEADS, HEAD)
    )
    key_normed, key_unit, key_inverse = layer_norm(
        projected[1].reshape(PACK, HEADS, HEAD), gains[2].reshape(HEADS, HEAD)
    )
    query = query_normed.astype(narrow)
    keys = key_normed.astype(narrow)
    values = projected[2].astype(narrow).reshape(PACK, HEADS, HEAD)
    mixed, log_total = attend(query, keys, values, segment)
    mixed_rows = mixed.astype(narrow).reshape(PACK, width)
    resid = embed + jnp.dot(mixed_rows, weights[4], preferred_element_type=wide)
    normed, unit_two, inverse_two = layer_norm(resid, gains[3])
    second = normed.astype(narrow)
    up_value = jnp.einsum("pd,kde->pke", second, weights[5:9], preferred_element_type=wide)
    act = gelu_exact(up_value).astype(narrow)
    outcome = resid + jnp.einsum("pke,ked->pd", act, weights[9:13], preferred_element_type=wide)
    final, unit_three, inverse_three = layer_norm(outcome, gains[4])
    member = (segment[None, :] == jnp.arange(2)[:, None]).astype(wide) / pack_lengths[
        :, None
    ].astype(wide)
    pooled = jnp.dot(member, final, precision=highest).astype(narrow)
    logits = jnp.dot(pooled, head_weight, preferred_element_type=wide)
    peak = jnp.max(logits, axis=-1, keepdims=True)
    expo = jnp.exp(logits - peak)
    total = jnp.sum(expo, axis=-1, keepdims=True)
    labels_hot = (pack_labels[:, None] == jnp.arange(logits.shape[1])[None, :]).astype(wide)
    picked = jnp.sum(logits * labels_hot, axis=-1)
    weight_rows = pack_weights.astype(wide)
    loss = jnp.sum(weight_rows * (peak[:, 0] + jnp.log(total[:, 0]) - picked))
    logit_grad = (weight_rows[:, None] * (expo / total - labels_hot)).astype(narrow)
    saved = dict(
        patch_rows=patch_rows,
        row_hot=row_hot,
        col_hot=col_hot,
        unit_one=unit_one,
        inverse_one=inverse_one,
        first=first,
        query_unit=query_unit,
        query_inverse=query_inverse,
        key_unit=key_unit,
        key_inverse=key_inverse,
        query=query,
        keys=keys,
        values=values,
        segment=segment,
        log_total=log_total,
        mixed_rows=mixed_rows,
        unit_two=unit_two,
        inverse_two=inverse_two,
        second=second,
        up_value=up_value,
        act=act,
        unit_three=unit_three,
        inverse_three=inverse_three,
        member=member,
        pooled=pooled,
        logit_grad=logit_grad,
    )
    return (loss, saved)


def layer_backward(full, saved):
    weights, table, gain_rows, head_weight = full
    gains = gain_rows.astype(wide)
    width = weights.shape[2]
    logit_grad = saved["logit_grad"]
    head_grad = jnp.einsum("sd,sc->dc", saved["pooled"], logit_grad, preferred_element_type=wide)
    pooled_grad = jnp.einsum("sc,dc->sd", logit_grad, head_weight, preferred_element_type=wide)
    final_grad = jnp.dot(saved["member"].T, pooled_grad, precision=highest)
    outcome_grad, final_gain = norm_back(
        saved["unit_three"], saved["inverse_three"], gains[4], final_grad
    )
    down_in = outcome_grad.astype(narrow)
    down_grad = jnp.einsum("pke,pd->ked", saved["act"], down_in, preferred_element_type=wide)
    act_grad = jnp.einsum("pd,ked->pke", down_in, weights[9:13], preferred_element_type=wide)
    _, gelu_pull = jax.vjp(gelu_exact, saved["up_value"])
    up_grad = gelu_pull(act_grad)[0].astype(narrow)
    up_weight_grad = jnp.einsum(
        "pd,pke->kde", saved["second"], up_grad, preferred_element_type=wide
    )
    second_grad = jnp.einsum("pke,kde->pd", up_grad, weights[5:9], preferred_element_type=wide)
    resid_part, second_gain = norm_back(
        saved["unit_two"], saved["inverse_two"], gains[3], second_grad
    )
    resid_grad = outcome_grad + resid_part
    resid_in = resid_grad.astype(narrow)
    out_grad = jnp.dot(saved["mixed_rows"].T, resid_in, preferred_element_type=wide)
    mixed_grad = jnp.einsum("pe,de->pd", resid_in, weights[4], preferred_element_type=wide).astype(
        narrow
    )
    query_grad, key_grad, value_grad = attend_back(
        saved["query"],
        saved["keys"],
        saved["values"],
        saved["segment"],
        saved["log_total"],
        mixed_grad.reshape(PACK, HEADS, HEAD),
    )
    query_raw, query_gain = norm_back(
        saved["query_unit"], saved["query_inverse"], gains[1].reshape(HEADS, HEAD), query_grad
    )
    key_raw, key_gain = norm_back(
        saved["key_unit"], saved["key_inverse"], gains[2].reshape(HEADS, HEAD), key_grad
    )
    projected_grad = jnp.stack(
        [
            query_raw.reshape(PACK, width),
            key_raw.reshape(PACK, width),
            value_grad.reshape(PACK, width),
        ]
    ).astype(narrow)
    project_weight_grad = jnp.einsum(
        "pd,kpe->kde", saved["first"], projected_grad, preferred_element_type=wide
    )
    first_grad = jnp.einsum(
        "kpe,kde->pd", projected_grad, weights[1:4], preferred_element_type=wide
    )
    embed_part, first_gain = norm_back(
        saved["unit_one"], saved["inverse_one"], gains[0], first_grad
    )
    embed_in = (resid_grad + embed_part).astype(narrow)
    embed_grad = jnp.dot(saved["patch_rows"].T, embed_in, preferred_element_type=wide)
    table_grad = jnp.stack(
        [
            jnp.dot(saved["row_hot"].T, embed_in, preferred_element_type=wide),
            jnp.dot(saved["col_hot"].T, embed_in, preferred_element_type=wide),
        ]
    )
    block_grad = jnp.concatenate(
        [embed_grad[None], project_weight_grad, out_grad[None], up_weight_grad, down_grad], axis=0
    )
    gain_grad = jnp.stack(
        [first_gain, query_gain.reshape(width), key_gain.reshape(width), second_gain, final_gain]
    )
    return (block_grad, table_grad, gain_grad, head_grad)


def adam(weight, grad, first, second, rate, decay):
    first_new = first_decay * first + (1 - first_decay) * grad
    second_new = second_decay * second + (1 - second_decay) * grad * grad
    corrected = (
        first_new
        / (1 - first_decay**STEP)
        / (jnp.sqrt(second_new / (1 - second_decay**STEP)) + adam_eps)
    )
    return (weight - rate * (corrected + decay * weight), first_new, second_new)


def local(
    patches,
    positions,
    lengths,
    res_weights,
    labels,
    block_slot,
    blocks,
    pos_table,
    gains,
    head,
    left_stats,
    right_stats,
    left_roots,
    right_roots,
    pos_first,
    pos_second,
    gain_first,
    gain_second,
    head_first,
    head_second,
):
    owned = (
        blocks.astype(narrow),
        pos_table.astype(narrow),
        gains.astype(narrow),
        head.astype(narrow),
    )
    summed = None
    loss_local = jnp.zeros((), wide)
    for micro in range(MB):
        full = (
            lax.all_gather(owned[0], "fsdp", axis=1, tiled=True),
            lax.all_gather(owned[1], "fsdp", axis=2, tiled=True),
            lax.all_gather(owned[2], "fsdp", axis=1, tiled=True),
            lax.all_gather(owned[3], "fsdp", axis=0, tiled=True),
        )
        loss_term, saved = layer_forward(
            full,
            patches[micro, 0],
            positions[:, micro, 0],
            lengths[micro, 0],
            res_weights[micro, 0],
            labels[micro, 0],
        )
        loss_local = loss_local + loss_term
        back_full = (
            lax.all_gather(owned[0], "fsdp", axis=1, tiled=True),
            lax.all_gather(owned[1], "fsdp", axis=2, tiled=True),
            lax.all_gather(owned[2], "fsdp", axis=1, tiled=True),
            lax.all_gather(owned[3], "fsdp", axis=0, tiled=True),
        )
        terms = layer_backward(back_full, saved)
        shares = (
            lax.psum_scatter(terms[0], "fsdp", scatter_dimension=1, tiled=True),
            lax.psum_scatter(terms[1], "fsdp", scatter_dimension=2, tiled=True),
            lax.psum_scatter(terms[2], "fsdp", scatter_dimension=1, tiled=True),
            lax.psum_scatter(terms[3], "fsdp", scatter_dimension=0, tiled=True),
        )
        shares = lax.psum((shares[0], shares[1], shares[2], shares[3]), "seq")
        summed = shares if summed is None else jax.tree.map(jnp.add, summed, shares)
    weight_local = jnp.sum(res_weights).astype(wide)
    loss_sum, weight_sum = lax.psum((loss_local, weight_local), ("seq", "fsdp"))
    grads = tuple((piece / weight_sum for piece in summed))
    local_squares = (
        jnp.sum(grads[0] * grads[0])
        + jnp.sum(grads[1] * grads[1])
        + jnp.sum(grads[2] * grads[2])
        + jnp.sum(grads[3] * grads[3])
    )
    clip_norm = jnp.sqrt(lax.psum(local_squares, "fsdp"))
    factor = jnp.minimum(1.0, clip_bound / clip_norm)
    block_grads, table_grad, gain_grad, head_grad = tuple((piece * factor for piece in grads))
    total_slots = left_stats.shape[0] * lax.axis_size("fsdp")
    slot_hot = (block_slot[None, :] == jnp.arange(total_slots)[:, None]).astype(wide)
    outgoing = jnp.einsum("sb,brd->srd", slot_hot, block_grads, precision=highest)
    slotted = lax.all_to_all(outgoing, "fsdp", split_axis=0, concat_axis=1, tiled=True)
    left_new = stat_decay * left_stats + (1 - stat_decay) * jnp.einsum(
        "sij,skj->sik", slotted, slotted, precision=highest
    )
    right_new = stat_decay * right_stats + (1 - stat_decay) * jnp.einsum(
        "sji,sjk->sik", slotted, slotted, precision=highest
    )
    inner = jnp.einsum("sij,sjk->sik", slotted, right_roots, precision=highest)
    direction = jnp.einsum("sij,sjk->sik", left_roots, inner, precision=highest)
    returned = lax.all_to_all(direction, "fsdp", split_axis=1, concat_axis=0, tiled=True)
    block_direction = jnp.einsum("sb,srd->brd", slot_hot, returned, precision=highest)
    blocks_new = blocks - shampoo_rate * (block_direction + decay_rate * blocks)
    pos_new, pos_first_new, pos_second_new = adam(
        pos_table, table_grad, pos_first, pos_second, table_rate, decay_rate
    )
    gains_new, gain_first_new, gain_second_new = adam(
        gains, gain_grad, gain_first, gain_second, gain_rate, 0.0
    )
    head_new, head_first_new, head_second_new = adam(
        head, head_grad, head_first, head_second, adam_rate, decay_rate
    )
    return (
        blocks_new,
        block_grads,
        left_new,
        right_new,
        pos_new,
        pos_first_new,
        pos_second_new,
        gains_new,
        gain_first_new,
        gain_second_new,
        head_new,
        head_first_new,
        head_second_new,
        clip_norm,
        loss_sum,
        weight_sum,
    )


def solution(mesh):
    placed = (
        P(None, ("seq", "fsdp"), None, None),
        P(None, None, ("seq", "fsdp"), None),
        P(None, ("seq", "fsdp"), None),
        P(None, ("seq", "fsdp"), None),
        P(None, ("seq", "fsdp"), None),
        P(),
        P(None, "fsdp", None),
        P(None, None, "fsdp"),
        P(None, "fsdp"),
        P("fsdp", None),
        P("fsdp", None, None),
        P("fsdp", None, None),
        P("fsdp", None, None),
        P("fsdp", None, None),
        P(None, None, "fsdp"),
        P(None, None, "fsdp"),
        P(None, "fsdp"),
        P(None, "fsdp"),
        P("fsdp", None),
        P("fsdp", None),
    )
    return jax.shard_map(
        local,
        mesh=mesh,
        in_specs=placed,
        out_specs=(
            P(None, "fsdp", None),
            P(None, "fsdp", None),
            P("fsdp", None, None),
            P("fsdp", None, None),
            P(None, None, "fsdp"),
            P(None, None, "fsdp"),
            P(None, None, "fsdp"),
            P(None, "fsdp"),
            P(None, "fsdp"),
            P(None, "fsdp"),
            P("fsdp", None),
            P("fsdp", None),
            P("fsdp", None),
            P(),
            P(),
            P(),
        ),
        check_vma=False,
    )
```

profile of v0, /device:TPU:0, one launch (start us, length us, event | category | flops | bytes accessed | tf_op | source)
XLA Modules:
  0.0 3388.1 jit_solution(37109885511355958)
XLA Ops:
  20.2 34.5 %all_gather.9 = bf16[2,64,768]{1,0,2:T(2,128)(2,1)S(1)} all-gather(bf16[2,64,96]{1,0,2:T(2,128)(2,1)S(1)} %copy.260), channel_id=1, replica_groups=mesh['seq'=4,'fsdp'=8] {'fsdp'}, dimensions={2}, use_global_device_ids=true | all-gather | bytes 221184 | tf_op jit(solution)/shard_map/all_gather | solution.py:321
  90.4 136.9 %all-gather.4.cloned.1.call-done = bf16[13,768,768]{2,1,0:T(8,128)(2,1)} async-done(((bf16[13,96,768]{2,1,0:T(8,128)(2,1)}), bf16[13,768,768]{2,1,0:T(8,128)(2,1)}) %all-gather.4.cloned.1.call-update) | async-done | bytes 15335440 | tf_op jit(solution)/shard_map/all_gather | solution.py:320
  345.3 161.1 %while.57 = (s32[]{:T(128)}, bf16[3,512,12,64]{1,3,2,0:T(8,128)(2,1)}, f32[3,12,512]{2,1,0:T(8,128)S(1)}, s32[3,512]{1,0:T(4,128)S(1)}, bf16[3,512,12,64]{1,3,2,...) while((s32[]{:T(128)}, ...), condition=%wide.region_40.41_spmd.clone, body=%wide.region_37.40_spmd.clone.sunk | while | flops 2529953280 | bytes 152037600 | solution.py:80
  541.5 45.4 %multiply_convert_fusion.2 = (bf16[1536,4,768]{2,0,1:T(8,128)(2,1)}, f32[1536,4,768]{2,0,1:T(8,128)}) fusion(f32[1536,4,768]{2,0,1:T(8,128)} %get-tuple-element.824, u8[1536,768]{1,0:T(8,128)(4,1)} %get-tuple-element.633, u8[1536,768]{1,0:T(8,128)(4,1)S(1)} %get-tuple-element.632), kind=kLoop, calls=%fused_computation.118 | loop fusion | flops 330301440 | bytes 49545216 | tf_op jit(solution)/shard_map/convert_element_type | solution.py:154
  692.0 465.6 %while.59 = (s32[]{:T(128)}, f32[1536,12,64]{0,2,1:T(8,128)}, f32[1536,12,64]{0,2,1:T(8,128)}, f32[3,512,12,64]{1,0,3,2:T(4,128)}, bf16[3,512,12,64]{1,3,2,0:T(8...) while((s32[]{:T(128)}, f32[1536,12,64]{0,2,1:T(8,128)}, ...), condition=%wide.region_53.54_spmd.clone, body=%wide.region_51.53_spmd.clone.sunk | while | flops 6188434944 | bytes 332851392 | solution.py:119
  739.3 31.6 multiply_convert_fusion.23
  814.6 31.0 dynamic_update_slice.41
  892.5 31.6 multiply_convert_fusion.23
  970.5 31.0 dynamic_update_slice.41
  1048.4 31.6 multiply_convert_fusion.23
  1167.0 162.9 %while.56 = (s32[]{:T(128)}, bf16[3,512,12,64]{1,3,2,0:T(8,128)(2,1)}, f32[3,12,512]{2,1,0:T(8,128)S(1)}, s32[3,512]{1,0:T(4,128)}, bf16[3,512,12,64]{1,3,2,0:T(...) while((s32[]{:T(128)}, ...), condition=%wide.region_9.10_spmd.clone, body=%wide.region_6.9_spmd.clone.sunk | while | flops 2529953280 | bytes 152037600 | solution.py:80
  1365.1 45.4 %multiply_convert_fusion.3 = (bf16[1536,4,768]{2,0,1:T(8,128)(2,1)}, f32[1536,4,768]{2,0,1:T(8,128)}) fusion(f32[1536,4,768]{2,0,1:T(8,128)} %get-tuple-element.833, u8[1536,768]{1,0:T(8,128)(4,1)} %get-tuple-element.635, u8[1536,768]{1,0:T(8,128)(4,1)S(1)} %get-tuple-element.634), kind=kLoop, calls=%fused_computation.132 | loop fusion | flops 330301440 | bytes 49545216 | tf_op jit(solution)/shard_map/convert_element_type | solution.py:154
  1508.4 466.1 %while.58 = (s32[]{:T(128)}, f32[1536,12,64]{0,2,1:T(8,128)}, f32[1536,12,64]{0,2,1:T(8,128)}, f32[3,512,12,64]{1,0,3,2:T(4,128)}, bf16[3,512,12,64]{1,3,2,0:T(8...) while((s32[]{:T(128)}, f32[1536,12,64]{0,2,1:T(8,128)}, ...), condition=%wide.region_22.23_spmd.clone, body=%wide.region_20.22_spmd.clone.sunk | while | flops 6188434944 | bytes 332851392 | solution.py:119
  1555.4 31.6 multiply_convert_fusion.22
  1708.7 31.6 multiply_convert_fusion.22
  1864.9 31.6 multiply_convert_fusion.22
  2163.5 31.2 add.382
  2194.7 34.9 %copy.306 = f32[13,768,768]{2,0,1:T(8,128)} copy(f32[13,768,768]{1,2,0:T(8,128)} %add.382) | data formatting | bytes 61341696 | tf_op jit(solution)/shard_map/add | solution.py:348
  2238.5 595.4 %reduce-scatter.9.cloned.1.call-done = f32[13,96,768]{2,0,1:T(8,128)} async-done(((f32[13,768,768]{2,0,1:T(8,128)}), f32[13,96,768]{2,0,1:T(8,128)}) %reduce-scatter.9.cloned.1.call-update) | async-done | bytes 3833872 | tf_op jit(solution)/shard_map/reduce_scatter | solution.py:342
  2837.2 39.6 %all-reduce = (f32[]{:T(128)}, f32[]{:T(128)}) all-reduce(f32[]{:T(128)S(6)} %convert_element_type.295, f32[]{:T(128)S(6)} %add.381), channel_id=1, replica_groups=mesh['seq'=4,'fsdp'=8] {'seq','fsdp'}, use_global_device_ids=true, to_apply=%region_63.64 | all-reduce | flops 2 | bytes 16 | tf_op jit(solution)/shard_map/psum | solution.py:350
  2899.4 63.6 %reduce-scatter.13.cloned.1.call-done = f32[96,128]{1,0:T(8,128)} async-done(((f32[768,128]{1,0:T(8,128)}), f32[96,128]{1,0:T(8,128)}) %reduce-scatter.13.cloned.1.call-update) | async-done | bytes 49168
  2978.4 87.1 %all-reduce.5.cloned.1.call-done = (f32[13,96,768]{2,0,1:T(8,128)}, f32[96,1000]{1,0:T(8,128)}) async-done(((f32[13,96,768]{2,0,1:T(8,128)}, f32[96,1000]{1,0:T(8,128)}), (f32[13,96,768]{2,0,1:T(8,128)}, f32[96,1000]{1,0:T(8,128)})) %all-reduce.5.cloned.1.call-update) | async-done | bytes 4217872 | tf_op jit(solution)/shard_map/psum | solution.py:347
  3105.8 103.5 %all_to_all.36 = f32[16,96,768]{2,1,0:T(8,128)S(1)} all-to-all(f32[16,96,768]{2,1,0:T(8,128)S(1)} %copy.310), channel_id=1, replica_groups=mesh['seq'=4,'fsdp'=8] {'fsdp'}, dimensions={0} | all-to-all | bytes 9437184 | tf_op jit(solution)/shard_map/all_to_all | solution.py:364
  3289.7 62.3 %all-to-all-done.1 = f32[2,768,768]{2,0,1:T(2,128)} async-done(((f32[2,768,768]{2,0,1:T(2,128)}), f32[2,768,768]{2,0,1:T(2,128)}, u32[]{:S(2)}, u32[]{:S(2)}) %all-to-all-start.1) | async-done | bytes 4718624 | tf_op jit(solution)/shard_map/all_to_all | solution.py:373
  (814 shorter events, 1828.3 us)
Async XLA Ops:
  7.2 220.0 %all-gather.4.cloned.1.call-start = ((), (), s32[]{:S(2)}) async-start(), calls=%async_computation.6 | async-start | bytes 17252352 | tf_op jit(solution)/shard_map/all_gather | solution.py:320
  10.9 594.8 %all-gather.6.cloned.1.call-start = ((), (), s32[]{:S(2)}) async-start(), calls=%async_computation.7 | async-start | bytes 1769472 | tf_op jit(solution)/shard_map/all_gather | solution.py:323
  11.7 2226.8 %reduce-scatter.11.cloned.1.call-start = ((), (), s32[]{:S(2)}) async-start(), calls=%async_computation.9 | async-start | bytes 3538944 | tf_op jit(solution)/shard_map/reduce_scatter | solution.py:345
  55.6 175.7 %copy-start.82 = (s32[1536]{0:T(1024)}, s32[1536]{0:T(1024)S(1)}, u32[]{:S(2)}) copy-start(s32[1536]{0:T(1024)S(1)} %get-tuple-element.666) | copy-start | bytes 18436
  55.6 216.4 %copy-start.86 = (s32[1536]{0:T(1024)}, s32[1536]{0:T(1024)S(1)}, u32[]{:S(2)}) copy-start(s32[1536]{0:T(1024)S(1)} %get-tuple-element.667) | copy-start | bytes 18436
  89.7 141.7 %copy-start.104 = (f32[768]{0:T(1024)}, f32[768]{0:T(1024)S(1)}, u32[]{:S(2)}) copy-start(f32[768]{0:T(1024)S(1)} %get-tuple-element.673) | copy-start | bytes 9220
  89.7 185.2 %copy-start.128 = (f32[768]{0:T(1024)}, f32[768]{0:T(1024)S(1)}, u32[]{:S(2)}) copy-start(f32[768]{0:T(1024)S(1)} %get-tuple-element.674) | copy-start | bytes 9220
  89.7 226.5 %copy-start.96 = (f32[12,64]{1,0:T(8,128)}, f32[12,64]{1,0:T(8,128)S(1)}, u32[]{:S(2)}) copy-start(f32[12,64]{1,0:T(8,128)S(1)} %mul.846) | copy-start | bytes 9220
  89.8 250.5 %copy-start.74 = (f32[12,64]{1,0:T(8,128)}, f32[12,64]{1,0:T(8,128)S(1)}, u32[]{:S(2)}) copy-start(f32[12,64]{1,0:T(8,128)S(1)} %mul.852) | copy-start | bytes 9220
  515.5 145.8 %copy-start.94 = (f32[1536]{0:T(1024)}, f32[1536]{0:T(1024)S(1)}, u32[]{:S(2)}) copy-start(f32[1536]{0:T(1024)S(1)} %broadcast_multiply_fusion.16) | copy-start | bytes 18436
  692.0 465.6 %copy-start.32 = (f32[1536,12]{0,1:T(8,128)S(1)}, f32[1536,12]{0,1:T(8,128)}, u32[]{:S(2)}) copy-start(f32[1536,12]{0,1:T(8,128)} %copy-done.31) | copy-start | bytes 221188
  692.0 465.7 %copy-start.35 = (f32[1536,12]{0,1:T(8,128)S(1)}, f32[1536,12]{0,1:T(8,128)}, u32[]{:S(2)}) copy-start(f32[1536,12]{0,1:T(8,128)} %copy-done.34) | copy-start | bytes 221188
  692.0 465.7 %copy-start.44 = (f32[1536,12]{0,1:T(8,128)S(1)}, f32[1536,12]{0,1:T(8,128)}, u32[]{:S(2)}) copy-start(f32[1536,12]{0,1:T(8,128)} %copy-done.43) | copy-start | bytes 221188
  692.0 465.7 %copy-start.75 = (f32[12,64]{1,0:T(8,128)S(1)}, f32[12,64]{1,0:T(8,128)}, u32[]{:S(2)}) copy-start(f32[12,64]{1,0:T(8,128)} %copy-done.74) | copy-start | bytes 9220
  2124.8 709.0 %reduce-scatter.9.cloned.1.call-start = ((), (), s32[]{:S(2)}) async-start(), calls=%async_computation.8 | async-start | bytes 42467328 | tf_op jit(solution)/shard_map/reduce_scatter | solution.py:342
  2229.8 668.8 %reduce-scatter.15.cloned.1.call-start = ((), (), s32[]{:S(2)}) async-start(), calls=%async_computation.11 | async-start | bytes 442368
  2236.5 597.4 %copy-start.134 = (s32[2,1,2]{2,1,0:T(1,128)S(1)}, s32[2,1,2]{2,1,0:T(1,128)}, u32[]{:S(2)}) copy-start(s32[2,1,2]{2,1,0:T(1,128)} %param.31) | copy-start | bytes 52
  2236.5 598.7 %copy-start.139 = (f32[2]{0:T(128)S(1)}, f32[2]{0:T(128)}, u32[]{:S(2)}) copy-start(f32[2]{0:T(128)} %copy-done.137) | copy-start | bytes 28
  2236.5 598.7 %copy-start.148 = (f32[2]{0:T(128)S(1)}, f32[2]{0:T(128)}, u32[]{:S(2)}) copy-start(f32[2]{0:T(128)} %copy-done.146) | copy-start | bytes 28
  2236.5 598.7 %copy-start.164 = (f32[2]{0:T(128)S(1)}, f32[2]{0:T(128)}, u32[]{:S(2)}) copy-start(f32[2]{0:T(128)} %get-tuple-element.675) | copy-start | bytes 28
  2236.5 598.7 %copy-start.165 = (f32[2]{0:T(128)S(1)}, f32[2]{0:T(128)}, u32[]{:S(2)}) copy-start(f32[2]{0:T(128)} %get-tuple-element.677) | copy-start | bytes 28
  2236.6 726.5 %reduce-scatter.13.cloned.1.call-start = ((), (), s32[]{:S(2)}) async-start(), calls=%async_computation.10 | async-start | bytes 442368
  2238.4 827.2 %all-reduce.5.cloned.1.call-start = ((), (), s32[]{:S(2)}) async-start(), calls=%async_computation.12 | async-start | bytes 10223616 | tf_op jit(solution)/shard_map/psum | solution.py:347
  3244.4 107.6 %all-to-all-start.1 = ((f32[2,768,768]{2,0,1:T(2,128)}), f32[2,768,768]{2,0,1:T(2,128)}, u32[]{:S(2)}, u32[]{:S(2)}) async-start(f32[2,768,768]{2,0,1:T(2,128)} %copy.313), calls=%async_computation.1 | async-start | bytes 9437184 | tf_op jit(solution)/shard_map/all_to_all | solution.py:373
  (208 other events, 2228.6 us)
Sparse Core Ops, SparseCore 0:
  11.0 216.1 all-gather.3
  230.0 42.3 all-gather.5
  2124.9 72.5 reduce-scatter.10
  2229.9 603.9 reduce-scatter.8
  2837.9 60.5 reduce-scatter.14
  2902.6 60.4 reduce-scatter.12
  2965.7 99.7 all-reduce.4
where the time goes:
time: 3400 us; the launch traced here: 3390 us
  matrix products  1140 us (34%)
  waiting for transfers between devices  967 us (28%)
  other arithmetic  571 us (17%)
  local copies, waits for them, and re-layouts  434 us (13%)
  blocking collectives  238 us (7%)
    reduce_scatter x1, waiting for transfers between devices, local(): lax.psum_scatter(terms[0], 'fsdp', scatter_dimension=1, tiled=True)  595 us
    dynamic_update_slice x12, local copies, waits for them, and re-layouts, attend(): lax.map(one_block, (query.reshape(count, block_rows, HEADS, HEAD), segmen...  203 us
    dot_general x12, matrix products, masked_scores(): jnp.einsum('qhd,khd->hqk', query_block, keys, preferred_element_type=wide)  198 us
    convert_element_type x6, other arithmetic, one_block(): score_grad = (probs * (prob_grad - jnp.sum(probs * prob_grad, axis=-1, ke...  189 us
    dot_general x6, matrix products, one_block(): jnp.einsum('qhd,khd->hqk', grad_block, values, preferred_element_type=wide)  169 us
    all_gather x1, waiting for transfers between devices, local(): lax.all_gather(owned[0], 'fsdp', axis=1, tiled=True)  137 us
    dot_general x6, matrix products, one_block(): jnp.einsum('hqk,qhd->khd', probs.astype(narrow), grad_block, preferred_el...  122 us
    reduce_sum x6, other arithmetic, one_block(): total = jnp.sum(expo, axis=-1, keepdims=True)  106 us
  transfers between devices with their start and end apart: 8, of which 6 were waited for; matrix products, arithmetic and copies ran while one was open for 16% of the time, Pallas kernels for 0%

commit v1 on v0

v1 whole, which is shorter than its diff:
```python
import functools
import math
import jax
import jax.numpy as jnp
from jax import lax
from jax.experimental import pallas as pl
from jax.experimental.pallas import tpu as pltpu
from jax.sharding import PartitionSpec as P

HEADS = 12
HEAD = 64
PACK = 1536
LONG = 1152
SHORT = 256
ROWS = LONG + SHORT
TILE = 352
STEP = 10
clip_bound = 0.01
stat_decay = 0.95
shampoo_rate = 0.1
decay_rate = 0.01
first_decay = 0.9
second_decay = 0.95
adam_rate = 0.04
table_rate = 0.5
gain_rate = 0.25
adam_eps = 1e-10
norm_eps = 1e-06
narrow = jnp.bfloat16
wide = jnp.float32
log2e = math.log2(math.e)
VM = 60 * 1024 * 1024


def params(limit=VM):
    return pltpu.CompilerParams(vmem_limit_bytes=limit)


def dot(a, b, ca=1, cb=0):
    return lax.dot_general(a, b, (((ca,), (cb,)), ((), ())), preferred_element_type=wide)


def norm_rows(v):
    c = v - jnp.mean(v, axis=-1, keepdims=True)
    r = lax.rsqrt(jnp.mean(c * c, axis=-1, keepdims=True) + norm_eps)
    return c * r, r


def back_rows(unit, r, scaled):
    return r * (
        scaled
        - jnp.mean(scaled, axis=-1, keepdims=True)
        - unit * jnp.mean(scaled * unit, axis=-1, keepdims=True)
    )


def spec(shape, index):
    return pl.BlockSpec(shape, index)


def held(shape):
    return pl.BlockSpec(shape, lambda *_: (0,) * len(shape), pipeline_mode=pl.Buffered(1))


def cost(flops, moved, trans=0):
    return pl.CostEstimate(flops=int(flops), bytes_accessed=int(moved), transcendentals=int(trans))


def embed_kernel(patch_ref, hot_ref, e_ref, table_ref, gain_ref, embed_ref, first_ref):
    v = dot(patch_ref[0, 0], e_ref[...]) + dot(hot_ref[0], table_ref[...])
    embed_ref[0] = v
    unit, _ = norm_rows(v)
    first_ref[0] = (unit * gain_ref[0:1]).astype(narrow)


def embed_call(patches, hot, e, table, gains):
    mb, width = patches.shape[0], e.shape[1]
    steps = ROWS // TILE
    return pl.pallas_call(
        embed_kernel,
        grid=(mb, steps),
        in_specs=[
            spec((1, 1, TILE, patches.shape[3]), lambda m, i: (m, 0, i, 0)),
            spec((1, TILE, hot.shape[2]), lambda m, i: (m, i, 0)),
            held(e.shape),
            held(table.shape),
            held(gains.shape),
        ],
        out_specs=[spec((1, TILE, width), lambda m, i: (m, i, 0))] * 2,
        out_shape=[
            jax.ShapeDtypeStruct((mb, ROWS, width), wide),
            jax.ShapeDtypeStruct((mb, ROWS, width), narrow),
        ],
        compiler_params=params(),
        cost_estimate=cost(2 * mb * ROWS * width * 896, 20e6),
    )(patches, hot, e, table, gains)


def group_mean(v, ones):
    return jnp.concatenate(
        [dot(v[:, at : at + 256].astype(narrow), ones) for at in range(0, v.shape[1], 256)], axis=1
    )


def project_kernel(first_ref, w_ref, gain_ref, ones_ref, q_ref, k_ref, v_ref, qraw_ref, kraw_ref):
    x = first_ref[0]
    ones = ones_ref[...]
    for i, (ref, raw_ref) in enumerate(((q_ref, qraw_ref), (k_ref, kraw_ref))):
        raw = dot(x, w_ref[i])
        raw_ref[0] = raw.astype(narrow)
        c = raw - group_mean(raw, ones)
        r = lax.rsqrt(group_mean(c * c, ones) + norm_eps)
        out = (c * r * gain_ref[1 + i : 2 + i]).astype(narrow)
        if i == 0:
            out = out * narrow(HEAD**-0.5)
        ref[0] = out
    v_ref[0] = dot(x, w_ref[2]).astype(narrow)


def project_call(first, w, gains, ones):
    mb, _, width = first.shape
    rows = spec((1, TILE, width), lambda m, i: (m, i, 0))
    return pl.pallas_call(
        project_kernel,
        grid=(mb, ROWS // TILE),
        in_specs=[rows, held(w.shape), held(gains.shape), held(ones.shape)],
        out_specs=[rows] * 5,
        out_shape=[jax.ShapeDtypeStruct((mb, ROWS, width), narrow)] * 5,
        compiler_params=params(),
        cost_estimate=cost(2 * mb * ROWS * width * width * 3, 30e6),
    )(first, w, gains, ones)


ROWS_Q = 384


def attend_kernel(lengths_ref, q_ref, k_ref, v_ref, mixed_ref, rest_ref, stat_ref):
    pack, pair = pl.program_id(0), pl.program_id(1)
    lane = lax.broadcasted_iota(jnp.int32, (1, 2 * HEAD), 1)

    def part(start, count, tile, masked):
        k = k_ref[0, start : start + count]
        v = v_ref[0, start : start + count]
        zero = jnp.zeros_like(k)
        one = jnp.ones_like(k)
        k_both = [jnp.where(lane < HEAD, k, zero), jnp.where(lane < HEAD, zero, k)]
        ext = jnp.concatenate(
            [
                jnp.concatenate([jnp.where(lane < HEAD, v, zero), jnp.where(lane < HEAD, one, zero)], axis=1),
                jnp.concatenate([jnp.where(lane < HEAD, zero, v), jnp.where(lane < HEAD, zero, one)], axis=1),
            ],
            axis=0,
        )
        for at in range(start, start + count, tile):
            q = q_ref[0, at : at + tile]
            expos, peaks = [], []
            for h in range(2):
                s = dot(q, k_both[h], 1, 1)
                if masked:
                    limit = lengths_ref[pack, 1]
                    row = lax.broadcasted_iota(jnp.int32, s.shape, 0) + (at - start)
                    col = lax.broadcasted_iota(jnp.int32, s.shape, 1)
                    s = jnp.where((row < limit) == (col < limit), s, -1e30)
                peak = jnp.max(s, axis=1, keepdims=True)
                expos.append(jnp.exp2(s * log2e - peak * log2e).astype(narrow))
                peaks.append(peak)
            both = dot(jnp.concatenate(expos, axis=1), ext)
            total = both[:, 2 * HEAD :]
            mixed = both[:, : 2 * HEAD] / total
            rounded = mixed.astype(narrow)
            mixed_ref[0, at : at + tile] = rounded
            rest_ref[0, at : at + tile] = (mixed - rounded.astype(wide)).astype(narrow)
            lse = (jnp.where(lane < HEAD, peaks[0], peaks[1]) + jnp.log(total)) * log2e
            for h in range(2):
                column = jnp.sum(jnp.where(lane == h * HEAD, lse, 0.0), axis=1, keepdims=True)
                old = stat_ref[0, at : at + tile]
                stat_ref[0, at : at + tile] = jnp.where(lane == 2 * pair + h, column, old)

    part(0, LONG, ROWS_Q, False)
    part(LONG, SHORT, SHORT, True)


def attend_call(lengths, q, k, v):
    mb, _, width = q.shape
    block = pl.BlockSpec((1, ROWS, 2 * HEAD), lambda m, p, *_: (m, 0, p))
    pairs = width // (2 * HEAD)
    moved = mb * ROWS * width * 8
    return pl.pallas_call(
        attend_kernel,
        grid_spec=pltpu.PrefetchScalarGridSpec(
            num_scalar_prefetch=1,
            grid=(mb, pairs),
            in_specs=[block] * 3,
            out_specs=[block, block, pl.BlockSpec((1, ROWS, 128), lambda m, p, *_: (m, 0, 0))],
        ),
        out_shape=[
            jax.ShapeDtypeStruct((mb, ROWS, width), narrow),
            jax.ShapeDtypeStruct((mb, ROWS, width), narrow),
            jax.ShapeDtypeStruct((mb, ROWS, 128), wide),
        ],
        compiler_params=params(),
        cost_estimate=cost(16 * mb * 2 * pairs * (LONG**2 + SHORT**2) * HEAD, moved),
    )(lengths, q, k, v)


def cdf_and_slope(up):
    e = jnp.exp2(up * up * (-0.5 * log2e))
    d = 1.0 + (0.3275911 * 0.5**0.5) * jnp.abs(up)
    t = pl.reciprocal(d, approx=True)
    t = t * (2.0 - d * t)
    poly = t * (0.5 * 1.061405429) + (0.5 * -1.453152027)
    poly = poly * t + (0.5 * 1.421413741)
    poly = poly * t + (0.5 * -0.284496736)
    poly = poly * t + (0.5 * 0.254829592)
    tail = poly * t * e
    cdf = jnp.where(up < 0, tail, 1.0 - tail)
    slope = cdf + up * e * 0.3989422804014327
    return cdf, slope


def forward_kernel(
    lengths_ref, embed_ref, mixed_ref, w_ref, gain_ref,
    second_ref, act_ref, slope_ref, unit2_ref, unit3_ref, stat_ref, pool_ref,
):
    pack, step = pl.program_id(0), pl.program_id(1)
    width = embed_ref.shape[2]
    resid = embed_ref[0] + dot(mixed_ref[0], w_ref[0])
    unit, r2 = norm_rows(resid)
    unit2_ref[0] = unit.astype(narrow)
    second = (unit * gain_ref[3:4]).astype(narrow)
    second_ref[0] = second
    outcome = resid
    for j in range(4):
        up = dot(second, w_ref[1 + j])
        cdf, slope = cdf_and_slope(up)
        act = (up * cdf).astype(narrow)
        act_ref[j, 0] = act
        slope_ref[j, 0] = slope.astype(narrow)
        outcome = outcome + dot(act, w_ref[5 + j])
    unit, r3 = norm_rows(outcome)
    unit3_ref[0] = unit.astype(narrow)
    lane = lax.broadcasted_iota(jnp.int32, (1, 128), 1)
    stat_ref[0] = jnp.where(lane == 0, r2, r3)
    final = unit * gain_ref[4:5]

    @pl.when(step == 0)
    def _():
        pool_ref[...] = jnp.zeros_like(pool_ref)

    row = lax.broadcasted_iota(jnp.int32, (TILE, 1), 0) + step * TILE
    first_len, second_len = lengths_ref[pack, 0], lengths_ref[pack, 1]
    inside = (row < first_len, (row >= first_len) & (row < first_len + second_len))
    for s in range(2):
        total = jnp.sum(jnp.where(inside[s], final, 0.0), axis=0, keepdims=True)
        pool_ref[0, s : s + 1] += total


def forward_call(lengths, embed, mixed, w, gains):
    mb, _, width = embed.shape
    rows = pl.BlockSpec((1, TILE, width), lambda m, i, *_: (m, i, 0))
    wider = pl.BlockSpec((4, 1, TILE, width), lambda m, i, *_: (0, m, i, 0))
    return pl.pallas_call(
        forward_kernel,
        grid_spec=pltpu.PrefetchScalarGridSpec(
            num_scalar_prefetch=1,
            grid=(mb, ROWS // TILE),
            in_specs=[rows, rows, held(w.shape), held(gains.shape)],
            out_specs=[
                rows, wider, wider, rows, rows,
                pl.BlockSpec((1, TILE, 128), lambda m, i, *_: (m, i, 0)),
                pl.BlockSpec((1, 8, width), lambda m, i, *_: (m, 0, 0)),
            ],
        ),
        out_shape=[
            jax.ShapeDtypeStruct((mb, ROWS, width), narrow),
            jax.ShapeDtypeStruct((4, mb, ROWS, width), narrow),
            jax.ShapeDtypeStruct((4, mb, ROWS, width), narrow),
            jax.ShapeDtypeStruct((mb, ROWS, width), narrow),
            jax.ShapeDtypeStruct((mb, ROWS, width), narrow),
            jax.ShapeDtypeStruct((mb, ROWS, 128), wide),
            jax.ShapeDtypeStruct((mb, 8, width), wide),
        ],
        compiler_params=params(),
        cost_estimate=cost(2 * mb * ROWS * width * width * 9, 80e6),
    )(lengths, embed, mixed, w, gains)


def head_kernel(pool_ref, scale_ref, weight_ref, label_ref, head_ref, loss_ref, dhead_ref, dpool_ref):
    pooled = (pool_ref[...] * scale_ref[:, 0:1]).astype(narrow)
    logits = dot(pooled, head_ref[...])
    peak = jnp.max(logits, axis=1, keepdims=True)
    expo = jnp.exp(logits - peak)
    total = jnp.sum(expo, axis=1, keepdims=True)
    hot = lax.broadcasted_iota(jnp.int32, logits.shape, 1) == label_ref[:, 0:1]
    picked = jnp.sum(jnp.where(hot, logits, 0.0), axis=1, keepdims=True)
    weight = weight_ref[:, 0:1].astype(wide)
    loss = jnp.where(weight > 0, weight * (peak + jnp.log(total) - picked), 0.0)
    loss_ref[...] = jnp.broadcast_to(jnp.sum(loss, axis=0, keepdims=True), loss_ref.shape)
    dlogits = (weight * (expo / total - hot.astype(wide))).astype(narrow)
    dhead_ref[...] = dot(pooled, dlogits, 0, 0).astype(dhead_ref.dtype)
    dpool_ref[...] = dot(dlogits, head_ref[...], 1, 1) * scale_ref[:, 0:1]


def head_call(pool, scale, weight, label, head, out=wide):
    rows, width = pool.shape
    return pl.pallas_call(
        head_kernel,
        out_shape=[
            jax.ShapeDtypeStruct((8, 128), wide),
            jax.ShapeDtypeStruct(head.shape, out),
            jax.ShapeDtypeStruct((rows, width), wide),
        ],
        compiler_params=params(),
        cost_estimate=cost(6 * rows * width * 1000, 8e6),
    )(pool, scale, weight, label, head)


def backward_kernel(
    lengths_ref, dpool_ref, unit3_ref, unit2_ref, stat_ref, slope_ref, mixed_ref, rest_ref, w_ref, gain_ref, pick_ref,
    dm_ref, dup_ref, dr_ref, dmixed_ref, delta_ref, dgain_ref,
):
    pack, step = pl.program_id(0), pl.program_id(1)
    row = lax.broadcasted_iota(jnp.int32, (TILE, 1), 0) + step * TILE
    first_len, second_len = lengths_ref[pack, 0], lengths_ref[pack, 1]
    dfinal = jnp.where(
        row < first_len,
        dpool_ref[0, 0:1],
        jnp.where(row < first_len + second_len, dpool_ref[0, 1:2], 0.0),
    )
    unit3 = unit3_ref[0].astype(wide)
    r2, r3 = stat_ref[0, :, 0:1], stat_ref[0, :, 1:2]
    doutcome = back_rows(unit3, r3, dfinal * gain_ref[4:5])
    dgf = jnp.sum(dfinal * unit3, axis=0, keepdims=True)
    dm = doutcome.astype(narrow)
    dm_ref[0] = dm
    dsecond = None
    for j in range(4):
        dact = dot(dm, w_ref[5 + j], 1, 1)
        dup = (dact * slope_ref[j, 0].astype(wide)).astype(narrow)
        dup_ref[j, 0] = dup
        term = dot(dup, w_ref[1 + j], 1, 1)
        dsecond = term if dsecond is None else dsecond + term
    unit2 = unit2_ref[0].astype(wide)
    dg2 = jnp.sum(dsecond * unit2, axis=0, keepdims=True)
    dresid = doutcome + back_rows(unit2, r2, dsecond * gain_ref[3:4])
    dr = dresid.astype(narrow)
    dr_ref[0] = dr
    dmixed = dot(dr, w_ref[0], 1, 1).astype(narrow)
    dmixed_ref[0] = dmixed
    product = dmixed.astype(wide) * (mixed_ref[0].astype(wide) + rest_ref[0].astype(wide))
    high = product.astype(narrow)
    low = (product - high.astype(wide)).astype(narrow)
    delta_ref[0] = dot(high, pick_ref[...]) + dot(low, pick_ref[...])

    @pl.when((pack == 0) & (step == 0))
    def _():
        dgain_ref[...] = jnp.zeros_like(dgain_ref)

    dgain_ref[3:4] += dg2
    dgain_ref[4:5] += dgf


def backward_call(lengths, dpool, unit3, unit2, stat, slope, mixed, rest, w, gains, pick):
    mb, _, width = unit3.shape
    rows = pl.BlockSpec((1, TILE, width), lambda m, i, *_: (m, i, 0))
    lanes = pl.BlockSpec((1, TILE, 128), lambda m, i, *_: (m, i, 0))
    wider = pl.BlockSpec((4, 1, TILE, width), lambda m, i, *_: (0, m, i, 0))
    return pl.pallas_call(
        backward_kernel,
        grid_spec=pltpu.PrefetchScalarGridSpec(
            num_scalar_prefetch=1,
            grid=(mb, ROWS // TILE),
            in_specs=[
                pl.BlockSpec((1, 2, width), lambda m, i, *_: (m, 0, 0)),
                rows, rows, lanes, wider, rows, rows,
                held(w.shape), held(gains.shape), held(pick.shape),
            ],
            out_specs=[rows, wider, rows, rows, lanes, pl.BlockSpec((8, width), lambda m, i, *_: (0, 0))],
        ),
        out_shape=[
            jax.ShapeDtypeStruct((mb, ROWS, width), narrow),
            jax.ShapeDtypeStruct((4, mb, ROWS, width), narrow),
            jax.ShapeDtypeStruct((mb, ROWS, width), narrow),
            jax.ShapeDtypeStruct((mb, ROWS, width), narrow),
            jax.ShapeDtypeStruct((mb, ROWS, 128), wide),
            jax.ShapeDtypeStruct((8, width), wide),
        ],
        compiler_params=params(),
        cost_estimate=cost(2 * mb * ROWS * width * width * 9, 70e6),
    )(lengths, dpool, unit3, unit2, stat, slope, mixed, rest, w, gains, pick)


def attend_back_kernel(
    lengths_ref, q_ref, k_ref, v_ref, do_ref, qraw_ref, kraw_ref, stat_ref, gain_ref, ones_ref,
    dq_ref, dk_ref, dv_ref, dgain_ref, dq_acc, dk_acc, dv_acc,
):
    pack = pl.program_id(1)
    lane = lax.broadcasted_iota(jnp.int32, (1, 2 * HEAD), 1)

    def both(x, axis=0):
        zero = jnp.zeros_like(x)
        return jnp.concatenate([jnp.where(lane < HEAD, x, zero), jnp.where(lane < HEAD, zero, x)], axis=axis)

    def part(start, count, tile, chunk, masked):
        for ti in range(start, start + count, tile):
            q2 = both(q_ref[0, ti : ti + tile])
            do2 = both(do_ref[0, ti : ti + tile])
            lse = jnp.concatenate([stat_ref[0, h : h + 1, ti : ti + tile] for h in (0, 1)], axis=1)
            delta = jnp.concatenate([stat_ref[0, h : h + 1, ti : ti + tile] for h in (2, 3)], axis=1)
            for ui in range(start, start + count, chunk):
                k = k_ref[0, ui : ui + chunk]
                v = v_ref[0, ui : ui + chunk]
                s = dot(k, q2, 1, 1)
                p = jnp.exp2(s * log2e - lse)
                if masked:
                    limit = lengths_ref[pack, 1]
                    row = lax.broadcasted_iota(jnp.int32, s.shape, 0) + (ui - start)
                    col = lax.broadcasted_iota(jnp.int32, s.shape, 1)
                    col = jnp.where(col < tile, col, col - tile) + (ti - start)
                    p = jnp.where((row < limit) == (col < limit), p, 0.0)
                dp = dot(v, do2, 1, 1)
                ds = (p * (dp - delta)).astype(narrow)
                dv_new = dot(p.astype(narrow), do2)
                dk_new = dot(ds, q2)
                k2 = both(k)
                ds_rows = jnp.concatenate([ds[:, :tile], ds[:, tile:]], axis=0)
                dq_new = dot(ds_rows, k2, 0, 0)
                if ti == start:
                    dv_acc[ui : ui + chunk] = dv_new
                    dk_acc[ui : ui + chunk] = dk_new
                else:
                    dv_acc[ui : ui + chunk] += dv_new
                    dk_acc[ui : ui + chunk] += dk_new
                if ui == start:
                    dq_acc[ti : ti + tile] = dq_new
                else:
                    dq_acc[ti : ti + tile] += dq_new

    part(0, LONG, 384, 384, False)
    part(LONG, SHORT, SHORT, SHORT, True)
    dv_ref[0] = dv_acc[...].astype(narrow)
    ones = ones_ref[...]

    def mean(x):
        return dot(x.astype(narrow), ones)

    @pl.when(pack == 0)
    def _():
        dgain_ref[...] = jnp.zeros_like(dgain_ref)

    for i, (acc, raw_ref, ref, factor) in enumerate(
        ((dq_acc, qraw_ref, dq_ref, HEAD**-0.5), (dk_acc, kraw_ref, dk_ref, 1.0))
    ):
        raw = raw_ref[0].astype(wide)
        c = raw - mean(raw)
        r = lax.rsqrt(mean(c * c) + norm_eps)
        unit = c * r
        dy = acc[...] * factor
        dgain_ref[0, i : i + 1] += jnp.sum(dy * unit, axis=0, keepdims=True)
        scaled = dy * gain_ref[1 + i : 2 + i]
        ref[0] = (r * (scaled - mean(scaled) - unit * mean(scaled * unit))).astype(narrow)


def attend_back_call(lengths, q, k, v, do, qraw, kraw, stat, gains, ones, first_pair, pairs):
    mb, _, width = q.shape
    block = pl.BlockSpec((1, ROWS, 2 * HEAD), lambda p, m, *_: (m, 0, p + first_pair))
    out = pl.BlockSpec((1, ROWS, 2 * HEAD), lambda p, m, *_: (m, 0, p))
    shape = jax.ShapeDtypeStruct((mb, ROWS, pairs * 2 * HEAD), narrow)
    return pl.pallas_call(
        attend_back_kernel,
        grid_spec=pltpu.PrefetchScalarGridSpec(
            num_scalar_prefetch=1,
            grid=(pairs, mb),
            in_specs=[
                block, block, block, block, block, block,
                pl.BlockSpec((1, 8, ROWS), lambda p, m, *_: (m, p + first_pair, 0)),
                pl.BlockSpec((8, 2 * HEAD), lambda p, m, *_: (0, p + first_pair)),
                pl.BlockSpec((2 * HEAD, 2 * HEAD), lambda p, m, *_: (0, 0)),
            ],
            out_specs=[out, out, out, pl.BlockSpec((1, 8, 2 * HEAD), lambda p, m, *_: (p, 0, 0))],
            scratch_shapes=[pltpu.VMEM((ROWS, 2 * HEAD), wide)] * 3,
        ),
        out_shape=[shape, shape, shape, jax.ShapeDtypeStruct((pairs, 8, 2 * HEAD), wide)],
        compiler_params=params(),
        cost_estimate=cost(20 * mb * 2 * pairs * (LONG**2 + SHORT**2) * HEAD * 2, mb * ROWS * pairs * 128 * 18),
    )(lengths, q, k, v, do, qraw, kraw, stat, gains, ones)


def first_kernel(*refs, parts):
    grads = refs[: 3 * parts]
    embed_ref, dr_ref, w_ref, gain_ref, out_ref, dgain_ref = refs[3 * parts :]
    step = pl.program_id(0) * pl.num_programs(1) + pl.program_id(1)
    total = None
    for i in range(3):
        rows = jnp.concatenate([grads[3 * p + i][0] for p in range(parts)], axis=1)
        term = dot(rows, w_ref[i], 1, 1)
        total = term if total is None else total + term
    unit, r = norm_rows(embed_ref[0])

    @pl.when(step == 0)
    def _():
        dgain_ref[...] = jnp.zeros_like(dgain_ref)

    dgain_ref[0:1] += jnp.sum(total * unit, axis=0, keepdims=True)
    out_ref[0] = (dr_ref[0].astype(wide) + back_rows(unit, r, total * gain_ref[0:1])).astype(narrow)


def first_call(grads, embed, dr, w, gains):
    mb, _, width = embed.shape
    rows = spec((1, TILE, width), lambda m, i: (m, i, 0))
    parts = len(grads) // 3
    return pl.pallas_call(
        functools.partial(first_kernel, parts=parts),
        grid=(mb, ROWS // TILE),
        in_specs=[spec((1, TILE, g.shape[2]), lambda m, i: (m, i, 0)) for g in grads]
        + [rows, rows, held(w.shape), held(gains.shape)],
        out_specs=[rows, spec((8, width), lambda m, i: (0, 0))],
        out_shape=[
            jax.ShapeDtypeStruct((mb, ROWS, width), narrow),
            jax.ShapeDtypeStruct((8, width), wide),
        ],
        compiler_params=params(),
        cost_estimate=cost(2 * mb * ROWS * width * width * 3, 32e6),
    )(*grads, embed, dr, w, gains)


def fold(parts):
    while len(parts) > 1:
        parts = [parts[i] + parts[i + 1] for i in range(0, len(parts), 2)]
    return parts[0]


def swap(x, axis, bits):
    if bits == 0:
        return x
    return lax.ppermute(x, axis, [(i, i ^ bits) for i in range(lax.axis_size(axis))])


def tied(x, *after):
    return lax.optimization_barrier((x, *after))[0]


def pick_index(x, index, dim):
    return lax.dynamic_index_in_dim(x, index, dim, keepdims=False)


def y_size():
    return 1 << ((lax.axis_size("fsdp").bit_length() - 1) // 2)


def levels():
    across, deep = lax.axis_size("seq"), lax.axis_size("fsdp")
    y = y_size()
    return (("seq", 1, 2), ("seq", 2, across // 2), ("fsdp", 1, y), ("fsdp", y, deep // y))


def scatter_sum(grad):
    n, rows, width = grad.shape
    core, x, y, z = levels()
    part = rows // (core[2] * x[2] * y[2] * z[2])
    view = grad.reshape(n, z[2], y[2], x[2], core[2], part, width)
    for dim, (axis, stride, size) in ((4, core), (3, x), (2, y), (1, z)):
        at = lax.axis_index(axis) // stride % size
        parts = [
            swap(pick_index(view, at ^ k, dim).astype(narrow), axis, k * stride).astype(wide)
            for k in range(size)
        ]
        view = fold(parts)
    return view


def all_sum(x):
    for axis in ("fsdp", "seq"):
        x = fold([swap(x, axis, k) for k in range(lax.axis_size(axis))])
    return x


def place_kernel(*refs, count):
    base_ref, sources, out_ref, sem = refs[0], refs[1 : 1 + count], refs[1 + count], refs[2 + count]
    copies = [
        pltpu.make_async_copy(ref, out_ref.at[base_ref[0] ^ i], sem.at[i]) for i, ref in enumerate(sources)
    ]
    for copy in copies:
        copy.start()
    for copy in copies:
        copy.wait()


def placed(parts, base):
    return pl.pallas_call(
        functools.partial(place_kernel, count=len(parts)),
        in_specs=[pl.BlockSpec(memory_space=pltpu.SMEM)] + [pl.BlockSpec(memory_space=pl.ANY)] * len(parts),
        out_specs=pl.BlockSpec(memory_space=pl.ANY),
        out_shape=jax.ShapeDtypeStruct((len(parts), *parts[0].shape), parts[0].dtype),
        scratch_shapes=[pltpu.SemaphoreType.DMA((len(parts),))],
        cost_estimate=cost(0, 2 * len(parts) * parts[0].size * 2),
    )(base.reshape(1).astype(jnp.int32), *parts)


def across(x):
    size = lax.axis_size("seq")
    me = lax.axis_index("seq")
    held_parts = [swap(x, "seq", k) for k in range(0, size, 2)]
    pair = held_parts + [swap(part, "seq", 1) for part in held_parts]
    half = size // 2
    order = [pair[(k // 2) + (k % 2) * half] for k in range(size)]
    return placed(order, me)


def gather_rows(shard):
    n, rows, width = shard.shape
    size, deep = lax.axis_size("seq"), lax.axis_size("fsdp")
    me = lax.axis_index("seq")
    mine = pick_index(shard.reshape(n, size, rows // size, width), me, 1)
    every = placed([swap(mine, "fsdp", k) for k in range(deep)], lax.axis_index("fsdp"))
    full = across(every)
    return full.transpose(2, 1, 0, 3, 4).reshape(n, deep * rows, width)


def gather_direct(x):
    return placed([swap(x, "fsdp", k) for k in range(lax.axis_size("fsdp"))], lax.axis_index("fsdp"))


def adam(weight, grad, first, second, rate, decay):
    first_new = first_decay * first + (1 - first_decay) * grad
    second_new = second_decay * second + (1 - second_decay) * grad * grad
    corrected = (
        first_new
        / (1 - first_decay**STEP)
        / (jnp.sqrt(second_new / (1 - second_decay**STEP)) + adam_eps)
    )
    return (weight - rate * (corrected + decay * weight), first_new, second_new)


def product(spec_text, a, b):
    return jnp.einsum(spec_text, a, b, preferred_element_type=wide)


def local(
    patches, positions, lengths, res_weights, labels, block_slot, blocks, pos_table, gains, head,
    left_stats, right_stats, left_roots, right_roots,
    pos_first, pos_second, gain_first, gain_second, head_first, head_second,
):
    mb = patches.shape[0]
    deep, size = lax.axis_size("fsdp"), lax.axis_size("seq")
    me_f, me_s = lax.axis_index("fsdp"), lax.axis_index("seq")
    lengths, res_weights, labels = (x[:, 0] for x in (lengths, res_weights, labels))
    lanes = pos_table.shape[2]
    width = lanes * deep
    grid_rows = pos_table.shape[1]
    low = blocks.astype(narrow)

    small = jnp.concatenate(
        [pos_table.reshape(2 * grid_rows, lanes), gains, jnp.zeros((3, lanes), wide)], axis=0
    ).astype(narrow)
    small = gather_direct(small).transpose(1, 0, 2).reshape(2 * grid_rows + 8, width)
    table = small[: 2 * grid_rows]
    gains_full = small[2 * grid_rows :].astype(wide)
    w_embed = gather_rows(low[0:1])
    w_project = gather_rows(low[1:4])
    w_rest = lax.all_gather(
        pick_index(tied(low[4:13], w_embed).reshape(9, size, -1, width), me_s, 1), ("fsdp", "seq"), axis=1, tiled=True
    )
    w_head = lax.all_gather(
        pick_index(tied(head.astype(narrow), w_embed).reshape(size, -1, head.shape[1]), me_s, 0), ("fsdp", "seq"), axis=0, tiled=True
    )

    places = positions[:, :, 0, :ROWS]
    grid = jnp.arange(grid_rows)
    hot = jnp.concatenate([places[i][:, :, None] == grid for i in range(2)], axis=2).astype(narrow)
    index = jnp.arange(256)
    ones = jnp.where(index[:, None] // HEAD == index[None] // HEAD, 1 / HEAD, 0).astype(narrow)
    pick = (jnp.arange(width)[:, None] // HEAD == jnp.arange(128)[None]).astype(narrow)
    embed, first = embed_call(patches, hot, w_embed[0], table, gains_full)
    query, keys, values, query_raw, key_raw = project_call(first, w_project, gains_full, ones)
    mixed, rest, stat = attend_call(lengths, query, keys, values)
    second, act, slope, unit2, unit3, row_stat, pool = forward_call(lengths, embed, mixed, w_rest, gains_full)

    seqs = 2 * mb
    spare = -seqs % 8

    def column(x):
        return jnp.broadcast_to(jnp.pad(x.reshape(seqs), (0, spare))[:, None], (seqs + spare, 128))

    pool = jnp.pad(pool[:, :2].reshape(seqs, width), ((0, spare), (0, 0)))
    loss, d_head, d_pool = head_call(
        pool, column(1.0 / lengths.astype(wide)), column(res_weights), column(labels), w_head, narrow
    )
    lane = jnp.arange(128)[None]
    totals = all_sum(jnp.where(lane == 0, loss[:1], jnp.where(lane == 1, jnp.sum(res_weights).astype(wide), 0.0)))
    loss_sum, weight_sum = totals[0, 0], totals[0, 1]

    dm, d_up, dr, d_mixed, delta, d_gain_rest = backward_call(
        lengths, d_pool[:seqs].reshape(mb, 2, width), unit3, unit2, row_stat, slope, mixed, rest, w_rest, gains_full, pick
    )
    d_down = product("kmpe,mpd->ked", act, dm).astype(narrow)
    d_upper = product("mpd,kmpe->kde", second, d_up).astype(narrow)
    d_out = product("mpd,mpe->de", mixed, dr).astype(narrow)
    own_down = scatter_sum(d_down)
    own_upper = scatter_sum(d_upper)
    own_out = scatter_sum(d_out[None])
    own_head = scatter_sum(d_head[None])[0]
    pairs = HEADS // 2
    stats = jnp.stack([s[:, :, :HEADS].reshape(mb, ROWS, pairs, 2) for s in (stat, delta)], axis=3)
    stats = jnp.pad(stats.transpose(0, 2, 3, 4, 1).reshape(mb, pairs, 4, ROWS), ((0, 0), (0, 0), (0, 4), (0, 0)))
    stats = stats.reshape(mb, 8 * pairs, ROWS)
    dq, dk, dv, d_gain_heads = attend_back_call(
        lengths, query, keys, values, d_mixed, query_raw, key_raw, stats, gains_full, ones[:128, :128], 0, pairs
    )
    d_project = jnp.stack([product("mpd,mpe->de", first, x).astype(narrow) for x in (dq, dk, dv)])
    own_project = scatter_sum(d_project)
    d_embed, d_gain_first = first_call((dq, dk, dv), embed, dr, w_project, gains_full)
    d_e = product("mpd,mpe->de", patches[:, 0, :ROWS], d_embed).astype(narrow)
    own_e = scatter_sum(d_e[None])
    d_table = product("mpd,mpe->de", hot, d_embed)
    d_gain_heads = d_gain_heads.transpose(1, 0, 2).reshape(8, width)
    d_small = jnp.concatenate(
        [d_table, d_gain_first[:1], d_gain_heads[:2], d_gain_rest[3:5], jnp.zeros((3, width), wide)], axis=0
    )
    d_small = d_small.reshape(-1, deep, lanes).transpose(1, 0, 2)
    d_small = fold([swap(pick_index(d_small, me_f ^ k, 0), "fsdp", k) for k in range(deep)])
    d_small = fold([swap(d_small, "seq", k) for k in range(size)]) / weight_sum

    own = (jnp.concatenate([own_e, own_project, own_out, own_upper, own_down]) / weight_sum).astype(narrow)
    own_head = (own_head / weight_sum).astype(narrow)
    squares = (
        jnp.sum(jnp.square(own.astype(wide)))
        + jnp.sum(jnp.square(own_head.astype(wide)))
        + jnp.where(me_s == 0, jnp.sum(jnp.square(d_small)), 0.0)
    )
    clip_norm = jnp.sqrt(all_sum(jnp.broadcast_to(squares, (1, 128)))[0, 0])
    factor = jnp.minimum(1.0, clip_bound / clip_norm)

    per = left_stats.shape[0]
    part = own.shape[1]
    slot_hot = block_slot[None, :] == jnp.arange(per * deep)[:, None]
    outgoing = jnp.einsum("sb,brd->srd", slot_hot.astype(narrow), own).reshape(deep, per, part, width)
    arrived = placed([swap(pick_index(outgoing, me_f ^ k, 0), "fsdp", k) for k in range(deep)], me_f)
    slotted = across(arrived)
    slotted = slotted.transpose(2, 1, 0, 3, 4).reshape(per, width, width)
    left_part = pick_index(left_roots.reshape(per, deep, size, part, width), me_s, 2).reshape(per, deep * part, width)
    inner = jnp.einsum("sij,sjk->sik", left_part, slotted.astype(wide), precision=lax.Precision.HIGH)
    direction = jnp.einsum("sij,sjk->sik", inner, right_roots, precision=lax.Precision.HIGH).astype(narrow)
    direction = direction.reshape(per, deep, part, width)
    back = placed([swap(pick_index(direction, me_f ^ k, 1), "fsdp", k) for k in range(deep)], me_f)
    back = back.reshape(per * deep, part, width)
    back = jnp.einsum("sb,srd->brd", slot_hot.astype(narrow), back)

    def rows_of(x):
        return x.transpose(1, 0, 2, 3).reshape(x.shape[1], size * part, x.shape[3])

    block_direction = rows_of(across(back)).astype(wide) * factor
    blocks_new = blocks - shampoo_rate * (block_direction + decay_rate * blocks)
    block_grads = rows_of(across(own)).astype(wide) * factor
    gram_left = product("sij,skj->sik", slotted, slotted)
    gram_right = product("sji,sjk->sik", slotted, slotted)
    left_new = stat_decay * left_stats + ((1 - stat_decay) * factor * factor) * gram_left
    right_new = stat_decay * right_stats + ((1 - stat_decay) * factor * factor) * gram_right

    table_grad = d_small[: 2 * grid_rows].reshape(2, grid_rows, lanes) * factor
    gain_grad = d_small[2 * grid_rows : 2 * grid_rows + 5] * factor
    head_grad = rows_of(across(own_head[None]))[0].astype(wide) * factor
    pos_new, pos_first_new, pos_second_new = adam(
        pos_table, table_grad, pos_first, pos_second, table_rate, decay_rate
    )
    gains_new, gain_first_new, gain_second_new = adam(gains, gain_grad, gain_first, gain_second, gain_rate, 0.0)
    head_new, head_first_new, head_second_new = adam(
        head, head_grad, head_first, head_second, adam_rate, decay_rate
    )
    return (
        blocks_new, block_grads, left_new, right_new, pos_new, pos_first_new, pos_second_new,
        gains_new, gain_first_new, gain_second_new, head_new, head_first_new, head_second_new,
        clip_norm, loss_sum, weight_sum,
    )


def solution(mesh):
    placed = (
        P(None, ("seq", "fsdp"), None, None),
        P(None, None, ("seq", "fsdp"), None),
        P(None, ("seq", "fsdp"), None),
        P(None, ("seq", "fsdp"), None),
        P(None, ("seq", "fsdp"), None),
        P(),
        P(None, "fsdp", None),
        P(None, None, "fsdp"),
        P(None, "fsdp"),
        P("fsdp", None),
        P("fsdp", None, None),
        P("fsdp", None, None),
        P("fsdp", None, None),
        P("fsdp", None, None),
        P(None, None, "fsdp"),
        P(None, None, "fsdp"),
        P(None, "fsdp"),
        P(None, "fsdp"),
        P("fsdp", None),
        P("fsdp", None),
    )
    return jax.shard_map(
        local,
        mesh=mesh,
        in_specs=placed,
        out_specs=(
            P(None, "fsdp", None),
            P(None, "fsdp", None),
            P("fsdp", None, None),
            P("fsdp", None, None),
            P(None, None, "fsdp"),
            P(None, None, "fsdp"),
            P(None, None, "fsdp"),
            P(None, "fsdp"),
            P(None, "fsdp"),
            P(None, "fsdp"),
            P("fsdp", None),
            P("fsdp", None),
            P("fsdp", None),
            P(),
            P(),
            P(),
        ),
        check_vma=False,
    )
```

time: 3400 us -> 1340 us (0.39)
  matrix products: 1140 us -> 95.6 us
  waiting for transfers between devices: 967 us -> 184 us
  Pallas kernels: 0 us -> 774 us
  other arithmetic: 571 us -> 33.3 us
  local copies, waits for them, and re-layouts: 434 us -> 67.3 us
  blocking collectives: 238 us -> 0 us
  starting transfers between devices: 5.38 us -> 156 us
    dot_general x94 -> x14, matrix products: 1140 us -> 95.6 us  [the longest x10 88.3 us: product(): return jnp.einsum(spec_text, a, b, preferred_element_type=wide)]
    pallas_call x0 -> x19, Pallas kernels: none -> 774 us  [the longest x11 429 us: placed(): pl.pallas_call(functools.partial(place_kernel, count=len(parts)), in_spec...]
    reduce_scatter x2 -> x0, waiting for transfers between devices: 595 us -> none  [the longest x1 595 us: local(): lax.psum_scatter(terms[0], 'fsdp', scatter_dimension=1, tiled=True)]
    convert_element_type x15 -> x5, other arithmetic: 302 us -> 5.27 us  [the longest x1 2.3 us: local(): low = blocks.astype(narrow)]
    dynamic_update_slice x12 -> x0, local copies, waits for them, and re-layouts: 203 us -> none  [attend(): lax.map(one_block, (query.reshape(count, block_rows, HEADS, HEAD), segmen...]
    ppermute x0 -> x119, waiting for transfers between devices: none -> 183 us  [swap(): lax.ppermute(x, axis, [(i, i ^ bits) for i in range(lax.axis_size(axis))])]
    reduce_sum x31 -> x4, other arithmetic: 176 us -> 5.33 us  [the longest x1 1.5 us: local(): jnp.sum(jnp.square(own.astype(wide)))]
    ppermute x0 -> x119, starting transfers between devices: none -> 156 us  [swap(): lax.ppermute(x, axis, [(i, i ^ bits) for i in range(lax.axis_size(axis))])]
  transfers between devices with their start and end apart: 8 -> 121, of which waited for: 6 -> 38; matrix products, arithmetic and copies ran while one was open for 16% -> 13% of each run, Pallas kernels for 0% -> 48%
where the time goes in v1:
time: 1340 us; the launch traced here: 1330 us
  Pallas kernels  774 us (58%)
  waiting for transfers between devices  184 us (14%)
  starting transfers between devices  156 us (12%)
  matrix products  95.6 us (7%)
  local copies, waits for them, and re-layouts  67.3 us (5%)
  other arithmetic  33.3 us (2%)
  between operations  20.1 us (2%)
    pallas_call x11, Pallas kernels, placed(): pl.pallas_call(functools.partial(place_kernel, count=len(parts)), in_spec...  429 us
    ppermute x119, waiting for transfers between devices, swap(): lax.ppermute(x, axis, [(i, i ^ bits) for i in range(lax.axis_size(axis))])  183 us
    ppermute x119, starting transfers between devices, swap(): lax.ppermute(x, axis, [(i, i ^ bits) for i in range(lax.axis_size(axis))])  156 us
    pallas_call x1, Pallas kernels, attend_back_call(): pl.pallas_call(attend_back_kernel, grid_spec=pltpu.PrefetchScalarGridSpec...  109 us
    dot_general x10, matrix products, product(): return jnp.einsum(spec_text, a, b, preferred_element_type=wide)  88.3 us
    pallas_call x1, Pallas kernels, forward_call(): pl.pallas_call(forward_kernel, grid_spec=pltpu.PrefetchScalarGridSpec(num...  68.6 us
    pallas_call x1, Pallas kernels, backward_call(): pl.pallas_call(backward_kernel, grid_spec=pltpu.PrefetchScalarGridSpec(nu...  55.5 us
    pallas_call x1, Pallas kernels, attend_call(): pl.pallas_call(attend_kernel, grid_spec=pltpu.PrefetchScalarGridSpec(num_...  52.3 us
  transfers between devices with their start and end apart: 121, of which 38 were waited for; matrix products, arithmetic and copies ran while one was open for 13% of the time, Pallas kernels for 48%

profile of v1, /device:TPU:0, one launch (start us, length us, event | category | flops | bytes accessed | tf_op | source)
XLA Modules:
  0.0 1329.1 jit_solution(9254467990045531558)
XLA Ops:
  29.4 10.1 shard_map.315.refs_1_
  48.8 36.9 %shard_map.316 = bf16[4,8,1,24,768]{4,3,2,1,0:T(8,128)(2,1)} custom-call(s32[1]{0:T(128)} %bitcast.refs_0_, bf16[8,1,24,768]{3,2,1,0:T(8,128)(2,1)} %shard_map.315.refs_1_, bf16[8,1,24,768]{3,2,1,0:T(8,128)(2,1)} %copy-done.37, bf16[8,1,24,768]{3,2,1,0:T(8,128)(2,1)} %copy-done.36, bf16[8,1,24,768]{3,2,1,0:T(8,128)(2,1)} %copy-done.38), custom_call_target="tpu_custom_call" | custom-call | bytes 2359296 | tf_op jit(solution)/shard_map/pallas_call | solution.py:590
  103.3 8.8 collective-permute-done.20.refs_5_
  120.5 28.0 %shard_map.319.refs_1_ = bf16[8,3,24,768]{3,2,1,0:T(8,128)(2,1)} custom-call(s32[1]{0:T(128)} %bitcast.2.refs_0_, bf16[3,24,768]{2,1,0:T(8,128)(2,1)} %copy-done.34, bf16[3,24,768]{2,1,0:T(8,128)(2,1)} %copy-done.43, bf16[3,24,768]{2,1,0:T(8,128)(2,1)} %copy-done.44, bf16[3,24,768]{2,1,0:T(8,128)(2,1)} %copy-done.45, bf16[3,24,768]{2,1,0:T(8,128)(2,1)} %copy-done.46, ...), custom_call_target="tpu_custom_call" | custom-call | bytes 1769472 | tf_op jit(solution)/shard_map/pallas_call | solution.py:590
  152.7 34.3 %collective-permute-done.25.refs_3_ = bf16[8,3,24,768]{3,2,1,0:T(8,128)(2,1)S(1)} collective-permute-done((bf16[8,3,24,768]{3,2,1,0:T(8,128)(2,1)}, bf16[8,3,24,768]{3,2,1,0:T(8,128)(2,1)S(1)}, u32[]{:S(2)}, u32[]{:S(2)}) %collective-permute-start.25) | collective-permute-done | bytes 884768 | tf_op jit(solution)/shard_map/ppermute | solution.py:536
  200.2 9.6 shard_map.317
  214.7 11.6 shard_map.318
  228.2 108.3 %shard_map.320 = bf16[4,8,3,24,768]{4,3,2,1,0:T(8,128)(2,1)} custom-call(s32[1]{0:T(128)} %bitcast.refs_0_, bf16[8,3,24,768]{3,2,1,0:T(8,128)(2,1)} %shard_map.319.refs_1_, bf16[8,3,24,768]{3,2,1,0:T(8,128)(2,1)} %copy-done.27, bf16[8,3,24,768]{3,2,1,0:T(8,128)(2,1)} %copy-done.26, bf16[8,3,24,768]{3,2,1,0:T(8,128)(2,1)} %copy-done.28), custom_call_target="tpu_custom_call" | custom-call | bytes 7077888 | tf_op jit(solution)/shard_map/pallas_call | solution.py:590
  340.8 22.1 %shard_map.321 = (bf16[2,1408,768]{2,1,0:T(8,128)(2,1)}, bf16[2,1408,768]{2,1,0:T(8,128)(2,1)}, bf16[2,1408,768]{2,1,0:T(8,128)(2,1)}, bf16[2,1408,768]{2,1,0:T(8,128)(2,1)}, bf16[2,1408,768]{2,1,0:T(8,128)(2,1)}) custom-call(bf16[2,1408,768]{2,1,0:T(8,128)(2,1)} %get-tuple-element.50.first_ref, bf16[3,768,768]{2,1,0:T(8,128)(2,1)} %bitcast.419, ...), custom_call_target="tpu_custom_call" | custom-call | flops 9965666304 | bytes 30000000 | tf_op jit(solution)/shard_map/pallas_call | solution.py:123
  362.9 52.3 %shard_map.322 = (bf16[2,1408,768]{2,1,0:T(8,128)(2,1)}, bf16[2,1408,768]{2,1,0:T(8,128)(2,1)}, f32[2,1408,128]{2,1,0:T(8,128)}) custom-call(s32[2,2]{1,0:T(2,128)} %bitcast.462, bf16[2,1408,768]{2,1,0:T(8,128)(2,1)} %get-tuple-element.51.q_ref, bf16[2,1408,768]{2,1,0:T(8,128)(2,1)} %get-tuple-element.52.k_ref, bf16[2,1408,768]{2,1,0:T(8,128)(2,1)} %get-tuple-element.53.v_ref), custom_call_target="tpu_custom_call" | custom-call | flops 34225520640 | bytes 17301504 | tf_op jit(solution)/shard_map/pallas_call | solution.py:188
  417.0 68.6 %shard_map.323 = (bf16[2,1408,768]{2,1,0:T(8,128)(2,1)}, bf16[4,2,1408,768]{3,2,1,0:T(8,128)(2,1)}, bf16[4,2,1408,768]{3,2,1,0:T(8,128)(2,1)}, bf16[2,1408,768]{...) custom-call(s32[2,2]{1,0:T(2,128)} %bitcast.463, ...), custom_call_target="tpu_custom_call" | custom-call | flops 29896998912 | bytes 80000000 | tf_op jit(solution)/shard_map/pallas_call | solution.py:262
  503.4 55.5 %shard_map.325 = (bf16[2,1408,768]{2,1,0:T(8,128)(2,1)}, bf16[4,2,1408,768]{3,2,1,0:T(8,128)(2,1)}, bf16[2,1408,768]{2,1,0:T(8,128)(2,1)}, bf16[2,1408,768]{2,1,...) custom-call(s32[2,2]{1,0:T(2,128)} %bitcast.464, f32[2,2,768]{2,1,0:T(2,128)} %reshape.777.dpool_ref, ...), custom_call_target="tpu_custom_call" | custom-call | flops 29896998912 | bytes 70000000 | tf_op jit(solution)/shard_map/pallas_call | solution.py:368
  570.0 109.0 %shard_map.326 = (bf16[2,1408,768]{2,1,0:T(8,128)(2,1)}, bf16[2,1408,768]{2,1,0:T(8,128)(2,1)}, bf16[2,1408,768]{2,1,0:T(8,128)(2,1)}, f32[6,8,128]{2,1,0:T(8,128)}) custom-call(s32[2,2]{1,0:T(2,128)} %bitcast.465, bf16[2,1408,768]{2,1,0:T(8,128)(2,1)} %get-tuple-element.51.q_ref, bf16[2,1408,768]{2,1,0:T(8,128)(2,1)} %get-tuple-element.52.k_ref, ...), custom_call_target="tpu_custom_call" | custom-call | flops 85563801600 | bytes 38928384 | tf_op jit(solution)/shard_map/pallas_call | solution.py:469
  694.2 21.5 %shard_map.327 = (bf16[2,1408,768]{2,1,0:T(8,128)(2,1)}, f32[8,768]{1,0:T(8,128)}) custom-call(bf16[2,1408,768]{2,1,0:T(8,128)(2,1)} %get-tuple-element.70.refs_0_, bf16[2,1408,768]{2,1,0:T(8,128)(2,1)} %get-tuple-element.71.refs_1_, bf16[2,1408,768]{2,1,0:T(8,128)(2,1)} %get-tuple-element.72.refs_2_, f32[2,1408,768]{2,1,0:T(8,128)} %get-tuple-element.54.embed_ref.refs_3_, ...), custom_call_target="tpu_custom_call" | custom-call | flops 9965666304 | bytes 32000000 | tf_op jit(solution)/shard_map/pallas_call | solution.py:512
  740.8 18.4 %bitcast_convert_fusion = bf16[4,768,768]{2,1,0:T(8,128)(2,1)S(1)} fusion(bf16[4,2,1408,768]{3,2,1,0:T(8,128)(2,1)} %get-tuple-element.77, bf16[2,1408,768]{2,1,0:T(8,128)(2,1)} %get-tuple-element.78), kind=kOutput, calls=%fused_computation | convolution fusion | flops 13289914368 | bytes 26345472 | tf_op jit(solution)/shard_map/kmpe,mpd->ked/dot_general | solution.py:636
  761.0 18.1 %bitcast_convert_fusion.1 = bf16[4,768,768]{1,2,0:T(8,128)(2,1)S(1)} fusion(bf16[4,2,1408,768]{3,2,1,0:T(8,128)(2,1)} %get-tuple-element.75, bf16[2,1408,768]{2,1,0:T(8,128)(2,1)} %get-tuple-element.76), kind=kOutput, calls=%fused_computation.1 | convolution fusion | flops 13289914368 | bytes 26345472 | tf_op jit(solution)/shard_map/mpd,kmpe->kde/dot_general | solution.py:636
  865.5 10.8 collective-permute-done.34
  907.5 18.9 %collective-permute-done.52 = bf16[4,4,2,24,768]{4,3,0,1,2:T(8,128)(2,1)S(1)} collective-permute-done((bf16[4,4,2,24,768]{4,3,0,1,2:T(8,128)(2,1)S(1)}, bf16[4,4,2,24,768]{4,3,0,1,2:T(8,128)(2,1)S(1)}, u32[]{:S(2)}, u32[]{:S(2)}) %collective-permute-start.52) | collective-permute-done | bytes 1179680 | tf_op jit(solution)/shard_map/ppermute | solution.py:536
  930.1 12.3 collective-permute-done.47
  1012.6 19.0 %shard_map.328.refs_1_ = bf16[8,2,24,768]{3,2,1,0:T(8,128)(2,1)} custom-call(s32[1]{0:T(128)} %bitcast.2.refs_0_, bf16[2,24,768]{2,1,0:T(8,128)(2,1)} %get-tuple-element.136.refs_1_, bf16[2,24,768]{2,1,0:T(8,128)(2,1)} %copy-done.50, bf16[2,24,768]{2,1,0:T(8,128)(2,1)} %copy-done.51, bf16[2,24,768]{2,1,0:T(8,128)(2,1)} %copy-done.52, ...), custom_call_target="tpu_custom_call" | custom-call | bytes 1179648 | tf_op jit(solution)/shard_map/pallas_call | solution.py:590
  1058.7 72.6 %shard_map.329 = bf16[4,8,2,24,768]{4,3,2,1,0:T(8,128)(2,1)} custom-call(s32[1]{0:T(128)} %bitcast.refs_0_, bf16[8,2,24,768]{3,2,1,0:T(8,128)(2,1)} %shard_map.328.refs_1_, bf16[8,2,24,768]{3,2,1,0:T(8,128)(2,1)} %copy-done.31, bf16[8,2,24,768]{3,2,1,0:T(8,128)(2,1)} %copy-done.30, bf16[8,2,24,768]{3,2,1,0:T(8,128)(2,1)} %collective-permute-done.76.refs_4_), custom_call_target="tpu_custom_call" | custom-call | bytes 4718592 | tf_op jit(solution)/shard_map/pallas_call | solution.py:590
  1142.5 59.2 %shard_map.332 = bf16[4,13,24,768]{3,2,1,0:T(8,128)(2,1)} custom-call(s32[1]{0:T(128)} %bitcast.refs_0_, bf16[13,24,768]{2,1,0:T(8,128)(2,1)} %copy-done.6, bf16[13,24,768]{2,1,0:T(8,128)(2,1)} %collective-permute-done.113.refs_2_, bf16[13,24,768]{2,1,0:T(8,128)(2,1)} %collective-permute-done.114.refs_3_, bf16[13,24,768]{2,1,0:T(8,128)(2,1)} %collective-permute-done.115.refs_4_), custom_call_target="tpu_custom_call" | custom-call | bytes 3833856 | tf_op jit(solution)/shard_map/pallas_call | solution.py:590
  1217.3 19.0 %shard_map.330 = bf16[8,2,24,768]{3,2,1,0:T(8,128)(2,1)} custom-call(s32[1]{0:T(128)} %bitcast.2.refs_0_, bf16[2,24,768]{2,1,0:T(8,128)(2,1)} %get-tuple-element.128.refs_1_, bf16[2,24,768]{2,1,0:T(8,128)(2,1)} %copy-done.53, bf16[2,24,768]{2,1,0:T(8,128)(2,1)} %copy-done.54, bf16[2,24,768]{2,1,0:T(8,128)(2,1)} %copy-done.58, ...), custom_call_target="tpu_custom_call" | custom-call | bytes 1179648 | tf_op jit(solution)/shard_map/pallas_call | solution.py:590
  1254.9 59.2 %shard_map.331 = bf16[4,13,24,768]{3,2,1,0:T(8,128)(2,1)} custom-call(s32[1]{0:T(128)} %bitcast.refs_0_, bf16[13,24,768]{2,1,0:T(8,128)(2,1)} %copy-done.17, bf16[13,24,768]{2,1,0:T(8,128)(2,1)} %copy-done.33, bf16[13,24,768]{2,1,0:T(8,128)(2,1)} %copy-done.32, bf16[13,24,768]{2,1,0:T(8,128)(2,1)} %collective-permute-done.86.refs_4_), custom_call_target="tpu_custom_call" | custom-call | bytes 3833856 | tf_op jit(solution)/shard_map/pallas_call | solution.py:590
  (590 shorter events, 424.6 us)
Async XLA Ops:
  7.2 409.8 %all-gather.5.cloned.1.call-start = ((), (), s32[]{:S(2)}) async-start(), calls=%async_computation | async-start | bytes 10948608 | tf_op jit(solution)/shard_map/all_gather | solution.py:661
  89.0 398.1 %all-gather.7.cloned.1.call-start = ((), (), s32[]{:S(2)}) async-start(), calls=%async_computation.1 | async-start | bytes 1622016 | tf_op jit(solution)/shard_map/all_gather | solution.py:664
  102.7 49.9 %collective-permute-start.10 = (bf16[136,96]{1,0:T(8,128)(2,1)}, bf16[136,96]{1,0:T(8,128)(2,1)}, u32[]{:S(2)}, u32[]{:S(2)}) collective-permute-start(bf16[136,96]{1,0:T(8,128)(2,1)} %maximum_maximum_fusion.refs_1_), channel_id=1, source_target_pairs={{0,1},{1,0},{2,3},{3,2},{4,5},{5,4},{6,7},{7,6},{8,9},{9,8},{10,11... | collective-permute-start | bytes 78344 | tf_op jit(solution)/shard_map/ppermute | solution.py:536
  112.2 75.6 %collective-permute-start.11 = (bf16[136,96]{1,0:T(8,128)(2,1)}, bf16[136,96]{1,0:T(8,128)(2,1)}, u32[]{:S(2)}, u32[]{:S(2)}) collective-permute-start(bf16[136,96]{1,0:T(8,128)(2,1)} %maximum_maximum_fusion.refs_1_), channel_id=1, source_target_pairs={{0,2},{1,3},{2,0},{3,1},{4,6},{5,7},{6,4},{7,5},{8,10},{9,11},{10,... | collective-permute-start | bytes 78344 | tf_op jit(solution)/shard_map/ppermute | solution.py:536
  116.4 74.6 %collective-permute-start.12 = (bf16[136,96]{1,0:T(8,128)(2,1)}, bf16[136,96]{1,0:T(8,128)(2,1)}, u32[]{:S(2)}, u32[]{:S(2)}) collective-permute-start(bf16[136,96]{1,0:T(8,128)(2,1)} %maximum_maximum_fusion.refs_1_), channel_id=1, source_target_pairs={{0,3},{1,2},{2,1},{3,0},{4,7},{5,6},{6,5},{7,4},{8,11},{9,10},{10,... | collective-permute-start | bytes 78344 | tf_op jit(solution)/shard_map/ppermute | solution.py:536
  116.4 76.0 %collective-permute-start.13 = (bf16[136,96]{1,0:T(8,128)(2,1)}, bf16[136,96]{1,0:T(8,128)(2,1)}, u32[]{:S(2)}, u32[]{:S(2)}) collective-permute-start(bf16[136,96]{1,0:T(8,128)(2,1)} %maximum_maximum_fusion.refs_1_), channel_id=1, source_target_pairs={{0,4},{1,5},{2,6},{3,7},{4,0},{5,1},{6,2},{7,3},{8,12},{9,13},{10,... | collective-permute-start | bytes 78344 | tf_op jit(solution)/shard_map/ppermute | solution.py:536
  148.5 38.6 %collective-permute-start.25 = (bf16[8,3,24,768]{3,2,1,0:T(8,128)(2,1)}, bf16[8,3,24,768]{3,2,1,0:T(8,128)(2,1)S(1)}, u32[]{:S(2)}, u32[]{:S(2)}) collective-permute-start(bf16[8,3,24,768]{3,2,1,0:T(8,128)(2,1)} %shard_map.319.refs_1_), channel_id=1, source_target_pairs={{0,16},{8,24},{16,0},{24,8},{1,17},{9,25},{17,1},{25,9},{2,18},{10... | collective-permute-start | bytes 2654216 | tf_op jit(solution)/shard_map/ppermute | solution.py:536
  152.7 73.7 %collective-permute-start.24 = (bf16[8,3,24,768]{3,2,1,0:T(8,128)(2,1)}, bf16[8,3,24,768]{3,2,1,0:T(8,128)(2,1)S(1)}, u32[]{:S(2)}, u32[]{:S(2)}) collective-permute-start(bf16[8,3,24,768]{3,2,1,0:T(8,128)(2,1)} %shard_map.319.refs_1_), channel_id=1, source_target_pairs={{0,8},{8,0},{16,24},{24,16},{1,9},{9,1},{17,25},{25,17},{2,10},{10... | collective-permute-start | bytes 2654216 | tf_op jit(solution)/shard_map/ppermute | solution.py:536
  187.1 39.3 %collective-permute-start.26 = (bf16[8,3,24,768]{3,2,1,0:T(8,128)(2,1)S(1)}, bf16[8,3,24,768]{3,2,1,0:T(8,128)(2,1)S(1)}, u32[]{:S(2)}, u32[]{:S(2)}) collective-permute-start(bf16[8,3,24,768]{3,2,1,0:T(8,128)(2,1)S(1)} %collective-permute-done.25.refs_3_), channel_id=1, source_target_pairs={{0,8},{8,0},{16,24},{24,16},{1,9},{9,1},{17,25},{25,17},{2,10},{10... | collective-permute-start | bytes 2654216 | tf_op jit(solution)/shard_map/ppermute | solution.py:536
  494.1 296.1 %collective-permute-start.57 = (f32[1,128]{1,0:T(1,128)}, f32[1,128]{1,0:T(1,128)}, u32[]{:S(2)}, u32[]{:S(2)}) collective-permute-start(f32[1,128]{1,0:T(1,128)} %compare_select_fusion.1), channel_id=1, source_target_pairs={{0,1},{1,0},{2,3},{3,2},{4,5},{5,4},{6,7},{7,6},{8,9},{9,8},{10,11... | collective-permute-start | bytes 1544 | tf_op jit(solution)/shard_map/ppermute | solution.py:536
  495.6 296.2 %collective-permute-start.58 = (f32[1,128]{1,0:T(1,128)}, f32[1,128]{1,0:T(1,128)}, u32[]{:S(2)}, u32[]{:S(2)}) collective-permute-start(f32[1,128]{1,0:T(1,128)} %compare_select_fusion.1), channel_id=1, source_target_pairs={{0,2},{1,3},{2,0},{3,1},{4,6},{5,7},{6,4},{7,5},{8,10},{9,11},{10,... | collective-permute-start | bytes 1544 | tf_op jit(solution)/shard_map/ppermute | solution.py:536
  498.2 297.7 %collective-permute-start.59 = (f32[1,128]{1,0:T(1,128)}, f32[1,128]{1,0:T(1,128)}, u32[]{:S(2)}, u32[]{:S(2)}) collective-permute-start(f32[1,128]{1,0:T(1,128)} %compare_select_fusion.1), channel_id=1, source_target_pairs={{0,3},{1,2},{2,1},{3,0},{4,7},{5,6},{6,5},{7,4},{8,11},{9,10},{10,... | collective-permute-start | bytes 1544 | tf_op jit(solution)/shard_map/ppermute | solution.py:536
  498.9 297.9 %collective-permute-start.60 = (f32[1,128]{1,0:T(1,128)}, f32[1,128]{1,0:T(1,128)}, u32[]{:S(2)}, u32[]{:S(2)}) collective-permute-start(f32[1,128]{1,0:T(1,128)} %compare_select_fusion.1), channel_id=1, source_target_pairs={{0,4},{1,5},{2,6},{3,7},{4,0},{5,1},{6,2},{7,3},{8,12},{9,13},{10,... | collective-permute-start | bytes 1544 | tf_op jit(solution)/shard_map/ppermute | solution.py:536
  500.0 296.8 %collective-permute-start.61 = (f32[1,128]{1,0:T(1,128)}, f32[1,128]{1,0:T(1,128)}, u32[]{:S(2)}, u32[]{:S(2)}) collective-permute-start(f32[1,128]{1,0:T(1,128)} %compare_select_fusion.1), channel_id=1, source_target_pairs={{0,5},{1,4},{2,7},{3,6},{4,1},{5,0},{6,3},{7,2},{8,13},{9,12},{10,... | collective-permute-start | bytes 1544 | tf_op jit(solution)/shard_map/ppermute | solution.py:536
  819.8 43.2 %collective-permute-start.45 = (bf16[4,4,2,2,24,768]{5,4,0,1,2,3:T(8,128)(2,1)S(1)}, bf16[4,4,2,2,24,768]{5,4,0,1,2,3:T(8,128)(2,1)S(1)}, u32[]{:S(2)}, u32[]{:S(2)}) collective-permute-start(bf16[4,4,2,2,24,768]{5,4,0,1,2,3:T(8,128)(2,1)S(1)} %bitcast.423), channel_id=1, source_target_pairs={{0,8},{8,0},{16,24},{24,16},{1,9},{9,1},{17,25},{25,17},{2,10},{10... | collective-permute-start | bytes 7077896 | tf_op jit(solution)/shard_map/ppermute | solution.py:536
  819.8 36.1 %collective-permute-start.33 = (bf16[3,4,2,2,24,768]{5,4,0,1,2,3:T(8,128)(2,1)S(1)}, bf16[3,4,2,2,24,768]{5,4,0,1,2,3:T(8,128)(2,1)S(1)}, u32[]{:S(2)}, u32[]{:S(2)}) collective-permute-start(bf16[3,4,2,2,24,768]{5,4,0,1,2,3:T(8,128)(2,1)S(1)} %bitcast.426), channel_id=1, source_target_pairs={{0,8},{8,0},{16,24},{24,16},{1,9},{9,1},{17,25},{25,17},{2,10},{10... | collective-permute-start | bytes 5308424 | tf_op jit(solution)/shard_map/ppermute | solution.py:536
  886.2 40.1 %collective-permute-start.52 = (bf16[4,4,2,24,768]{4,3,0,1,2:T(8,128)(2,1)S(1)}, bf16[4,4,2,24,768]{4,3,0,1,2:T(8,128)(2,1)S(1)}, u32[]{:S(2)}, u32[]{:S(2)}) collective-permute-start(bf16[4,4,2,24,768]{4,3,0,1,2:T(8,128)(2,1)S(1)} %fusion.18), channel_id=1, source_target_pairs={{0,16},{8,24},{16,0},{24,8},{1,17},{9,25},{17,1},{25,9},{2,18},{10... | collective-permute-start | bytes 3538952 | tf_op jit(solution)/shard_map/ppermute | solution.py:536
  892.9 79.5 %collective-permute-start.100 = (f32[136,96]{1,0:T(8,128)S(1)}, f32[136,96]{1,0:T(8,128)S(1)}, u32[]{:S(2)}, u32[]{:S(2)}) collective-permute-start(f32[136,96]{1,0:T(8,128)S(1)} %fusion.72), channel_id=1, source_target_pairs={{0,8},{8,0},{16,24},{24,16},{1,9},{9,1},{17,25},{25,17},{2,10},{10... | collective-permute-start | bytes 156680 | tf_op jit(solution)/shard_map/ppermute | solution.py:536
  927.5 46.2 %collective-permute-start.101 = (f32[136,96]{1,0:T(8,128)S(1)}, f32[136,96]{1,0:T(8,128)S(1)}, u32[]{:S(2)}, u32[]{:S(2)}) collective-permute-start(f32[136,96]{1,0:T(8,128)S(1)} %fusion.72), channel_id=1, source_target_pairs={{0,16},{8,24},{16,0},{24,8},{1,17},{9,25},{17,1},{25,9},{2,18},{10... | collective-permute-start | bytes 156680 | tf_op jit(solution)/shard_map/ppermute | solution.py:536
  995.6 36.1 %collective-permute-start.116 = (bf16[1,24,1000]{2,1,0:T(8,128)(2,1)S(1)}, bf16[1,24,1000]{2,1,0:T(8,128)(2,1)S(1)}, u32[]{:S(2)}, u32[]{:S(2)}) collective-permute-start(bf16[1,24,1000]{2,1,0:T(8,128)(2,1)S(1)} %get-tuple-element.98.refs_1_), channel_id=1, source_target_pairs={{0,8},{8,0},{16,24},{24,16},{1,9},{9,1},{17,25},{25,17},{2,10},{10... | collective-permute-start | bytes 144008 | tf_op jit(solution)/shard_map/ppermute | solution.py:536
  1044.0 98.5 %collective-permute-start.113 = (bf16[13,24,768]{2,1,0:T(8,128)(2,1)S(1)}, bf16[13,24,768]{2,1,0:T(8,128)(2,1)}, u32[]{:S(2)}, u32[]{:S(2)}) collective-permute-start(bf16[13,24,768]{2,1,0:T(8,128)(2,1)S(1)} %get-tuple-element.100.refs_1_), channel_id=1, source_target_pairs={{0,8},{8,0},{16,24},{24,16},{1,9},{9,1},{17,25},{25,17},{2,10},{10... | collective-permute-start | bytes 1437704 | tf_op jit(solution)/shard_map/ppermute | solution.py:536
  1057.9 84.6 %collective-permute-start.115 = (bf16[13,24,768]{2,1,0:T(8,128)(2,1)}, bf16[13,24,768]{2,1,0:T(8,128)(2,1)}, u32[]{:S(2)}, u32[]{:S(2)}) collective-permute-start(bf16[13,24,768]{2,1,0:T(8,128)(2,1)} %collective-permute-done.114.refs_3_), channel_id=1, source_target_pairs={{0,8},{8,0},{16,24},{24,16},{1,9},{9,1},{17,25},{25,17},{2,10},{10... | collective-permute-start | bytes 1437704 | tf_op jit(solution)/shard_map/ppermute | solution.py:536
  1139.5 66.5 %collective-permute-start.77 = (bf16[2,24,768]{2,1,0:T(8,128)(2,1)}, bf16[2,24,768]{2,1,0:T(8,128)(2,1)S(1)}, u32[]{:S(2)}, u32[]{:S(2)}) collective-permute-start(bf16[2,24,768]{2,1,0:T(8,128)(2,1)} %get-tuple-element.127), channel_id=1, source_target_pairs={{0,1},{1,0},{2,3},{3,2},{4,5},{5,4},{6,7},{7,6},{8,9},{9,8},{10,11... | collective-permute-start | bytes 221192 | tf_op jit(solution)/shard_map/ppermute | solution.py:536
  1140.2 67.7 %collective-permute-start.78 = (bf16[2,24,768]{2,1,0:T(8,128)(2,1)S(1)}, bf16[2,24,768]{2,1,0:T(8,128)(2,1)S(1)}, u32[]{:S(2)}, u32[]{:S(2)}) collective-permute-start(bf16[2,24,768]{2,1,0:T(8,128)(2,1)S(1)} %get-tuple-element.126), channel_id=1, source_target_pairs={{0,2},{1,3},{2,0},{3,1},{4,6},{5,7},{6,4},{7,5},{8,10},{9,11},{10,... | collective-permute-start | bytes 221192 | tf_op jit(solution)/shard_map/ppermute | solution.py:536
  (189 other events, 2784.2 us)
Sparse Core Ops, SparseCore 0:
  89.1 116.2 all-gather.4
  214.8 54.1 all-gather.6

commit v2 on v1

--- a/solution.py
+++ b/solution.py
@@ -66,15 +66,16 @@
     return pl.CostEstimate(flops=int(flops), bytes_accessed=int(moved), transcendentals=int(trans))
 
 
-def embed_kernel(patch_ref, hot_ref, e_ref, table_ref, gain_ref, embed_ref, first_ref):
-    v = dot(patch_ref[0, 0], e_ref[...]) + dot(hot_ref[0], table_ref[...])
+def embed_kernel(patch_ref, hot_ref, e_ref, gain_ref, embed_ref, first_ref):
+    width = embed_ref.shape[2]
+    v = dot(patch_ref[0, 0], e_ref[:, :width]) + dot(hot_ref[0], e_ref[:, width : width + 128], 1, 1)
     embed_ref[0] = v
     unit, _ = norm_rows(v)
     first_ref[0] = (unit * gain_ref[0:1]).astype(narrow)
 
 
-def embed_call(patches, hot, e, table, gains):
-    mb, width = patches.shape[0], e.shape[1]
+def embed_call(patches, hot, e, gains):
+    mb, width = patches.shape[0], gains.shape[1]
     steps = ROWS // TILE
     return pl.pallas_call(
         embed_kernel,
@@ -83,7 +84,6 @@
             spec((1, 1, TILE, patches.shape[3]), lambda m, i: (m, 0, i, 0)),
             spec((1, TILE, hot.shape[2]), lambda m, i: (m, i, 0)),
             held(e.shape),
-            held(table.shape),
             held(gains.shape),
         ],
         out_specs=[spec((1, TILE, width), lambda m, i: (m, i, 0))] * 2,
@@ -93,7 +93,7 @@
         ],
         compiler_params=params(),
         cost_estimate=cost(2 * mb * ROWS * width * 896, 20e6),
-    )(patches, hot, e, table, gains)
+    )(patches, hot, e, gains)
 
 
 def group_mean(v, ones):
@@ -102,19 +102,22 @@
     )
 
 
-def project_kernel(first_ref, w_ref, gain_ref, ones_ref, q_ref, k_ref, v_ref, qraw_ref, kraw_ref):
+def project_kernel(first_ref, w_ref, gain_ref, ones_ref, q_ref, k_ref, v_ref, *kept):
     x = first_ref[0]
+    width = x.shape[1]
     ones = ones_ref[...]
-    for i, (ref, raw_ref) in enumerate(((q_ref, qraw_ref), (k_ref, kraw_ref))):
-        raw = dot(x, w_ref[i])
-        raw_ref[0] = raw.astype(narrow)
+    for i, ref in enumerate((q_ref, k_ref)):
+        raw = dot(x, w_ref[:, i * width : (i + 1) * width])
         c = raw - group_mean(raw, ones)
         r = lax.rsqrt(group_mean(c * c, ones) + norm_eps)
-        out = (c * r * gain_ref[1 + i : 2 + i]).astype(narrow)
+        unit = c * r
+        kept[i][0] = unit.astype(narrow)
+        kept[2 + i][0] = r.astype(narrow)
+        out = (unit * gain_ref[1 + i : 2 + i]).astype(narrow)
         if i == 0:
             out = out * narrow(HEAD**-0.5)
         ref[0] = out
-    v_ref[0] = dot(x, w_ref[2]).astype(narrow)
+    v_ref[0] = dot(x, w_ref[:, 2 * width :]).astype(narrow)
 
 
 def project_call(first, w, gains, ones):
@@ -124,8 +127,8 @@
         project_kernel,
         grid=(mb, ROWS // TILE),
         in_specs=[rows, held(w.shape), held(gains.shape), held(ones.shape)],
-        out_specs=[rows] * 5,
-        out_shape=[jax.ShapeDtypeStruct((mb, ROWS, width), narrow)] * 5,
+        out_specs=[rows] * 7,
+        out_shape=[jax.ShapeDtypeStruct((mb, ROWS, width), narrow)] * 7,
         compiler_params=params(),
         cost_estimate=cost(2 * mb * ROWS * width * width * 3, 30e6),
     )(first, w, gains, ones)
@@ -204,17 +207,8 @@
 
 
 def cdf_and_slope(up):
-    e = jnp.exp2(up * up * (-0.5 * log2e))
-    d = 1.0 + (0.3275911 * 0.5**0.5) * jnp.abs(up)
-    t = pl.reciprocal(d, approx=True)
-    t = t * (2.0 - d * t)
-    poly = t * (0.5 * 1.061405429) + (0.5 * -1.453152027)
-    poly = poly * t + (0.5 * 1.421413741)
-    poly = poly * t + (0.5 * -0.284496736)
-    poly = poly * t + (0.5 * 0.254829592)
-    tail = poly * t * e
-    cdf = jnp.where(up < 0, tail, 1.0 - tail)
-    slope = cdf + up * e * 0.3989422804014327
+    cdf = 0.5 + 0.5 * lax.erf(up * 0.7071067811865476)
+    slope = cdf + up * (jnp.exp2(up * up * (-0.5 * log2e)) * 0.3989422804014327)
     return cdf, slope
 
 
@@ -391,7 +385,7 @@
 
 
 def attend_back_kernel(
-    lengths_ref, q_ref, k_ref, v_ref, do_ref, qraw_ref, kraw_ref, stat_ref, gain_ref, ones_ref,
+    lengths_ref, q_ref, k_ref, v_ref, do_ref, qunit_ref, kunit_ref, qr_ref, kr_ref, stat_ref, gain_ref, ones_ref,
     dq_ref, dk_ref, dv_ref, dgain_ref, dq_acc, dk_acc, dv_acc,
 ):
     pack = pl.program_id(1)
@@ -448,20 +442,17 @@
     def _():
         dgain_ref[...] = jnp.zeros_like(dgain_ref)
 
-    for i, (acc, raw_ref, ref, factor) in enumerate(
-        ((dq_acc, qraw_ref, dq_ref, HEAD**-0.5), (dk_acc, kraw_ref, dk_ref, 1.0))
+    for i, (acc, unit_ref, r_ref, ref, factor) in enumerate(
+        ((dq_acc, qunit_ref, qr_ref, dq_ref, HEAD**-0.5), (dk_acc, kunit_ref, kr_ref, dk_ref, 1.0))
     ):
-        raw = raw_ref[0].astype(wide)
-        c = raw - mean(raw)
-        r = lax.rsqrt(mean(c * c) + norm_eps)
-        unit = c * r
+        unit, r = unit_ref[0].astype(wide), r_ref[0].astype(wide)
         dy = acc[...] * factor
         dgain_ref[0, i : i + 1] += jnp.sum(dy * unit, axis=0, keepdims=True)
         scaled = dy * gain_ref[1 + i : 2 + i]
         ref[0] = (r * (scaled - mean(scaled) - unit * mean(scaled * unit))).astype(narrow)
 
 
-def attend_back_call(lengths, q, k, v, do, qraw, kraw, stat, gains, ones, first_pair, pairs):
+def attend_back_call(lengths, q, k, v, do, kept, stat, gains, ones, first_pair, pairs):
     mb, _, width = q.shape
     block = pl.BlockSpec((1, ROWS, 2 * HEAD), lambda p, m, *_: (m, 0, p + first_pair))
     out = pl.BlockSpec((1, ROWS, 2 * HEAD), lambda p, m, *_: (m, 0, p))
@@ -472,7 +463,7 @@
             num_scalar_prefetch=1,
             grid=(pairs, mb),
             in_specs=[
-                block, block, block, block, block, block,
+                *[block] * 8,
                 pl.BlockSpec((1, 8, ROWS), lambda p, m, *_: (m, p + first_pair, 0)),
                 pl.BlockSpec((8, 2 * HEAD), lambda p, m, *_: (0, p + first_pair)),
                 pl.BlockSpec((2 * HEAD, 2 * HEAD), lambda p, m, *_: (0, 0)),
@@ -483,17 +474,18 @@
         out_shape=[shape, shape, shape, jax.ShapeDtypeStruct((pairs, 8, 2 * HEAD), wide)],
         compiler_params=params(),
         cost_estimate=cost(20 * mb * 2 * pairs * (LONG**2 + SHORT**2) * HEAD * 2, mb * ROWS * pairs * 128 * 18),
-    )(lengths, q, k, v, do, qraw, kraw, stat, gains, ones)
+    )(lengths, q, k, v, do, *kept, stat, gains, ones)
 
 
 def first_kernel(*refs, parts):
     grads = refs[: 3 * parts]
     embed_ref, dr_ref, w_ref, gain_ref, out_ref, dgain_ref = refs[3 * parts :]
     step = pl.program_id(0) * pl.num_programs(1) + pl.program_id(1)
+    width = embed_ref.shape[2]
     total = None
     for i in range(3):
         rows = jnp.concatenate([grads[3 * p + i][0] for p in range(parts)], axis=1)
-        term = dot(rows, w_ref[i], 1, 1)
+        term = dot(rows, w_ref[:, i * width : (i + 1) * width], 1, 1)
         total = term if total is None else total + term
     unit, r = norm_rows(embed_ref[0])
 
@@ -524,6 +516,161 @@
     )(*grads, embed, dr, w, gains)
 
 
+def split_rows(value, own_ref, sent_ref, me, n):
+    across, up, deep = own_ref.shape[:3]
+    part = own_ref.shape[4]
+    for x in range(across):
+        for y in range(up):
+            for z in range(deep):
+                at = ((z * up + y) * across + x) * 2 * part
+                first = value[at : at + part].astype(narrow)
+                second = value[at + part : at + 2 * part].astype(narrow)
+                own_ref[x, y, z, n] = jnp.where(me == 0, first, second)
+                sent_ref[x, y, z, n] = jnp.where(me == 0, second, first)
+
+
+def flat_rows(ref):
+    return ref[...].reshape(-1, ref.shape[-1])
+
+
+def weight_kernel(at_ref, act_ref, dm_ref, second_ref, dup_ref, own_ref, sent_ref):
+    step = pl.program_id(0)
+
+    def write(a_ref, b_ref):
+        split_rows(dot(flat_rows(a_ref), flat_rows(b_ref), 0, 0), own_ref, sent_ref, at_ref[0], 0)
+
+    pl.when(step < 4)(lambda: write(second_ref, dup_ref))
+    pl.when(step >= 4)(lambda: write(act_ref, dm_ref))
+
+
+def split_shape(rows):
+    core, x, y, z = (level[2] for level in levels())
+    return (x, y, z), rows // (core * x * y * z)
+
+
+def core_at():
+    return (lax.axis_index("seq") % 2).reshape(1).astype(jnp.int32)
+
+
+def weight_call(act, dm, second, dup):
+    width = dm.shape[2]
+    (x, y, z), part = split_shape(width)
+    rows = pl.BlockSpec(dm.shape, lambda i, *_: (0, 0, 0), pipeline_mode=pl.Buffered(1))
+    out = pl.BlockSpec((x, y, z, 1, part, width), lambda i, *_: (0, 0, 0, i, 0, 0))
+    one = (1, *dm.shape)
+    return pl.pallas_call(
+        weight_kernel,
+        grid_spec=pltpu.PrefetchScalarGridSpec(
+            num_scalar_prefetch=1,
+            grid=(8,),
+            in_specs=[
+                pl.BlockSpec(one, lambda i, *_: (jnp.maximum(i - 4, 0), 0, 0, 0)),
+                rows,
+                rows,
+                pl.BlockSpec(one, lambda i, *_: (jnp.minimum(i, 3), 0, 0, 0)),
+            ],
+            out_specs=[out, out],
+        ),
+        out_shape=[jax.ShapeDtypeStruct((x, y, z, 8, part, width), narrow)] * 2,
+        compiler_params=params(),
+        cost_estimate=cost(2 * 8 * dm.size * width, 60e6),
+    )(core_at(), act, dm, second, dup)
+
+
+def one_weight_kernel(at_ref, a_ref, *refs, count):
+    b_refs, own_ref, sent_ref, total = refs[:count], refs[count], refs[count + 1], refs[count + 2]
+    step = pl.program_id(0)
+    last = step == pl.num_programs(0) - 1
+    a = a_ref[0]
+    at = 0
+    for b_ref in b_refs:
+        lanes = pl.ds(at, b_ref.shape[-1])
+        at += b_ref.shape[-1]
+        value = dot(a, b_ref[0], 0, 0)
+
+        @pl.when(step == 0)
+        def _(value=value, lanes=lanes):
+            total[:, lanes] = value
+
+        @pl.when((step > 0) & ~last)
+        def _(value=value, lanes=lanes):
+            total[:, lanes] += value
+
+        @pl.when(last)
+        def _(value=value, lanes=lanes):
+            split_rows(total[:, lanes] + value, own_ref.at[..., lanes], sent_ref.at[..., lanes], at_ref[0], 0)
+
+
+def one_weight_call(a, *b):
+    mb, rows, depth = a.shape
+    width = sum(x.shape[-1] for x in b)
+    (x, y, z), part = split_shape(depth)
+    shape = (x, y, z, 1, part, width)
+    out = pl.BlockSpec(shape, lambda m, *_: (0,) * 6)
+    return pl.pallas_call(
+        functools.partial(one_weight_kernel, count=len(b)),
+        grid_spec=pltpu.PrefetchScalarGridSpec(
+            num_scalar_prefetch=1,
+            grid=(mb,),
+            in_specs=[pl.BlockSpec((1, *v.shape[1:]), lambda m, *_: (m, 0, 0)) for v in (a, *b)],
+            out_specs=[out] * 2,
+            scratch_shapes=[pltpu.VMEM((depth, width), wide)],
+        ),
+        out_shape=[jax.ShapeDtypeStruct(shape, narrow)] * 2,
+        compiler_params=params(),
+        cost_estimate=cost(2 * a.size * width, 12e6),
+    )(core_at(), a, *b)
+
+
+def embed_weight_kernel(at_ref, patch_ref, hot_ref, grad_ref, gain_ref, own_ref, sent_ref, total):
+    step = pl.program_id(0)
+    grad = grad_ref[0]
+    width = grad.shape[1]
+    value = dot(patch_ref[0, 0], grad, 0, 0)
+    table = dot(grad, hot_ref[0], 0, 0)
+
+    @pl.when(step == 0)
+    def _():
+        total[:, :width] = value
+        total[:, width : width + 128] = table
+
+    @pl.when(step > 0)
+    def _():
+        total[:, :width] += value
+        total[:, width : width + 128] += table
+
+    @pl.when(step == pl.num_programs(0) - 1)
+    def _():
+        total[:, width + 128 :] = gain_ref[...]
+        split_rows(total[...], own_ref, sent_ref, at_ref[0], 0)
+
+
+def embed_weight_call(patches, hot, grad, gain_columns):
+    mb, _, width = grad.shape
+    pixels = patches.shape[3]
+    (x, y, z), part = split_shape(pixels)
+    shape = (x, y, z, 1, part, width + 256)
+    out = pl.BlockSpec(shape, lambda m, *_: (0,) * 6)
+    return pl.pallas_call(
+        embed_weight_kernel,
+        grid_spec=pltpu.PrefetchScalarGridSpec(
+            num_scalar_prefetch=1,
+            grid=(mb,),
+            in_specs=[
+                pl.BlockSpec((1, 1, ROWS, pixels), lambda m, *_: (m, 0, 0, 0)),
+                pl.BlockSpec((1, ROWS, hot.shape[2]), lambda m, *_: (m, 0, 0)),
+                pl.BlockSpec((1, ROWS, width), lambda m, *_: (m, 0, 0)),
+                pl.BlockSpec((width, 128), lambda m, *_: (0, 0)),
+            ],
+            out_specs=[out, out],
+            scratch_shapes=[pltpu.VMEM((pixels, width + 256), wide)],
+        ),
+        out_shape=[jax.ShapeDtypeStruct(shape, narrow)] * 2,
+        compiler_params=params(),
+        cost_estimate=cost(2 * grad.size * (pixels + 128), 12e6),
+    )(core_at(), patches, hot, grad, gain_columns)
+
+
 def fold(parts):
     while len(parts) > 1:
         parts = [parts[i] + parts[i + 1] for i in range(0, len(parts), 2)]
@@ -544,81 +691,267 @@
     return lax.dynamic_index_in_dim(x, index, dim, keepdims=False)
 
 
-def y_size():
-    return 1 << ((lax.axis_size("fsdp").bit_length() - 1) // 2)
-
-
 def levels():
     across, deep = lax.axis_size("seq"), lax.axis_size("fsdp")
-    y = y_size()
+    y = 1 << ((deep.bit_length() - 1) // 2)
     return (("seq", 1, 2), ("seq", 2, across // 2), ("fsdp", 1, y), ("fsdp", y, deep // y))
 
 
-def scatter_sum(grad):
-    n, rows, width = grad.shape
-    core, x, y, z = levels()
-    part = rows // (core[2] * x[2] * y[2] * z[2])
-    view = grad.reshape(n, z[2], y[2], x[2], core[2], part, width)
-    for dim, (axis, stride, size) in ((4, core), (3, x), (2, y), (1, z)):
+CORE, X, Y, Z = range(4)
+
+
+class Sum:
+    def __init__(self, terms, which):
+        axis, stride, size = levels()[which]
         at = lax.axis_index(axis) // stride % size
-        parts = [
-            swap(pick_index(view, at ^ k, dim).astype(narrow), axis, k * stride).astype(wide)
-            for k in range(size)
+
+        def part(k):
+            return fold([pick_index(term, at ^ k, 0).astype(wide) for term in terms])
+
+        self.sent = [part(k).astype(narrow) for k in range(1, size)]
+        self.terms = [part(0)] + [swap(x, axis, (k + 1) * stride) for k, x in enumerate(self.sent)]
+
+    def after(self, *others):
+        return [tied(self.terms[0], *others), *self.terms[1:]]
+
+    def total(self):
+        return fold([term.astype(wide) for term in self.terms])
+
+
+def core_terms(own, sent):
+    return [own, swap(sent, "seq", 1)]
+
+
+def settle_kernel(at_ref, *refs, count, moves):
+    sources, outs = refs[:count], refs[count:]
+    for source, index, out, target in moves:
+        outs[out][target(at_ref[0], at_ref[1])] = sources[source][index]
+
+
+def mesh_at():
+    return jnp.stack([lax.axis_index("fsdp"), lax.axis_index("seq")]).astype(jnp.int32)
+
+
+def in_vmem(count):
+    return [pl.BlockSpec(memory_space=pltpu.VMEM)] * count
+
+
+def settled(parts, shapes, moves):
+    size = sum(part.size for part in parts) * parts[0].dtype.itemsize
+    return pl.pallas_call(
+        functools.partial(settle_kernel, count=len(parts), moves=moves),
+        in_specs=[pl.BlockSpec(memory_space=pltpu.SMEM)] + in_vmem(len(parts)),
+        out_specs=in_vmem(len(shapes)),
+        out_shape=[jax.ShapeDtypeStruct(shape, parts[0].dtype) for shape in shapes],
+        compiler_params=params(),
+        cost_estimate=cost(0, 2 * size),
+    )(mesh_at(), *parts)
+
+
+def seq_parts(x, *after):
+    half = [swap(x, "seq", k) for k in range(0, lax.axis_size("seq"), 2)]
+    if after:
+        half = [half[0]] + [tied(y, *after) for y in half[1:]]
+    return [part for y in half for part in (y, swap(y, "seq", 1))]
+
+
+def settle_rows(parts, cuts, shapes):
+    deep = parts[0].shape[0]
+    moves = [
+        (j, (k, slice(start, stop)), out, lambda f, s, j=j, k=k, index=index: (*index, k ^ f, j ^ s))
+        for j in range(len(parts))
+        for k in range(deep)
+        for start, stop, out, index in cuts
+    ]
+    return settled(parts, shapes, moves)
+
+
+def near_exchange(x):
+    return jnp.stack([swap(x, "fsdp", k) for k in range(levels()[Y][2])])
+
+
+def far_exchange(x):
+    _, stride, far = levels()[Z]
+    return [swap(x, "fsdp", k * stride) for k in range(far)]
+
+
+def stacked(parts):
+    return jnp.stack(parts).reshape(-1, *parts[0].shape[1:])
+
+
+def my_rows(x):
+    size = lax.axis_size("seq")
+    return pick_index(x.reshape(x.shape[0], size, x.shape[1] // size, x.shape[2]), lax.axis_index("seq"), 1)
+
+
+def grads_kernel(at_ref, factor_ref, *refs, count, part):
+    parts, (out_ref, small_ref) = refs[:count], refs[count:]
+    factor = factor_ref[0]
+    for j, ref in enumerate(parts):
+        to = at_ref[1] ^ j
+        for b in range(out_ref.shape[0]):
+            out_ref[b, to] = ref[b * part : (b + 1) * part].astype(wide) * factor
+        small_ref[to] = ref[out_ref.shape[0] * part :].astype(wide) * factor
+
+
+def collect_kernel(at_ref, slot_ref, scalar_ref, rest_ref, mid_ref, *refs, count, deep, per, columns):
+    terms, (own_ref, *out_refs) = refs[:count], refs[count : count + 1 + deep]
+    blocks = refs[-1]
+    part, width = rest_ref.shape[1:]
+    scale = 1.0 / scalar_ref[0]
+    both = fold([ref[0].astype(wide) for ref in terms])
+    late = both[:, width + 256 :]
+    remain = width - columns
+    pieces = [both[:, :width]]
+    for i in range(3):
+        first = mid_ref[:, width + i * columns : width + (i + 1) * columns]
+        pieces.append(jnp.concatenate([first, late[:, i * remain : (i + 1) * remain]], axis=1))
+    pieces.append(mid_ref[:, :width])
+    pieces += [rest_ref[i] for i in range(rest_ref.shape[0])]
+    squares = jnp.zeros((1, 1), wide)
+    total = jnp.zeros((part, width), wide)
+    for b, piece in enumerate(pieces):
+        piece = (piece * scale).astype(narrow)
+        blocks[b] = piece
+        own_ref[b * part : (b + 1) * part] = piece
+        total += jnp.square(piece.astype(wide))
+    small = (both[:, width : width + 256] * scale).astype(narrow)
+    third = part // 3
+    small = small.astype(wide)
+    squares = jnp.sum(total, keepdims=True) + jnp.sum(jnp.square(small), keepdims=True) + scalar_ref[1]
+    small = jnp.concatenate([small[i * third : (i + 1) * third] for i in range(3)], axis=1)
+    own_ref[len(pieces) * part :] = small.astype(narrow)
+    row = lax.broadcasted_iota(jnp.int32, (8, width), 0)
+    notes = jnp.zeros((8, width), wide)
+    for at, value in ((0, squares), (3, jnp.full((1, 1), scalar_ref[2]))):
+        for i in range(3):
+            piece = value.astype(narrow).astype(wide)
+            value = value - piece
+            notes = jnp.where(row == at + i, piece, notes)
+    notes = notes.astype(narrow)
+    blocks[len(pieces)] = jnp.zeros((part, width), narrow)
+    for k, out_ref in enumerate(out_refs):
+        for i in range(per):
+            slot = (at_ref[0] ^ k) * per + i
+            found = len(pieces)
+            for b in range(len(pieces)):
+                found = jnp.where(slot_ref[b] == slot, b, found)
+            out_ref[i * part : (i + 1) * part] = blocks[found]
+        out_ref[per * part :] = notes
+
+
+def collect_call(block_slot, scalars, rest, mid, terms, per, columns):
+    part, width = rest.shape[1:]
+    deep = lax.axis_size("fsdp")
+    count = block_slot.shape[0]
+    smem = pl.BlockSpec(memory_space=pltpu.SMEM)
+    message = jax.ShapeDtypeStruct((per * part + 8, width), narrow)
+    return pl.pallas_call(
+        functools.partial(collect_kernel, count=len(terms), deep=deep, per=per, columns=columns),
+        in_specs=[smem, smem, smem] + in_vmem(2 + len(terms)),
+        out_specs=in_vmem(1 + deep),
+        out_shape=[jax.ShapeDtypeStruct((count * part + part // 3, width), narrow)] + [message] * deep,
+        scratch_shapes=[pltpu.VMEM((count + 1, part, width), narrow)],
+        compiler_params=params(),
+        cost_estimate=cost(0, 4e6),
+    )(mesh_at(), block_slot, scalars, rest, mid, *terms)
+
+
+def halves(x):
+    high = x.astype(narrow)
+    return high, (x - high.astype(wide)).astype(narrow)
+
+
+def direction_kernel(at_ref, left_ref, right_ref, *refs, count, deep):
+    parts, slotted_ref, notes_ref = refs[:count], refs[count], refs[count + 1]
+    out_refs, rows, result = refs[count + 2 : count + 2 + deep], refs[-2], refs[-1]
+    per, _, part, width = left_ref.shape
+    for j, ref in enumerate(parts):
+        for k in range(deep):
+            f, s = at_ref[0] ^ k, at_ref[1] ^ j
+            for i in range(per):
+                rows[i, f * count + s] = ref[k, i * part : (i + 1) * part].astype(wide)
+            notes_ref[f, s] = ref[k, per * part :]
+    for i in range(per):
+        grad = rows[i].reshape(deep * count * part, width).astype(narrow)
+        slotted_ref[i] = grad
+        left_high, left_low = halves(left_ref[i].reshape(deep * part, width))
+        inner_high, inner_low = halves(dot(left_high, grad) + dot(left_low, grad))
+        right_high, right_low = halves(right_ref[i])
+        value = dot(inner_high, right_high) + dot(inner_low, right_high) + dot(inner_high, right_low)
+        result[i] = value.reshape(deep, part, width)
+    for k, out_ref in enumerate(out_refs):
+        for i in range(per):
+            out_ref[i] = result[i, at_ref[0] ^ k].astype(narrow)
+
+
+def direction_call(left, right, parts):
+    per, deep, part, width = left.shape
+    count = len(parts)
+    return pl.pallas_call(
+        functools.partial(direction_kernel, count=count, deep=deep),
+        in_specs=[pl.BlockSpec(memory_space=pltpu.SMEM)] + in_vmem(2 + count),
+        out_specs=in_vmem(2 + deep),
+        out_shape=[
+            jax.ShapeDtypeStruct((per, width, width), narrow),
+            jax.ShapeDtypeStruct((deep, count, 8, width), narrow),
         ]
-        view = fold(parts)
-    return view
-
-
-def all_sum(x):
-    for axis in ("fsdp", "seq"):
-        x = fold([swap(x, axis, k) for k in range(lax.axis_size(axis))])
-    return x
-
-
-def place_kernel(*refs, count):
-    base_ref, sources, out_ref, sem = refs[0], refs[1 : 1 + count], refs[1 + count], refs[2 + count]
-    copies = [
-        pltpu.make_async_copy(ref, out_ref.at[base_ref[0] ^ i], sem.at[i]) for i, ref in enumerate(sources)
-    ]
-    for copy in copies:
-        copy.start()
-    for copy in copies:
-        copy.wait()
-
-
-def placed(parts, base):
-    return pl.pallas_call(
-        functools.partial(place_kernel, count=len(parts)),
-        in_specs=[pl.BlockSpec(memory_space=pltpu.SMEM)] + [pl.BlockSpec(memory_space=pl.ANY)] * len(parts),
-        out_specs=pl.BlockSpec(memory_space=pl.ANY),
-        out_shape=jax.ShapeDtypeStruct((len(parts), *parts[0].shape), parts[0].dtype),
-        scratch_shapes=[pltpu.SemaphoreType.DMA((len(parts),))],
-        cost_estimate=cost(0, 2 * len(parts) * parts[0].size * 2),
-    )(base.reshape(1).astype(jnp.int32), *parts)
-
-
-def across(x):
-    size = lax.axis_size("seq")
-    me = lax.axis_index("seq")
-    held_parts = [swap(x, "seq", k) for k in range(0, size, 2)]
-    pair = held_parts + [swap(part, "seq", 1) for part in held_parts]
-    half = size // 2
-    order = [pair[(k // 2) + (k % 2) * half] for k in range(size)]
-    return placed(order, me)
-
-
-def gather_rows(shard):
-    n, rows, width = shard.shape
-    size, deep = lax.axis_size("seq"), lax.axis_size("fsdp")
-    me = lax.axis_index("seq")
-    mine = pick_index(shard.reshape(n, size, rows // size, width), me, 1)
-    every = placed([swap(mine, "fsdp", k) for k in range(deep)], lax.axis_index("fsdp"))
-    full = across(every)
-    return full.transpose(2, 1, 0, 3, 4).reshape(n, deep * rows, width)
-
-
-def gather_direct(x):
-    return placed([swap(x, "fsdp", k) for k in range(lax.axis_size("fsdp"))], lax.axis_index("fsdp"))
+        + [jax.ShapeDtypeStruct((per, part, width), narrow)] * deep,
+        scratch_shapes=[
+            pltpu.VMEM((per, deep * count, part, width), wide),
+            pltpu.VMEM((per, deep, part, width), wide),
+        ],
+        compiler_params=params(),
+        cost_estimate=cost(10 * per * deep * part * width * width, 16e6),
+    )(mesh_at(), left, right, *parts)
+
+
+def select_kernel(at_ref, slot_ref, *refs, deep):
+    parts, out_ref, slots = refs[:deep], refs[deep], refs[deep + 1]
+    per, part = parts[0].shape[:2]
+    for k, ref in enumerate(parts):
+        for i in range(per):
+            slots[(at_ref[0] ^ k) * per + i] = ref[i]
+    for b in range(out_ref.shape[0] // part):
+        out_ref[b * part : (b + 1) * part] = slots[slot_ref[b]]
+
+
+def select_call(block_slot, parts):
+    per, part, width = parts[0].shape
+    deep = len(parts)
+    smem = pl.BlockSpec(memory_space=pltpu.SMEM)
+    return pl.pallas_call(
+        functools.partial(select_kernel, deep=deep),
+        in_specs=[smem, smem] + in_vmem(deep),
+        out_specs=pl.BlockSpec(memory_space=pltpu.VMEM),
+        out_shape=jax.ShapeDtypeStruct((block_slot.shape[0] * part, width), narrow),
+        scratch_shapes=[pltpu.VMEM((deep * per, part, width), narrow)],
+        compiler_params=params(),
+        cost_estimate=cost(0, 2e6),
+    )(mesh_at(), block_slot, *parts)
+
+
+def update_kernel(at_ref, factor_ref, block_ref, *refs, count, part):
+    parts, out_ref = refs[:count], refs[count]
+    factor = factor_ref[0]
+    for j, ref in enumerate(parts):
+        to = at_ref[1] ^ j
+        for b in range(out_ref.shape[0]):
+            old = block_ref[b, to]
+            step = ref[b * part : (b + 1) * part].astype(wide) * factor
+            out_ref[b, to] = old - shampoo_rate * (step + decay_rate * old)
+
+
+def finish_call(kernel, factor, arrays, parts, part, shapes):
+    smem = pl.BlockSpec(memory_space=pltpu.SMEM)
+    return pl.pallas_call(
+        functools.partial(kernel, count=len(parts), part=part),
+        in_specs=[smem, smem] + in_vmem(len(arrays) + len(parts)),
+        out_specs=in_vmem(len(shapes)),
+        out_shape=[jax.ShapeDtypeStruct(shape, wide) for shape in shapes],
+        compiler_params=params(),
+        cost_estimate=cost(0, 12e6),
+    )(mesh_at(), factor.reshape(1), *arrays, *parts)
 
 
 def adam(weight, grad, first, second, rate, decay):
@@ -648,22 +981,23 @@
     lanes = pos_table.shape[2]
     width = lanes * deep
     grid_rows = pos_table.shape[1]
-    low = blocks.astype(narrow)
-
+
+    part = blocks.shape[1] // size
+    seen = jnp.broadcast_to(jnp.sum(res_weights).astype(wide), (lanes, 3))
     small = jnp.concatenate(
-        [pos_table.reshape(2 * grid_rows, lanes), gains, jnp.zeros((3, lanes), wide)], axis=0
+        [pos_table.reshape(2 * grid_rows, lanes).T, gains.T, seen, jnp.zeros((lanes, 120), wide)], axis=1
     ).astype(narrow)
-    small = gather_direct(small).transpose(1, 0, 2).reshape(2 * grid_rows + 8, width)
-    table = small[: 2 * grid_rows]
-    gains_full = small[2 * grid_rows :].astype(wide)
-    w_embed = gather_rows(low[0:1])
-    w_project = gather_rows(low[1:4])
-    w_rest = lax.all_gather(
-        pick_index(tied(low[4:13], w_embed).reshape(9, size, -1, width), me_s, 1), ("fsdp", "seq"), axis=1, tiled=True
-    )
-    w_head = lax.all_gather(
-        pick_index(tied(head.astype(narrow), w_embed).reshape(size, -1, head.shape[1]), me_s, 0), ("fsdp", "seq"), axis=0, tiled=True
-    )
+    opening = my_rows(jnp.concatenate([blocks[0].astype(narrow), small], axis=1)[None])[0]
+    project = my_rows(blocks[1:4]).astype(narrow).transpose(1, 0, 2).reshape(part, 3 * width)
+    every = far_exchange(near_exchange(jnp.concatenate([opening, project], axis=1)))
+    opening = seq_parts(stacked([x[:, :, : width + 256] for x in every]))
+    project = stacked([x[:, :, width + 256 :] for x in every])
+    w_embed = settle_rows(opening, [(0, part, 0, ())], [(deep, size, part, width + 256)])[0]
+    w_embed = w_embed.reshape(width, width + 256)
+    gains_full = w_embed[:, width + 128 :].T[:8].astype(wide)
+    weight_sum = jnp.sum(gains_full[5].reshape(deep * size, part)[:, 0])
+    w_rest = lax.all_gather(my_rows(tied(blocks[4:13], opening[-1])).astype(narrow), ("fsdp", "seq"), axis=1, tiled=True)
+    w_head = lax.all_gather(tied(my_rows(head.astype(narrow)[None])[0], opening[-1]), ("fsdp", "seq"), axis=0, tiled=True)
 
     places = positions[:, :, 0, :ROWS]
     grid = jnp.arange(grid_rows)
@@ -671,8 +1005,11 @@
     index = jnp.arange(256)
     ones = jnp.where(index[:, None] // HEAD == index[None] // HEAD, 1 / HEAD, 0).astype(narrow)
     pick = (jnp.arange(width)[:, None] // HEAD == jnp.arange(128)[None]).astype(narrow)
-    embed, first = embed_call(patches, hot, w_embed[0], table, gains_full)
-    query, keys, values, query_raw, key_raw = project_call(first, w_project, gains_full, ones)
+    embed, first = embed_call(patches, hot, tied(w_embed, project), gains_full)
+    w_project = settle_rows(
+        seq_parts(tied(project, opening[-1]), first), [(0, part, 0, ())], [(deep, size, part, 3 * width)]
+    )[0].reshape(width, 3 * width)
+    query, keys, values, *kept = project_call(first, w_project, gains_full, ones)
     mixed, rest, stat = attend_call(lengths, query, keys, values)
     second, act, slope, unit2, unit3, row_stat, pool = forward_call(lengths, embed, mixed, w_rest, gains_full)
 
@@ -684,88 +1021,103 @@
 
     pool = jnp.pad(pool[:, :2].reshape(seqs, width), ((0, spare), (0, 0)))
     loss, d_head, d_pool = head_call(
-        pool, column(1.0 / lengths.astype(wide)), column(res_weights), column(labels), w_head, narrow
-    )
-    lane = jnp.arange(128)[None]
-    totals = all_sum(jnp.where(lane == 0, loss[:1], jnp.where(lane == 1, jnp.sum(res_weights).astype(wide), 0.0)))
-    loss_sum, weight_sum = totals[0, 0], totals[0, 1]
+        pool, column(1.0 / lengths.astype(wide)), column(res_weights), column(labels), w_head
+    )
+    head_sum = lax.psum_scatter(d_head, "fsdp", scatter_dimension=0, tiled=True)
 
     dm, d_up, dr, d_mixed, delta, d_gain_rest = backward_call(
         lengths, d_pool[:seqs].reshape(mb, 2, width), unit3, unit2, row_stat, slope, mixed, rest, w_rest, gains_full, pick
     )
-    d_down = product("kmpe,mpd->ked", act, dm).astype(narrow)
-    d_upper = product("mpd,kmpe->kde", second, d_up).astype(narrow)
-    d_out = product("mpd,mpe->de", mixed, dr).astype(narrow)
-    own_down = scatter_sum(d_down)
-    own_upper = scatter_sum(d_upper)
-    own_out = scatter_sum(d_out[None])
-    own_head = scatter_sum(d_head[None])[0]
+    rest_core = core_terms(*weight_call(act, dm, second, d_up))
+    out_own, out_sent = one_weight_call(tied(mixed, rest_core[0]), dr)
+    rest_x = Sum([tied(rest_core[0], out_own), rest_core[1]], X)
+
     pairs = HEADS // 2
+    early = 4
     stats = jnp.stack([s[:, :, :HEADS].reshape(mb, ROWS, pairs, 2) for s in (stat, delta)], axis=3)
     stats = jnp.pad(stats.transpose(0, 2, 3, 4, 1).reshape(mb, pairs, 4, ROWS), ((0, 0), (0, 0), (0, 4), (0, 0)))
     stats = stats.reshape(mb, 8 * pairs, ROWS)
-    dq, dk, dv, d_gain_heads = attend_back_call(
-        lengths, query, keys, values, d_mixed, query_raw, key_raw, stats, gains_full, ones[:128, :128], 0, pairs
-    )
-    d_project = jnp.stack([product("mpd,mpe->de", first, x).astype(narrow) for x in (dq, dk, dv)])
-    own_project = scatter_sum(d_project)
-    d_embed, d_gain_first = first_call((dq, dk, dv), embed, dr, w_project, gains_full)
-    d_e = product("mpd,mpe->de", patches[:, 0, :ROWS], d_embed).astype(narrow)
-    own_e = scatter_sum(d_e[None])
-    d_table = product("mpd,mpe->de", hot, d_embed)
-    d_gain_heads = d_gain_heads.transpose(1, 0, 2).reshape(8, width)
-    d_small = jnp.concatenate(
-        [d_table, d_gain_first[:1], d_gain_heads[:2], d_gain_rest[3:5], jnp.zeros((3, width), wide)], axis=0
-    )
-    d_small = d_small.reshape(-1, deep, lanes).transpose(1, 0, 2)
-    d_small = fold([swap(pick_index(d_small, me_f ^ k, 0), "fsdp", k) for k in range(deep)])
-    d_small = fold([swap(d_small, "seq", k) for k in range(size)]) / weight_sum
-
-    own = (jnp.concatenate([own_e, own_project, own_out, own_upper, own_down]) / weight_sum).astype(narrow)
-    own_head = (own_head / weight_sum).astype(narrow)
-    squares = (
-        jnp.sum(jnp.square(own.astype(wide)))
-        + jnp.sum(jnp.square(own_head.astype(wide)))
-        + jnp.where(me_s == 0, jnp.sum(jnp.square(d_small)), 0.0)
-    )
-    clip_norm = jnp.sqrt(all_sum(jnp.broadcast_to(squares, (1, 128)))[0, 0])
+
+    def heads_back(after, start, count):
+        out = attend_back_call(
+            lengths, tied(query, *after), keys, values, d_mixed, kept, stats, gains_full,
+            ones, start, count,
+        )
+        return out[:3], out[3]
+
+    grads_one, gain_one = heads_back(rest_x.sent, 0, early)
+    rest_y = Sum(rest_x.after(grads_one[0]), Y)
+    head_sum = lax.psum(tied(head_sum, *rest_y.sent), "seq")
+    one_own, one_sent = one_weight_call(tied(first, *rest_y.sent), *grads_one)
+    mid_core = core_terms(
+        jnp.concatenate([out_own, one_own], axis=5), jnp.concatenate([out_sent, one_sent], axis=5)
+    )
+    mid_x = Sum(mid_core, X)
+    grads_two, gain_two = heads_back(rest_y.sent + mid_x.sent, early, pairs - early)
+    rest_z = Sum(rest_y.after(grads_two[0]), Z)
+    mid_y = Sum(mid_x.after(grads_two[0]), Y)
+    late_core = core_terms(*one_weight_call(tied(first, *rest_z.sent, *mid_y.sent), *grads_two))
+    late_x = Sum(late_core, X)
+    mid_z = Sum(mid_y.after(late_core[0]), Z)
+    d_embed, d_gain_first = first_call(
+        (*grads_one, *grads_two), embed, tied(dr, *late_x.sent, *mid_z.sent), w_project, gains_full
+    )
+    late_y = Sum(late_x.after(d_embed), Y)
+    own_rest, own_mid = fold([x.astype(wide) for x in rest_z.after(d_embed)]), fold(
+        [x.astype(wide) for x in mid_z.after(d_embed)]
+    )
+    d_gain_heads = jnp.concatenate([gain_one, gain_two], axis=0).transpose(1, 0, 2).reshape(8, width)
+    d_gains = jnp.concatenate(
+        [d_gain_first[:1], d_gain_heads[:2], d_gain_rest[3:5], jnp.zeros((123, width), wide)], axis=0
+    ).T
+    head_sum = tied(head_sum, late_core[0]) / weight_sum
+    head_squares = jnp.where(me_s == 0, jnp.sum(jnp.square(head_sum)), 0.0)
+    scalars = jnp.stack([weight_sum, head_squares, loss[0, 0]])
+    left_part = pick_index(left_roots.reshape(left_roots.shape[0], deep, size, part, width), me_s, 2)
+    e_own, e_sent = embed_weight_call(
+        patches, hot, tied(d_embed, own_rest, own_mid, scalars, left_part, *late_y.sent), d_gains
+    )
+    last_y = Sum(Sum(core_terms(e_own, e_sent), X).terms, Y)
+    both_z = Sum(
+        [jnp.concatenate([a.astype(wide), b.astype(wide)], axis=3) for a, b in zip(last_y.terms, late_y.terms)], Z
+    )
+
+    per = left_stats.shape[0]
+    count = blocks.shape[0]
+    own, *outgoing = collect_call(
+        block_slot, scalars, own_rest, own_mid[0], both_z.terms, per,
+        early * 2 * HEAD,
+    )
+    arrived = seq_parts(jnp.stack([swap(x, "fsdp", k) for k, x in enumerate(outgoing)]))
+    slotted, notes, *directions = direction_call(left_part, right_roots, arrived)
+    notes = jnp.sum(notes[:, :, :, 0].astype(wide), axis=(0, 1))
+    loss_sum = notes[3] + notes[4] + notes[5]
+    clip_norm = jnp.sqrt(notes[0] + notes[1] + notes[2])
     factor = jnp.minimum(1.0, clip_bound / clip_norm)
-
-    per = left_stats.shape[0]
-    part = own.shape[1]
-    slot_hot = block_slot[None, :] == jnp.arange(per * deep)[:, None]
-    outgoing = jnp.einsum("sb,brd->srd", slot_hot.astype(narrow), own).reshape(deep, per, part, width)
-    arrived = placed([swap(pick_index(outgoing, me_f ^ k, 0), "fsdp", k) for k in range(deep)], me_f)
-    slotted = across(arrived)
-    slotted = slotted.transpose(2, 1, 0, 3, 4).reshape(per, width, width)
-    left_part = pick_index(left_roots.reshape(per, deep, size, part, width), me_s, 2).reshape(per, deep * part, width)
-    inner = jnp.einsum("sij,sjk->sik", left_part, slotted.astype(wide), precision=lax.Precision.HIGH)
-    direction = jnp.einsum("sij,sjk->sik", inner, right_roots, precision=lax.Precision.HIGH).astype(narrow)
-    direction = direction.reshape(per, deep, part, width)
-    back = placed([swap(pick_index(direction, me_f ^ k, 1), "fsdp", k) for k in range(deep)], me_f)
-    back = back.reshape(per * deep, part, width)
-    back = jnp.einsum("sb,srd->brd", slot_hot.astype(narrow), back)
-
-    def rows_of(x):
-        return x.transpose(1, 0, 2, 3).reshape(x.shape[1], size * part, x.shape[3])
-
-    block_direction = rows_of(across(back)).astype(wide) * factor
-    blocks_new = blocks - shampoo_rate * (block_direction + decay_rate * blocks)
-    block_grads = rows_of(across(own)).astype(wide) * factor
+    back = select_call(block_slot, [swap(x, "fsdp", k) for k, x in enumerate(directions)])
+    split = (count, size, part, width)
+    block_grads, small_grad = finish_call(
+        grads_kernel, factor, [], seq_parts(tied(own, slotted)), part, [split, (size, part // 3, width)]
+    )
+    blocks_new = finish_call(update_kernel, factor, [blocks.reshape(split)], seq_parts(back), part, [split])[0]
+    blocks_new = blocks_new.reshape(blocks.shape)
+    block_grads = block_grads.reshape(blocks.shape)
+    slotted = tied(slotted, back)
     gram_left = product("sij,skj->sik", slotted, slotted)
     gram_right = product("sji,sjk->sik", slotted, slotted)
     left_new = stat_decay * left_stats + ((1 - stat_decay) * factor * factor) * gram_left
     right_new = stat_decay * right_stats + ((1 - stat_decay) * factor * factor) * gram_right
 
-    table_grad = d_small[: 2 * grid_rows].reshape(2, grid_rows, lanes) * factor
-    gain_grad = d_small[2 * grid_rows : 2 * grid_rows + 5] * factor
-    head_grad = rows_of(across(own_head[None]))[0].astype(wide) * factor
+    small_grad = jnp.concatenate([small_grad[:, :, i * 256 : (i + 1) * 256] for i in range(3)], axis=1)
+    small_grad = small_grad.reshape(lanes, 256).T
+    table_grad = small_grad[: 2 * grid_rows].reshape(2, grid_rows, lanes)
+    gain_grad = small_grad[2 * grid_rows : 2 * grid_rows + 5]
     pos_new, pos_first_new, pos_second_new = adam(
         pos_table, table_grad, pos_first, pos_second, table_rate, decay_rate
     )
     gains_new, gain_first_new, gain_second_new = adam(gains, gain_grad, gain_first, gain_second, gain_rate, 0.0)
     head_new, head_first_new, head_second_new = adam(
-        head, head_grad, head_first, head_second, adam_rate, decay_rate
+        head, tied(head_sum, back) * factor, head_first, head_second, adam_rate, decay_rate
     )
     return (
         blocks_new, block_grads, left_new, right_new, pos_new, pos_first_new, pos_second_new,

time: 1340 us -> 732 us (0.55)
  Pallas kernels: 774 us -> 432 us
  starting transfers between devices: 156 us -> 68.9 us
  matrix products: 95.6 us -> 12.4 us
  waiting for transfers between devices: 184 us -> 106 us
  local copies, waits for them, and re-layouts: 67.3 us -> 32.7 us
  other arithmetic: 33.3 us -> 51.2 us
    pallas_call x11 -> x12, Pallas kernels: 429 us -> 106 us  [the longest x1 36 us: weight_call(): pl.pallas_call(weight_kernel, grid_spec=pltpu.PrefetchScalarGridSpec(num_...]
    ppermute x119 -> x54, waiting for transfers between devices: 183 us -> 91.2 us  [swap(): lax.ppermute(x, axis, [(i, i ^ bits) for i in range(lax.axis_size(axis))])]
    ppermute x119 -> x54, starting transfers between devices: 156 us -> 68.6 us  [swap(): lax.ppermute(x, axis, [(i, i ^ bits) for i in range(lax.axis_size(axis))])]
    dot_general x10 -> x2, matrix products: 88.3 us -> 12.4 us  [product(): return jnp.einsum(spec_text, a, b, preferred_element_type=wide)]
    pallas_call x1, Pallas kernels: 68.6 us -> 50.8 us  [forward_call(): pl.pallas_call(forward_kernel, grid_spec=pltpu.PrefetchScalarGridSpec(num...]
    dynamic_slice x13 -> x0, local copies, waits for them, and re-layouts: 17 us -> none  [pick_index(): return lax.dynamic_index_in_dim(x, index, dim, keepdims=False)]
    psum x0 -> x1, waiting for transfers between devices: none -> 14.9 us  [local(): head_sum = lax.psum(tied(head_sum, *rest_y.sent), 'seq')]
    convert_element_type x3 -> x9, other arithmetic: 3.72 us -> 17.7 us  [the longest x7 17.1 us: __init__(): self.sent = [part(k).astype(narrow) for k in range(1, size)]]
  transfers between devices with their start and end apart: 121 -> 58, of which waited for: 38 -> 20; matrix products, arithmetic and copies ran while one was open for 13% -> 11% of each run, Pallas kernels for 48% -> 43%
where the time goes in v2:
time: 732 us; the launch traced here: 726 us
  Pallas kernels  432 us (59%)
  waiting for transfers between devices  106 us (14%)
  starting transfers between devices  68.9 us (9%)
  other arithmetic  51.2 us (7%)
  local copies, waits for them, and re-layouts  32.7 us (4%)
  between operations  22.5 us (3%)
  matrix products  12.4 us (2%)
    pallas_call x2, Pallas kernels, attend_back_call(): pl.pallas_call(attend_back_kernel, grid_spec=pltpu.PrefetchScalarGridSpec...  107 us
    ppermute x54, waiting for transfers between devices, swap(): lax.ppermute(x, axis, [(i, i ^ bits) for i in range(lax.axis_size(axis))])  91.2 us
    ppermute x54, starting transfers between devices, swap(): lax.ppermute(x, axis, [(i, i ^ bits) for i in range(lax.axis_size(axis))])  68.6 us
    pallas_call x1, Pallas kernels, backward_call(): pl.pallas_call(backward_kernel, grid_spec=pltpu.PrefetchScalarGridSpec(nu...  55.1 us
    pallas_call x1, Pallas kernels, attend_call(): pl.pallas_call(attend_kernel, grid_spec=pltpu.PrefetchScalarGridSpec(num_...  52.3 us
    pallas_call x1, Pallas kernels, forward_call(): pl.pallas_call(forward_kernel, grid_spec=pltpu.PrefetchScalarGridSpec(num...  50.8 us
    pallas_call x1, Pallas kernels, weight_call(): pl.pallas_call(weight_kernel, grid_spec=pltpu.PrefetchScalarGridSpec(num_...  36 us
    pallas_call x3, Pallas kernels, one_weight_call(): pl.pallas_call(functools.partial(one_weight_kernel, count=len(b)), grid_s...  32.2 us
  transfers between devices with their start and end apart: 58, of which 20 were waited for; matrix products, arithmetic and copies ran while one was open for 11% of the time, Pallas kernels for 43%

profile of v2, /device:TPU:0, one launch (start us, length us, event | category | flops | bytes accessed | tf_op | source)
XLA Modules:
  0.0 726.0 jit_solution(728485851049285606)
XLA Ops:
  26.3 20.0 %collective-permute-done.2 = bf16[2,24,3328]{2,1,0:T(8,128)(2,1)S(1)} collective-permute-done((bf16[2,24,3328]{2,1,0:T(8,128)(2,1)S(1)}, bf16[2,24,3328]{2,1,0:T(8,128)(2,1)S(1)}, u32[]{:S(2)}, u32[]{:S(2)}) %collective-permute-start.2) | collective-permute-done | bytes 319520 | tf_op jit(solution)/shard_map/ppermute | solution.py:683
  48.7 7.4 %collective-permute-done.5.refs_2_ = bf16[8,24,1024]{2,1,0:T(8,128)(2,1)S(1)} collective-permute-done((bf16[8,24,1024]{2,1,0:T(8,128)(2,1)S(1)}, bf16[8,24,1024]{2,1,0:T(8,128)(2,1)S(1)}, u32[]{:S(2)}, u32[]{:S(2)}) %collective-permute-start.5) | collective-permute-done | bytes 393248 | tf_op jit(solution)/shard_map/ppermute | solution.py:683
  70.7 12.0 %shard_map.316 = (f32[2,1408,768]{2,1,0:T(8,128)}, bf16[2,1408,768]{2,1,0:T(8,128)(2,1)}) custom-call(bf16[2,1,1536,768]{3,2,1,0:T(8,128)(2,1)} %patch_ref.3, bf16[2,1408,128]{2,1,0:T(8,128)(2,1)} %add_convert_fusion.3.hot_ref, bf16[768,1024]{1,0:T(8,128)(2,1)} %bitcast.202, f32[8,768]{1,0:T(8,128)} %slice_convert_fusion.1.gain_ref.refs_9_), custom_call_target="tpu_custom_call" | custom-call | flops 3875536896 | bytes 20000000 | tf_op jit(solution)/shard_map/pallas_call | solution.py:80
  93.1 22.7 %shard_map.318 = (bf16[2,1408,768]{2,1,0:T(8,128)(2,1)}, bf16[2,1408,768]{2,1,0:T(8,128)(2,1)}, bf16[2,1408,768]{2,1,0:T(8,128)(2,1)}, bf16[2,1408,768]{2,1,0:T(...) custom-call(bf16[2,1408,768]{2,1,0:T(8,128)(2,1)} %get-tuple-element.150.fi, ...), custom_call_target="tpu_custom_call" | custom-call | flops 9965666304 | bytes 30000000 | tf_op jit(solution)/shard_map/pallas_call | solution.py:126
  115.8 52.3 %shard_map.319 = (bf16[2,1408,768]{2,1,0:T(8,128)(2,1)}, bf16[2,1408,768]{2,1,0:T(8,128)(2,1)}, f32[2,1408,128]{2,1,0:T(8,128)}) custom-call(s32[2,2]{1,0:T(2,128)} %bitcast.236, bf16[2,1408,768]{2,1,0:T(8,128)(2,1)} %get-tuple-element.156.q_ref, bf16[2,1408,768]{2,1,0:T(8,128)(2,1)} %get-tuple-element.116.k_ref, bf16[2,1408,768]{2,1,0:T(8,128)(2,1)} %get-tuple-element.117.v_ref), custom_call_target="tpu_custom_call" | custom-call | flops 34225520640 | bytes 17301504 | tf_op jit(solution)/shard_map/pallas_call | solution.py:191
  168.1 50.8 %shard_map.320 = (bf16[2,1408,768]{2,1,0:T(8,128)(2,1)}, bf16[4,2,1408,768]{3,2,1,0:T(8,128)(2,1)}, bf16[4,2,1408,768]{3,2,1,0:T(8,128)(2,1)}, bf16[2,1408,768]{...) custom-call(s32[2,2]{1,0:T(2,128)} %bitcast.237, ...), custom_call_target="tpu_custom_call" | custom-call | flops 29896998912 | bytes 80000000 | tf_op jit(solution)/shard_map/pallas_call | solution.py:256
  228.1 55.1 %shard_map.322 = (bf16[2,1408,768]{2,1,0:T(8,128)(2,1)}, bf16[4,2,1408,768]{3,2,1,0:T(8,128)(2,1)}, bf16[2,1408,768]{2,1,0:T(8,128)(2,1)}, bf16[2,1408,768]{2,1,...) custom-call(s32[2,2]{1,0:T(2,128)} %bitcast.238, f32[2,2,768]{2,1,0:T(2,128)} %reshape.919.dpool_ref, ...), custom_call_target="tpu_custom_call" | custom-call | flops 29896998912 | bytes 70000000 | tf_op jit(solution)/shard_map/pallas_call | solution.py:362
  283.2 36.0 %shard_map.323 = (bf16[2,2,4,8,24,768]{5,4,3,2,1,0:T(8,128)(2,1)}, bf16[2,2,4,8,24,768]{5,4,3,2,1,0:T(8,128)(2,1)}) custom-call(s32[1]{0:T(128)} %bitcast.35.at_ref, bf16[4,2,1408,768]{3,2,1,0:T(8,128)(2,1)} %get-tuple-element.123.act_ref, bf16[2,1408,768]{2,1,0:T(8,128)(2,1)} %get-tuple-element.130.dm_ref, ...), custom_call_target="tpu_custom_call" | custom-call | flops 26575110144 | bytes 60000000 | tf_op jit(solution)/shard_map/pallas_call | solution.py:561
  320.2 8.0 %shard_map.324 = (bf16[2,2,4,1,24,768]{5,4,3,2,1,0:T(8,128)(2,1)}, bf16[2,2,4,1,24,768]{5,4,3,2,1,0:T(8,128)(2,1)}) custom-call(s32[1]{0:T(128)} %bitcast.35.at_ref, bf16[2,1408,768]{2,1,0:T(8,128)(2,1)} %get-tuple-element.134.mixed_ref.a_ref, bf16[2,1408,768]{2,1,0:T(8,128)(2,1)} %get-tuple-element.168.refs_0_.refs_7_), custom_call_target="tpu_custom_call" | custom-call | flops 3321888768 | bytes 12000000 | tf_op jit(solution)/shard_map/pallas_call | solution.py:610
  329.8 7.2 fusion
  338.4 70.6 %shard_map.325 = (bf16[2,1408,512]{2,1,0:T(8,128)(2,1)}, bf16[2,1408,512]{2,1,0:T(8,128)(2,1)}, bf16[2,1408,512]{2,1,0:T(8,128)(2,1)}, f32[4,8,128]{2,1,0:T(8,128)}) custom-call(s32[2,2]{1,0:T(2,128)} %bitcast.239, bf16[2,1408,768]{2,1,0:T(8,128)(2,1)} %get-tuple-element.156.q_ref, bf16[2,1408,768]{2,1,0:T(8,128)(2,1)} %get-tuple-element.116.k_ref, ...), custom_call_target="tpu_custom_call" | custom-call | flops 57042534400 | bytes 25952256 | tf_op jit(solution)/shard_map/pallas_call | solution.py:460
  413.7 13.3 %shard_map.326 = (bf16[2,2,4,1,24,1536]{5,4,3,2,1,0:T(8,128)(2,1)}, bf16[2,2,4,1,24,1536]{5,4,3,2,1,0:T(8,128)(2,1)}) custom-call(s32[1]{0:T(128)} %bitcast.35.at_ref, bf16[2,1408,768]{2,1,0:T(8,128)(2,1)} %get-tuple-element.150.first_ref.a_ref, bf16[2,1408,512]{2,1,0:T(8,128)(2,1)} %get-tuple-element.147.refs_0_, ...), custom_call_target="tpu_custom_call" | custom-call | flops 6643777536 | bytes 12000000 | tf_op jit(solution)/shard_map/pallas_call | solution.py:610
  443.9 36.6 %shard_map.327 = (bf16[2,1408,256]{2,1,0:T(8,128)(2,1)}, bf16[2,1408,256]{2,1,0:T(8,128)(2,1)}, bf16[2,1408,256]{2,1,0:T(8,128)(2,1)}, f32[2,8,128]{2,1,0:T(8,128)}) custom-call(s32[2,2]{1,0:T(2,128)} %bitcast.240, bf16[2,1408,768]{2,1,0:T(8,128)(2,1)} %get-tuple-element.156.q_ref, bf16[2,1408,768]{2,1,0:T(8,128)(2,1)} %get-tuple-element.116.k_ref, ...), custom_call_target="tpu_custom_call" | custom-call | flops 28521267200 | bytes 12976128 | tf_op jit(solution)/shard_map/pallas_call | solution.py:460
  487.0 7.9 %collective-permute-start.18 = (bf16[8,24,768]{2,1,0:T(8,128)(2,1)}, bf16[8,24,768]{2,1,0:T(8,128)(2,1)}, u32[]{:S(2)}, u32[]{:S(2)}) collective-permute-start(bf16[8,24,768]{2,1,0:T(8,128)(2,1)} %get-tuple-element.225), channel_id=1, source_target_pairs={{0,4},{1,5},{2,6},{3,7},{4,0},{5,1},{6,2},{7,3},{8,12},{9,13},{10,... | collective-permute-start | bytes 884744 | tf_op jit(solution)/shard_map/ppermute | solution.py:683
  495.5 10.9 %shard_map.328 = (bf16[2,2,4,1,24,768]{5,4,3,2,1,0:T(8,128)(2,1)}, bf16[2,2,4,1,24,768]{5,4,3,2,1,0:T(8,128)(2,1)}) custom-call(s32[1]{0:T(128)} %bitcast.35.at_ref, bf16[2,1408,768]{2,1,0:T(8,128)(2,1)} %get-tuple-element.150.first_ref.a_ref, bf16[2,1408,256]{2,1,0:T(8,128)(2,1)} %get-tuple-element.157.refs_0_.refs_3_, ...), custom_call_target="tpu_custom_call" | custom-call | flops 3321888768 | bytes 12000000 | tf_op jit(solution)/shard_map/pallas_call | solution.py:610
  506.4 14.9 %all-reduce.7.cloned.1.call-done = f32[96,1000]{1,0:T(8,128)} async-done(((f32[96,1000]{1,0:T(8,128)}), f32[96,1000]{1,0:T(8,128)}) %all-reduce.7.cloned.1.call-update) | async-done | bytes 384016 | tf_op jit(solution)/shard_map/psum | solution.py:1050
  540.2 21.2 %shard_map.329 = (bf16[2,1408,768]{2,1,0:T(8,128)(2,1)}, f32[8,768]{1,0:T(8,128)}) custom-call(bf16[2,1408,512]{2,1,0:T(8,128)(2,1)} %get-tuple-element.147.refs_0_, bf16[2,1408,512]{2,1,0:T(8,128)(2,1)} %get-tuple-element.151.refs_1_, bf16[2,1408,512]{2,1,0:T(8,128)(2,1)} %get-tuple-element.152.refs_2_, ...), custom_call_target="tpu_custom_call" | custom-call | flops 9965666304 | bytes 32000000 | tf_op jit(solution)/shard_map/pallas_call | solution.py:504
  571.1 9.6 %shard_map.330 = (bf16[2,2,4,1,24,1024]{5,4,3,2,1,0:T(8,128)(2,1)}, bf16[2,2,4,1,24,1024]{5,4,3,2,1,0:T(8,128)(2,1)}) custom-call(s32[1]{0:T(128)} %bitcast.35.at_ref, bf16[2,1,1536,768]{3,2,1,0:T(8,128)(2,1)} %patch_ref.3, bf16[2,1408,128]{2,1,0:T(8,128)(2,1)} %add_convert_fusion.3.hot_ref, bf16[2,1408,768]{2,1,0:T(8,128)(2,1)} %get-tuple-element.173.grad_ref, ...), custom_call_target="tpu_custom_call" | custom-call | flops 3875536896 | bytes 12000000 | tf_op jit(solution)/shard_map/pallas_call | solution.py:654
  585.1 10.7 %collective-permute-done.25 = bf16[2,4,1,24,1024]{4,3,1,2,0:T(8,128)(2,1)S(1)} collective-permute-done((bf16[2,4,1,24,1024]{4,3,1,2,0:T(8,128)(2,1)S(1)}, bf16[2,4,1,24,1024]{4,3,1,2,0:T(8,128)(2,1)S(1)}, u32[]{:S(2)}, u32[]{:S(2)}) %collective-permute-start.25) | collective-permute-done | bytes 393248 | tf_op jit(solution)/shard_map/ppermute | solution.py:683
  598.0 7.2 collective-permute-done.27
  637.7 12.1 %collective-permute-done.39.refs_2_ = bf16[8,56,768]{2,1,0:T(8,128)(2,1)S(1)} collective-permute-done((bf16[8,56,768]{2,1,0:T(8,128)(2,1)S(1)}, bf16[8,56,768]{2,1,0:T(8,128)(2,1)S(1)}, u32[]{:S(2)}, u32[]{:S(2)}) %collective-permute-start.39) | collective-permute-done | bytes 688160 | tf_op jit(solution)/shard_map/ppermute | solution.py:683
  652.9 8.5 %shard_map.332 = (bf16[2,768,768]{2,1,0:T(8,128)(2,1)}, bf16[8,4,8,768]{3,2,1,0:T(8,128)(2,1)}, bf16[2,24,768]{2,1,0:T(8,128)(2,1)}, bf16[2,24,768]{2,1,0:T(8,12...) custom-call(s32[2]{0:T(128)} %pad_add_fusion.at_ref, ...), custom_call_target="tpu_custom_call" | custom-call | flops 2264924160 | bytes 16000000 | tf_op jit(solution)/shard_map/pallas_call | solution.py:891
  661.9 5.8 collective-permute-start.42
  687.3 8.2 %multiply_add_fusion = f32[2,768,768]{2,1,0:T(8,128)} fusion(f32[2,768,768]{2,1,0:T(8,128)} %param.31, f32[]{:T(128)S(6)} %mul.149, bf16[2,768,768]{2,1,0:T(8,128)(2,1)} %get-tuple-element.201), kind=kOutput, calls=%fused_computation | convolution fusion | flops 1815478272 | bytes 11796484 | tf_op jit(solution)/shard_map/sji,sjk->sik/dot_general | solution.py:969
  (343 shorter events, 194.4 us)
Async XLA Ops:
  7.2 160.9 %all-gather.6.cloned.1.call-start = ((), (), s32[]{:S(2)}) async-start(), calls=%async_computation.4 | async-start | bytes 10948608 | tf_op jit(solution)/shard_map/all_gather | solution.py:999
  21.8 24.5 %collective-permute-start.2 = (bf16[2,24,3328]{2,1,0:T(8,128)(2,1)S(1)}, bf16[2,24,3328]{2,1,0:T(8,128)(2,1)S(1)}, u32[]{:S(2)}, u32[]{:S(2)}) collective-permute-start(bf16[2,24,3328]{2,1,0:T(8,128)(2,1)S(1)} %pad_maximum_fusion.2), channel_id=1, source_target_pairs={{0,4},{1,5},{2,6},{3,7},{4,0},{5,1},{6,2},{7,3},{8,12},{9,13},{10,... | collective-permute-start | bytes 958472 | tf_op jit(solution)/shard_map/ppermute | solution.py:683
  24.7 21.6 %collective-permute-start.1 = (bf16[2,24,3328]{2,1,0:T(8,128)(2,1)S(1)}, bf16[2,24,3328]{2,1,0:T(8,128)(2,1)S(1)}, u32[]{:S(2)}, u32[]{:S(2)}) collective-permute-start(bf16[2,24,3328]{2,1,0:T(8,128)(2,1)S(1)} %pad_maximum_fusion.2), channel_id=1, source_target_pairs={{0,2},{1,3},{2,0},{3,1},{4,6},{5,7},{6,4},{7,5},{8,10},{9,11},{10,... | collective-permute-start | bytes 958472 | tf_op jit(solution)/shard_map/ppermute | solution.py:683
  26.3 20.1 %collective-permute-start.3 = (bf16[2,24,3328]{2,1,0:T(8,128)(2,1)S(1)}, bf16[2,24,3328]{2,1,0:T(8,128)(2,1)S(1)}, u32[]{:S(2)}, u32[]{:S(2)}) collective-permute-start(bf16[2,24,3328]{2,1,0:T(8,128)(2,1)S(1)} %pad_maximum_fusion.2), channel_id=1, source_target_pairs={{0,6},{1,7},{2,4},{3,5},{4,2},{5,3},{6,0},{7,1},{8,14},{9,15},{10,... | collective-permute-start | bytes 958472 | tf_op jit(solution)/shard_map/ppermute | solution.py:683
  59.1 161.3 %all-gather.4.cloned.1.call-start = ((), (), s32[]{:S(2)}) async-start(), calls=%async_computation.1 | async-start | bytes 1622016 | tf_op jit(solution)/shard_map/all_gather | solution.py:1000
  62.1 24.1 %collective-permute-start.8 = (bf16[8,24,2304]{2,1,0:T(8,128)(2,1)S(1)}, bf16[8,24,2304]{2,1,0:T(8,128)(2,1)S(1)}, u32[]{:S(2)}, u32[]{:S(2)}) collective-permute-start(bf16[8,24,2304]{2,1,0:T(8,128)(2,1)S(1)} %bitcast.197), channel_id=1, source_target_pairs={{0,16},{8,24},{16,0},{24,8},{1,17},{9,25},{17,1},{25,9},{2,18},{10... | collective-permute-start | bytes 2654216 | tf_op jit(solution)/shard_map/ppermute | solution.py:683
  69.8 19.2 %collective-permute-start.7 = (bf16[8,24,2304]{2,1,0:T(8,128)(2,1)S(1)}, bf16[8,24,2304]{2,1,0:T(8,128)(2,1)}, u32[]{:S(2)}, u32[]{:S(2)}) collective-permute-start(bf16[8,24,2304]{2,1,0:T(8,128)(2,1)S(1)} %bitcast.198), channel_id=1, source_target_pairs={{0,8},{8,0},{16,24},{24,16},{1,9},{9,1},{17,25},{25,17},{2,10},{10... | collective-permute-start | bytes 2654216 | tf_op jit(solution)/shard_map/ppermute | solution.py:683
  88.8 392.4 %reduce-scatter.2.cloned.1.call-start = ((), (), s32[]{:S(2)}) async-start(), calls=%async_computation.2 | async-start | bytes 3538944 | tf_op jit(solution)/shard_map/reduce_scatter | solution.py:1026
  320.1 201.1 %all-reduce.7.cloned.1.call-start = ((), (), s32[]{:S(2)}) async-start(), calls=%async_computation.3 | async-start | bytes 786432 | tf_op jit(solution)/shard_map/psum | solution.py:1050
  336.9 72.1 %collective-permute-start.11 = (bf16[2,4,8,24,768]{4,3,2,1,0:T(8,128)(2,1)S(1)}, bf16[2,4,8,24,768]{4,3,2,1,0:T(8,128)(2,1)}, u32[]{:S(2)}, u32[]{:S(2)}) collective-permute-start(bf16[2,4,8,24,768]{4,3,2,1,0:T(8,128)(2,1)S(1)} %get-tuple-element.217), channel_id=1, source_target_pairs={{0,16},{8,24},{16,0},{24,8},{1,17},{9,25},{17,1},{25,9},{2,18},{10... | collective-permute-start | bytes 7077896 | tf_op jit(solution)/shard_map/ppermute | solution.py:683
  438.4 43.8 %collective-permute-start.13 = (bf16[4,8,24,768]{3,2,1,0:T(8,128)(2,1)}, bf16[4,8,24,768]{3,2,1,0:T(8,128)(2,1)}, u32[]{:S(2)}, u32[]{:S(2)}) collective-permute-start(bf16[4,8,24,768]{3,2,1,0:T(8,128)(2,1)} %get-tuple-element.220), channel_id=1, source_target_pairs={{0,1},{1,0},{2,3},{3,2},{4,5},{5,4},{6,7},{7,6},{8,9},{9,8},{10,11... | collective-permute-start | bytes 3538952 | tf_op jit(solution)/shard_map/ppermute | solution.py:683
  443.4 77.8 %collective-permute-start.14 = (bf16[2,4,1,24,2304]{4,3,1,2,0:T(8,128)(2,1)}, bf16[2,4,1,24,2304]{4,3,1,2,0:T(8,128)(2,1)}, u32[]{:S(2)}, u32[]{:S(2)}) collective-permute-start(bf16[2,4,1,24,2304]{4,3,1,2,0:T(8,128)(2,1)} %get-tuple-element.221), channel_id=1, source_target_pairs={{0,16},{8,24},{16,0},{24,8},{1,17},{9,25},{17,1},{25,9},{2,18},{10... | collective-permute-start | bytes 2654216 | tf_op jit(solution)/shard_map/ppermute | solution.py:683
  484.5 78.9 %collective-permute-start.19 = (bf16[8,24,768]{2,1,0:T(8,128)(2,1)}, bf16[8,24,768]{2,1,0:T(8,128)(2,1)}, u32[]{:S(2)}, u32[]{:S(2)}) collective-permute-start(bf16[8,24,768]{2,1,0:T(8,128)(2,1)} %get-tuple-element.224), channel_id=1, source_target_pairs={{0,6},{1,7},{2,4},{3,5},{4,2},{5,3},{6,0},{7,1},{8,14},{9,15},{10,... | collective-permute-start | bytes 884744 | tf_op jit(solution)/shard_map/ppermute | solution.py:683
  487.0 76.5 %collective-permute-start.18 = (bf16[8,24,768]{2,1,0:T(8,128)(2,1)}, bf16[8,24,768]{2,1,0:T(8,128)(2,1)}, u32[]{:S(2)}, u32[]{:S(2)}) collective-permute-start(bf16[8,24,768]{2,1,0:T(8,128)(2,1)} %get-tuple-element.225), channel_id=1, source_target_pairs={{0,4},{1,5},{2,6},{3,7},{4,0},{5,1},{6,2},{7,3},{8,12},{9,13},{10,... | collective-permute-start | bytes 884744 | tf_op jit(solution)/shard_map/ppermute | solution.py:683
  494.9 69.6 %collective-permute-start.17 = (bf16[8,24,768]{2,1,0:T(8,128)(2,1)}, bf16[8,24,768]{2,1,0:T(8,128)(2,1)}, u32[]{:S(2)}, u32[]{:S(2)}) collective-permute-start(bf16[8,24,768]{2,1,0:T(8,128)(2,1)} %get-tuple-element.226), channel_id=1, source_target_pairs={{0,2},{1,3},{2,0},{3,1},{4,6},{5,7},{6,4},{7,5},{8,10},{9,11},{10,... | collective-permute-start | bytes 884744 | tf_op jit(solution)/shard_map/ppermute | solution.py:683
  531.5 35.1 %collective-permute-start.23 = (bf16[2,4,1,24,768]{4,3,1,2,0:T(8,128)(2,1)}, bf16[2,4,1,24,768]{4,3,1,2,0:T(8,128)(2,1)}, u32[]{:S(2)}, u32[]{:S(2)}) collective-permute-start(bf16[2,4,1,24,768]{4,3,1,2,0:T(8,128)(2,1)} %get-tuple-element.241), channel_id=1, source_target_pairs={{0,16},{8,24},{16,0},{24,8},{1,17},{9,25},{17,1},{25,9},{2,18},{10... | collective-permute-start | bytes 884744 | tf_op jit(solution)/shard_map/ppermute | solution.py:683
  536.8 30.8 %collective-permute-start.22 = (bf16[1,24,2304]{2,1,0:T(8,128)(2,1)}, bf16[1,24,2304]{2,1,0:T(8,128)(2,1)S(1)}, u32[]{:S(2)}, u32[]{:S(2)}) collective-permute-start(bf16[1,24,2304]{2,1,0:T(8,128)(2,1)} %get-tuple-element.236), channel_id=1, source_target_pairs={{0,6},{1,7},{2,4},{3,5},{4,2},{5,3},{6,0},{7,1},{8,14},{9,15},{10,... | collective-permute-start | bytes 331784 | tf_op jit(solution)/shard_map/ppermute | solution.py:683
  622.2 15.0 %collective-permute-start.35 = (bf16[56,768]{1,0:T(8,128)(2,1)}, bf16[56,768]{1,0:T(8,128)(2,1)S(1)}, u32[]{:S(2)}, u32[]{:S(2)}) collective-permute-start(bf16[56,768]{1,0:T(8,128)(2,1)} %get-tuple-element.185), channel_id=1, source_target_pairs={{0,5},{1,4},{2,7},{3,6},{4,1},{5,0},{6,3},{7,2},{8,13},{9,12},{10,... | collective-permute-start | bytes 258056 | tf_op jit(solution)/shard_map/ppermute | solution.py:683
  667.7 14.4 %collective-permute-start.43 = (bf16[2,24,768]{2,1,0:T(8,128)(2,1)}, bf16[2,24,768]{2,1,0:T(8,128)(2,1)S(1)}, u32[]{:S(2)}, u32[]{:S(2)}) collective-permute-start(bf16[2,24,768]{2,1,0:T(8,128)(2,1)} %get-tuple-element.192), channel_id=1, source_target_pairs={{0,3},{1,2},{2,1},{3,0},{4,7},{5,6},{6,5},{7,4},{8,11},{9,10},{10,... | collective-permute-start | bytes 221192 | tf_op jit(solution)/shard_map/ppermute | solution.py:683
  668.8 13.8 %collective-permute-start.44 = (bf16[2,24,768]{2,1,0:T(8,128)(2,1)}, bf16[2,24,768]{2,1,0:T(8,128)(2,1)S(1)}, u32[]{:S(2)}, u32[]{:S(2)}) collective-permute-start(bf16[2,24,768]{2,1,0:T(8,128)(2,1)} %get-tuple-element.193), channel_id=1, source_target_pairs={{0,4},{1,5},{2,6},{3,7},{4,0},{5,1},{6,2},{7,3},{8,12},{9,13},{10,... | collective-permute-start | bytes 221192 | tf_op jit(solution)/shard_map/ppermute | solution.py:683
  682.1 14.2 %collective-permute-start.52 = (bf16[320,768]{1,0:T(8,128)(2,1)S(1)}, bf16[320,768]{1,0:T(8,128)(2,1)S(1)}, u32[]{:S(2)}, u32[]{:S(2)}) collective-permute-start(bf16[320,768]{1,0:T(8,128)(2,1)S(1)} %copy-done.17), channel_id=1, source_target_pairs={{0,16},{8,24},{16,0},{24,8},{1,17},{9,25},{17,1},{25,9},{2,18},{10... | collective-permute-start | bytes 1474568 | tf_op jit(solution)/shard_map/ppermute | solution.py:683
  682.6 21.5 %collective-permute-start.51 = (bf16[320,768]{1,0:T(8,128)(2,1)S(1)}, bf16[320,768]{1,0:T(8,128)(2,1)S(1)}, u32[]{:S(2)}, u32[]{:S(2)}) collective-permute-start(bf16[320,768]{1,0:T(8,128)(2,1)S(1)} %copy-done.17), channel_id=1, source_target_pairs={{0,8},{8,0},{16,24},{24,16},{1,9},{9,1},{17,25},{25,17},{2,10},{10... | collective-permute-start | bytes 1474568 | tf_op jit(solution)/shard_map/ppermute | solution.py:683
  685.4 18.6 %collective-permute-start.49 = (bf16[312,768]{1,0:T(8,128)(2,1)}, bf16[312,768]{1,0:T(8,128)(2,1)S(1)}, u32[]{:S(2)}, u32[]{:S(2)}) collective-permute-start(bf16[312,768]{1,0:T(8,128)(2,1)} %shard_map.333.refs_0_), channel_id=1, source_target_pairs={{0,16},{8,24},{16,0},{24,8},{1,17},{9,25},{17,1},{25,9},{2,18},{10... | collective-permute-start | bytes 1437704 | tf_op jit(solution)/shard_map/ppermute | solution.py:683
  687.1 23.9 %collective-permute-start.48 = (bf16[312,768]{1,0:T(8,128)(2,1)}, bf16[312,768]{1,0:T(8,128)(2,1)S(1)}, u32[]{:S(2)}, u32[]{:S(2)}) collective-permute-start(bf16[312,768]{1,0:T(8,128)(2,1)} %shard_map.333.refs_0_), channel_id=1, source_target_pairs={{0,8},{8,0},{16,24},{24,16},{1,9},{9,1},{17,25},{25,17},{2,10},{10... | collective-permute-start | bytes 1437704 | tf_op jit(solution)/shard_map/ppermute | solution.py:683
  (88 other events, 820.9 us)
Sparse Core Ops, SparseCore 0:
  59.2 97.0 all-gather.5
  159.8 53.3 all-gather.3
  320.2 82.3 reduce-scatter.1
  481.4 39.7 all-reduce.6

commit v3 on v2

--- a/solution.py
+++ b/solution.py
@@ -58,6 +58,14 @@
     return pl.BlockSpec(shape, index)
 
 
+def beside(kernel, inputs, count):
+    return lambda *refs: kernel(*refs[:inputs], *refs[inputs + count :])
+
+
+def anywhere(arrays):
+    return [pl.BlockSpec(memory_space=pl.ANY)] * len(arrays)
+
+
 def held(shape):
     return pl.BlockSpec(shape, lambda *_: (0,) * len(shape), pipeline_mode=pl.Buffered(1))
 
@@ -137,7 +145,7 @@
 ROWS_Q = 384
 
 
-def attend_kernel(lengths_ref, q_ref, k_ref, v_ref, mixed_ref, rest_ref, stat_ref):
+def attend_kernel(lengths_ref, q_ref, k_ref, v_ref, mixed_ref, stat_ref):
     pack, pair = pl.program_id(0), pl.program_id(1)
     lane = lax.broadcasted_iota(jnp.int32, (1, 2 * HEAD), 1)
 
@@ -169,10 +177,7 @@
                 peaks.append(peak)
             both = dot(jnp.concatenate(expos, axis=1), ext)
             total = both[:, 2 * HEAD :]
-            mixed = both[:, : 2 * HEAD] / total
-            rounded = mixed.astype(narrow)
-            mixed_ref[0, at : at + tile] = rounded
-            rest_ref[0, at : at + tile] = (mixed - rounded.astype(wide)).astype(narrow)
+            mixed_ref[0, at : at + tile] = (both[:, : 2 * HEAD] / total).astype(narrow)
             lse = (jnp.where(lane < HEAD, peaks[0], peaks[1]) + jnp.log(total)) * log2e
             for h in range(2):
                 column = jnp.sum(jnp.where(lane == h * HEAD, lse, 0.0), axis=1, keepdims=True)
@@ -194,10 +199,9 @@
             num_scalar_prefetch=1,
             grid=(mb, pairs),
             in_specs=[block] * 3,
-            out_specs=[block, block, pl.BlockSpec((1, ROWS, 128), lambda m, p, *_: (m, 0, 0))],
+            out_specs=[block, pl.BlockSpec((1, ROWS, 128), lambda m, p, *_: (m, 0, 0))],
         ),
         out_shape=[
-            jax.ShapeDtypeStruct((mb, ROWS, width), narrow),
             jax.ShapeDtypeStruct((mb, ROWS, width), narrow),
             jax.ShapeDtypeStruct((mb, ROWS, 128), wide),
         ],
@@ -310,7 +314,7 @@
 
 
 def backward_kernel(
-    lengths_ref, dpool_ref, unit3_ref, unit2_ref, stat_ref, slope_ref, mixed_ref, rest_ref, w_ref, gain_ref, pick_ref,
+    lengths_ref, dpool_ref, unit3_ref, unit2_ref, stat_ref, slope_ref, mixed_ref, w_ref, gain_ref, pick_ref,
     dm_ref, dup_ref, dr_ref, dmixed_ref, delta_ref, dgain_ref,
 ):
     pack, step = pl.program_id(0), pl.program_id(1)
@@ -341,10 +345,7 @@
     dr_ref[0] = dr
     dmixed = dot(dr, w_ref[0], 1, 1).astype(narrow)
     dmixed_ref[0] = dmixed
-    product = dmixed.astype(wide) * (mixed_ref[0].astype(wide) + rest_ref[0].astype(wide))
-    high = product.astype(narrow)
-    low = (product - high.astype(wide)).astype(narrow)
-    delta_ref[0] = dot(high, pick_ref[...]) + dot(low, pick_ref[...])
+    delta_ref[0] = dot(dmixed * mixed_ref[0], pick_ref[...])
 
     @pl.when((pack == 0) & (step == 0))
     def _():
@@ -354,7 +355,7 @@
     dgain_ref[4:5] += dgf
 
 
-def backward_call(lengths, dpool, unit3, unit2, stat, slope, mixed, rest, w, gains, pick):
+def backward_call(lengths, dpool, unit3, unit2, stat, slope, mixed, w, gains, pick):
     mb, _, width = unit3.shape
     rows = pl.BlockSpec((1, TILE, width), lambda m, i, *_: (m, i, 0))
     lanes = pl.BlockSpec((1, TILE, 128), lambda m, i, *_: (m, i, 0))
@@ -365,8 +366,8 @@
             num_scalar_prefetch=1,
             grid=(mb, ROWS // TILE),
             in_specs=[
-                pl.BlockSpec((1, 2, width), lambda m, i, *_: (m, 0, 0)),
-                rows, rows, lanes, wider, rows, rows,
+                pl.BlockSpec((1, 8, width), lambda m, i, *_: (m, 0, 0)),
+                rows, rows, lanes, wider, rows,
                 held(w.shape), held(gains.shape), held(pick.shape),
             ],
             out_specs=[rows, wider, rows, rows, lanes, pl.BlockSpec((8, width), lambda m, i, *_: (0, 0))],
@@ -381,7 +382,7 @@
         ],
         compiler_params=params(),
         cost_estimate=cost(2 * mb * ROWS * width * width * 9, 70e6),
-    )(lengths, dpool, unit3, unit2, stat, slope, mixed, rest, w, gains, pick)
+    )(lengths, dpool, unit3, unit2, stat, slope, mixed, w, gains, pick)
 
 
 def attend_back_kernel(
@@ -452,13 +453,13 @@
         ref[0] = (r * (scaled - mean(scaled) - unit * mean(scaled * unit))).astype(narrow)
 
 
-def attend_back_call(lengths, q, k, v, do, kept, stat, gains, ones, first_pair, pairs):
+def attend_back_call(lengths, q, k, v, do, kept, stat, gains, ones, first_pair, pairs, first=()):
     mb, _, width = q.shape
     block = pl.BlockSpec((1, ROWS, 2 * HEAD), lambda p, m, *_: (m, 0, p + first_pair))
     out = pl.BlockSpec((1, ROWS, 2 * HEAD), lambda p, m, *_: (m, 0, p))
     shape = jax.ShapeDtypeStruct((mb, ROWS, pairs * 2 * HEAD), narrow)
     return pl.pallas_call(
-        attend_back_kernel,
+        beside(attend_back_kernel, 12, len(first)),
         grid_spec=pltpu.PrefetchScalarGridSpec(
             num_scalar_prefetch=1,
             grid=(pairs, mb),
@@ -467,6 +468,7 @@
                 pl.BlockSpec((1, 8, ROWS), lambda p, m, *_: (m, p + first_pair, 0)),
                 pl.BlockSpec((8, 2 * HEAD), lambda p, m, *_: (0, p + first_pair)),
                 pl.BlockSpec((2 * HEAD, 2 * HEAD), lambda p, m, *_: (0, 0)),
+                *anywhere(first),
             ],
             out_specs=[out, out, out, pl.BlockSpec((1, 8, 2 * HEAD), lambda p, m, *_: (p, 0, 0))],
             scratch_shapes=[pltpu.VMEM((ROWS, 2 * HEAD), wide)] * 3,
@@ -474,7 +476,7 @@
         out_shape=[shape, shape, shape, jax.ShapeDtypeStruct((pairs, 8, 2 * HEAD), wide)],
         compiler_params=params(),
         cost_estimate=cost(20 * mb * 2 * pairs * (LONG**2 + SHORT**2) * HEAD * 2, mb * ROWS * pairs * 128 * 18),
-    )(lengths, q, k, v, do, *kept, stat, gains, ones)
+    )(lengths, q, k, v, do, *kept, stat, gains, ones, *first)
 
 
 def first_kernel(*refs, parts):
@@ -497,15 +499,16 @@
     out_ref[0] = (dr_ref[0].astype(wide) + back_rows(unit, r, total * gain_ref[0:1])).astype(narrow)
 
 
-def first_call(grads, embed, dr, w, gains):
+def first_call(grads, embed, dr, w, gains, first=()):
     mb, _, width = embed.shape
     rows = spec((1, TILE, width), lambda m, i: (m, i, 0))
     parts = len(grads) // 3
     return pl.pallas_call(
-        functools.partial(first_kernel, parts=parts),
+        beside(functools.partial(first_kernel, parts=parts), len(grads) + 4, len(first)),
         grid=(mb, ROWS // TILE),
         in_specs=[spec((1, TILE, g.shape[2]), lambda m, i: (m, i, 0)) for g in grads]
-        + [rows, rows, held(w.shape), held(gains.shape)],
+        + [rows, rows, held(w.shape), held(gains.shape)]
+        + anywhere(first),
         out_specs=[rows, spec((8, width), lambda m, i: (0, 0))],
         out_shape=[
             jax.ShapeDtypeStruct((mb, ROWS, width), narrow),
@@ -513,7 +516,7 @@
         ],
         compiler_params=params(),
         cost_estimate=cost(2 * mb * ROWS * width * width * 3, 32e6),
-    )(*grads, embed, dr, w, gains)
+    )(*grads, embed, dr, w, gains, *first)
 
 
 def split_rows(value, own_ref, sent_ref, me, n):
@@ -533,11 +536,14 @@
     return ref[...].reshape(-1, ref.shape[-1])
 
 
-def weight_kernel(at_ref, act_ref, dm_ref, second_ref, dup_ref, own_ref, sent_ref):
+def weight_kernel(act_ref, dm_ref, second_ref, dup_ref, out_ref):
     step = pl.program_id(0)
 
     def write(a_ref, b_ref):
-        split_rows(dot(flat_rows(a_ref), flat_rows(b_ref), 0, 0), own_ref, sent_ref, at_ref[0], 0)
+        value = dot(flat_rows(a_ref), flat_rows(b_ref), 0, 0)
+        part = out_ref.shape[2]
+        for to in range(out_ref.shape[0]):
+            out_ref[to, 0] = value[to * part : (to + 1) * part].astype(narrow)
 
     pl.when(step < 4)(lambda: write(second_ref, dup_ref))
     pl.when(step >= 4)(lambda: write(act_ref, dm_ref))
@@ -554,72 +560,78 @@
 
 def weight_call(act, dm, second, dup):
     width = dm.shape[2]
-    (x, y, z), part = split_shape(width)
-    rows = pl.BlockSpec(dm.shape, lambda i, *_: (0, 0, 0), pipeline_mode=pl.Buffered(1))
-    out = pl.BlockSpec((x, y, z, 1, part, width), lambda i, *_: (0, 0, 0, i, 0, 0))
+    parts = lax.axis_size("fsdp") * lax.axis_size("seq")
+    rows = held(dm.shape)
     one = (1, *dm.shape)
     return pl.pallas_call(
         weight_kernel,
-        grid_spec=pltpu.PrefetchScalarGridSpec(
-            num_scalar_prefetch=1,
-            grid=(8,),
-            in_specs=[
-                pl.BlockSpec(one, lambda i, *_: (jnp.maximum(i - 4, 0), 0, 0, 0)),
-                rows,
-                rows,
-                pl.BlockSpec(one, lambda i, *_: (jnp.minimum(i, 3), 0, 0, 0)),
-            ],
-            out_specs=[out, out],
-        ),
-        out_shape=[jax.ShapeDtypeStruct((x, y, z, 8, part, width), narrow)] * 2,
+        grid=(8,),
+        in_specs=[
+            spec(one, lambda i: (jnp.maximum(i - 4, 0), 0, 0, 0)),
+            rows,
+            rows,
+            spec(one, lambda i: (jnp.minimum(i, 3), 0, 0, 0)),
+        ],
+        out_specs=spec((parts, 1, width // parts, width), lambda i: (0, i, 0, 0)),
+        out_shape=jax.ShapeDtypeStruct((parts, 8, width // parts, width), narrow),
         compiler_params=params(),
         cost_estimate=cost(2 * 8 * dm.size * width, 60e6),
-    )(core_at(), act, dm, second, dup)
-
-
-def one_weight_kernel(at_ref, a_ref, *refs, count):
-    b_refs, own_ref, sent_ref, total = refs[:count], refs[count], refs[count + 1], refs[count + 2]
+    )(act, dm, second, dup)
+
+
+def one_weight_kernel(at_ref, *refs, groups):
+    count = len(groups) + sum(groups)
+    own_ref, sent_ref, total = refs[count:]
     step = pl.program_id(0)
     last = step == pl.num_programs(0) - 1
-    a = a_ref[0]
-    at = 0
-    for b_ref in b_refs:
-        lanes = pl.ds(at, b_ref.shape[-1])
-        at += b_ref.shape[-1]
-        value = dot(a, b_ref[0], 0, 0)
-
-        @pl.when(step == 0)
-        def _(value=value, lanes=lanes):
-            total[:, lanes] = value
-
-        @pl.when((step > 0) & ~last)
-        def _(value=value, lanes=lanes):
-            total[:, lanes] += value
-
-        @pl.when(last)
-        def _(value=value, lanes=lanes):
-            split_rows(total[:, lanes] + value, own_ref.at[..., lanes], sent_ref.at[..., lanes], at_ref[0], 0)
-
-
-def one_weight_call(a, *b):
-    mb, rows, depth = a.shape
-    width = sum(x.shape[-1] for x in b)
+    at, ref = 0, 0
+    for members in groups:
+        a = refs[ref][0]
+        for b_ref in refs[ref + 1 : ref + 1 + members]:
+            lanes = pl.ds(at, b_ref.shape[-1])
+            at += b_ref.shape[-1]
+            value = dot(a, b_ref[0], 0, 0)
+
+            @pl.when(step == 0)
+            def _(value=value, lanes=lanes):
+                total[:, lanes] = value
+
+            @pl.when((step > 0) & ~last)
+            def _(value=value, lanes=lanes):
+                total[:, lanes] += value
+
+            @pl.when(last)
+            def _(value=value, lanes=lanes):
+                split_rows(total[:, lanes] + value, own_ref.at[..., lanes], sent_ref.at[..., lanes], at_ref[0], 0)
+
+        ref += 1 + members
+
+
+def one_weight_call(*groups, first=()):
+    arrays = [array for group in groups for array in group]
+    mb, rows, depth = arrays[0].shape
+    width = sum(x.shape[-1] for group in groups for x in group[1:])
     (x, y, z), part = split_shape(depth)
     shape = (x, y, z, 1, part, width)
     out = pl.BlockSpec(shape, lambda m, *_: (0,) * 6)
     return pl.pallas_call(
-        functools.partial(one_weight_kernel, count=len(b)),
+        beside(
+            functools.partial(one_weight_kernel, groups=[len(group) - 1 for group in groups]),
+            1 + len(arrays),
+            len(first),
+        ),
         grid_spec=pltpu.PrefetchScalarGridSpec(
             num_scalar_prefetch=1,
             grid=(mb,),
-            in_specs=[pl.BlockSpec((1, *v.shape[1:]), lambda m, *_: (m, 0, 0)) for v in (a, *b)],
+            in_specs=[pl.BlockSpec((1, *v.shape[1:]), lambda m, *_: (m, 0, 0)) for v in arrays]
+            + anywhere(first),
             out_specs=[out] * 2,
             scratch_shapes=[pltpu.VMEM((depth, width), wide)],
         ),
         out_shape=[jax.ShapeDtypeStruct(shape, narrow)] * 2,
         compiler_params=params(),
-        cost_estimate=cost(2 * a.size * width, 12e6),
-    )(core_at(), a, *b)
+        cost_estimate=cost(2 * mb * rows * depth * width, 12e6),
+    )(core_at(), *arrays, *first)
 
 
 def embed_weight_kernel(at_ref, patch_ref, hot_ref, grad_ref, gain_ref, own_ref, sent_ref, total):
@@ -645,14 +657,14 @@
         split_rows(total[...], own_ref, sent_ref, at_ref[0], 0)
 
 
-def embed_weight_call(patches, hot, grad, gain_columns):
+def embed_weight_call(patches, hot, grad, gain_columns, first=()):
     mb, _, width = grad.shape
     pixels = patches.shape[3]
     (x, y, z), part = split_shape(pixels)
     shape = (x, y, z, 1, part, width + 256)
     out = pl.BlockSpec(shape, lambda m, *_: (0,) * 6)
     return pl.pallas_call(
-        embed_weight_kernel,
+        beside(embed_weight_kernel, 5, len(first)),
         grid_spec=pltpu.PrefetchScalarGridSpec(
             num_scalar_prefetch=1,
             grid=(mb,),
@@ -661,6 +673,7 @@
                 pl.BlockSpec((1, ROWS, hot.shape[2]), lambda m, *_: (m, 0, 0)),
                 pl.BlockSpec((1, ROWS, width), lambda m, *_: (m, 0, 0)),
                 pl.BlockSpec((width, 128), lambda m, *_: (0, 0)),
+                *anywhere(first),
             ],
             out_specs=[out, out],
             scratch_shapes=[pltpu.VMEM((pixels, width + 256), wide)],
@@ -668,7 +681,7 @@
         out_shape=[jax.ShapeDtypeStruct(shape, narrow)] * 2,
         compiler_params=params(),
         cost_estimate=cost(2 * grad.size * (pixels + 128), 12e6),
-    )(core_at(), patches, hot, grad, gain_columns)
+    )(core_at(), patches, hot, grad, gain_columns, *first)
 
 
 def fold(parts):
@@ -807,7 +820,7 @@
         first = mid_ref[:, width + i * columns : width + (i + 1) * columns]
         pieces.append(jnp.concatenate([first, late[:, i * remain : (i + 1) * remain]], axis=1))
     pieces.append(mid_ref[:, :width])
-    pieces += [rest_ref[i] for i in range(rest_ref.shape[0])]
+    pieces += [rest_ref[i].astype(wide) for i in range(rest_ref.shape[0])]
     squares = jnp.zeros((1, 1), wide)
     total = jnp.zeros((part, width), wide)
     for b, piece in enumerate(pieces):
@@ -990,47 +1003,47 @@
     opening = my_rows(jnp.concatenate([blocks[0].astype(narrow), small], axis=1)[None])[0]
     project = my_rows(blocks[1:4]).astype(narrow).transpose(1, 0, 2).reshape(part, 3 * width)
     every = far_exchange(near_exchange(jnp.concatenate([opening, project], axis=1)))
+    places = positions[:, :, 0, :ROWS]
+    grid = jnp.arange(grid_rows)
+    hot = jnp.concatenate([places[i][:, :, None] == grid for i in range(2)], axis=2).astype(narrow)
+    index = jnp.arange(256)
+    ones = jnp.where(index[:, None] // HEAD == index[None] // HEAD, 1 / HEAD, 0).astype(narrow)
+    pick = (jnp.arange(width)[:, None] // HEAD == jnp.arange(128)[None]).astype(narrow)
+
+    def column(x):
+        x = jnp.pad(x, ((0, 0), (0, 6))).reshape(8 * mb, 1)
+        return jnp.broadcast_to(x, (8 * mb, 128))
+
+    seq_columns = [column(1.0 / lengths.astype(wide)), column(res_weights), column(labels)]
+    rest_part = my_rows(blocks[4:13]).astype(narrow)
+    head_part = my_rows(head[None])[0].astype(narrow)
+    ahead = (hot, ones, pick, rest_part, head_part, *seq_columns)
+    every = [every[0], tied(every[1], *ahead), *every[2:]]
     opening = seq_parts(stacked([x[:, :, : width + 256] for x in every]))
     project = stacked([x[:, :, width + 256 :] for x in every])
     w_embed = settle_rows(opening, [(0, part, 0, ())], [(deep, size, part, width + 256)])[0]
     w_embed = w_embed.reshape(width, width + 256)
     gains_full = w_embed[:, width + 128 :].T[:8].astype(wide)
     weight_sum = jnp.sum(gains_full[5].reshape(deep * size, part)[:, 0])
-    w_rest = lax.all_gather(my_rows(tied(blocks[4:13], opening[-1])).astype(narrow), ("fsdp", "seq"), axis=1, tiled=True)
-    w_head = lax.all_gather(tied(my_rows(head.astype(narrow)[None])[0], opening[-1]), ("fsdp", "seq"), axis=0, tiled=True)
-
-    places = positions[:, :, 0, :ROWS]
-    grid = jnp.arange(grid_rows)
-    hot = jnp.concatenate([places[i][:, :, None] == grid for i in range(2)], axis=2).astype(narrow)
-    index = jnp.arange(256)
-    ones = jnp.where(index[:, None] // HEAD == index[None] // HEAD, 1 / HEAD, 0).astype(narrow)
-    pick = (jnp.arange(width)[:, None] // HEAD == jnp.arange(128)[None]).astype(narrow)
+    w_rest = lax.all_gather(tied(rest_part, opening[-1]), ("fsdp", "seq"), axis=1, tiled=True)
+    w_head = lax.all_gather(tied(head_part, opening[-1]), ("fsdp", "seq"), axis=0, tiled=True)
+
     embed, first = embed_call(patches, hot, tied(w_embed, project), gains_full)
     w_project = settle_rows(
         seq_parts(tied(project, opening[-1]), first), [(0, part, 0, ())], [(deep, size, part, 3 * width)]
     )[0].reshape(width, 3 * width)
     query, keys, values, *kept = project_call(first, w_project, gains_full, ones)
-    mixed, rest, stat = attend_call(lengths, query, keys, values)
+    mixed, stat = attend_call(lengths, query, keys, values)
     second, act, slope, unit2, unit3, row_stat, pool = forward_call(lengths, embed, mixed, w_rest, gains_full)
 
-    seqs = 2 * mb
-    spare = -seqs % 8
-
-    def column(x):
-        return jnp.broadcast_to(jnp.pad(x.reshape(seqs), (0, spare))[:, None], (seqs + spare, 128))
-
-    pool = jnp.pad(pool[:, :2].reshape(seqs, width), ((0, spare), (0, 0)))
-    loss, d_head, d_pool = head_call(
-        pool, column(1.0 / lengths.astype(wide)), column(res_weights), column(labels), w_head
-    )
-    head_sum = lax.psum_scatter(d_head, "fsdp", scatter_dimension=0, tiled=True)
+    loss, d_head, d_pool = head_call(pool.reshape(8 * mb, width), *seq_columns, w_head)
+    head_sum = lax.psum_scatter(d_head, ("fsdp", "seq"), scatter_dimension=0, tiled=True)
 
     dm, d_up, dr, d_mixed, delta, d_gain_rest = backward_call(
-        lengths, d_pool[:seqs].reshape(mb, 2, width), unit3, unit2, row_stat, slope, mixed, rest, w_rest, gains_full, pick
-    )
-    rest_core = core_terms(*weight_call(act, dm, second, d_up))
-    out_own, out_sent = one_weight_call(tied(mixed, rest_core[0]), dr)
-    rest_x = Sum([tied(rest_core[0], out_own), rest_core[1]], X)
+        lengths, d_pool.reshape(mb, 8, width), unit3, unit2, row_stat, slope, mixed, w_rest, gains_full, pick
+    )
+    d_rest = weight_call(act, dm, second, d_up)
+    own_rest = lax.psum_scatter(d_rest, ("fsdp", "seq"), scatter_dimension=0, tiled=True)[0]
 
     pairs = HEADS // 2
     early = 4
@@ -1040,42 +1053,32 @@
 
     def heads_back(after, start, count):
         out = attend_back_call(
-            lengths, tied(query, *after), keys, values, d_mixed, kept, stats, gains_full,
-            ones, start, count,
+            lengths, query, keys, values, d_mixed, kept, stats, gains_full, ones, start, count, after,
         )
         return out[:3], out[3]
 
-    grads_one, gain_one = heads_back(rest_x.sent, 0, early)
-    rest_y = Sum(rest_x.after(grads_one[0]), Y)
-    head_sum = lax.psum(tied(head_sum, *rest_y.sent), "seq")
-    one_own, one_sent = one_weight_call(tied(first, *rest_y.sent), *grads_one)
-    mid_core = core_terms(
-        jnp.concatenate([out_own, one_own], axis=5), jnp.concatenate([out_sent, one_sent], axis=5)
-    )
+    grads_one, gain_one = heads_back([d_rest], 0, early)
+    mid_core = core_terms(*one_weight_call((mixed, dr), (first, *grads_one), first=[head_sum]))
     mid_x = Sum(mid_core, X)
-    grads_two, gain_two = heads_back(rest_y.sent + mid_x.sent, early, pairs - early)
-    rest_z = Sum(rest_y.after(grads_two[0]), Z)
+    grads_two, gain_two = heads_back(mid_x.sent, early, pairs - early)
     mid_y = Sum(mid_x.after(grads_two[0]), Y)
-    late_core = core_terms(*one_weight_call(tied(first, *rest_z.sent, *mid_y.sent), *grads_two))
+    late_core = core_terms(*one_weight_call((first, *grads_two), first=mid_y.sent))
     late_x = Sum(late_core, X)
     mid_z = Sum(mid_y.after(late_core[0]), Z)
     d_embed, d_gain_first = first_call(
-        (*grads_one, *grads_two), embed, tied(dr, *late_x.sent, *mid_z.sent), w_project, gains_full
+        (*grads_one, *grads_two), embed, dr, w_project, gains_full, [own_rest, *late_x.sent, *mid_z.sent]
     )
     late_y = Sum(late_x.after(d_embed), Y)
-    own_rest, own_mid = fold([x.astype(wide) for x in rest_z.after(d_embed)]), fold(
-        [x.astype(wide) for x in mid_z.after(d_embed)]
-    )
+    own_mid = fold([x.astype(wide) for x in mid_z.after(d_embed)])
     d_gain_heads = jnp.concatenate([gain_one, gain_two], axis=0).transpose(1, 0, 2).reshape(8, width)
     d_gains = jnp.concatenate(
         [d_gain_first[:1], d_gain_heads[:2], d_gain_rest[3:5], jnp.zeros((123, width), wide)], axis=0
     ).T
-    head_sum = tied(head_sum, late_core[0]) / weight_sum
-    head_squares = jnp.where(me_s == 0, jnp.sum(jnp.square(head_sum)), 0.0)
-    scalars = jnp.stack([weight_sum, head_squares, loss[0, 0]])
-    left_part = pick_index(left_roots.reshape(left_roots.shape[0], deep, size, part, width), me_s, 2)
-    e_own, e_sent = embed_weight_call(
-        patches, hot, tied(d_embed, own_rest, own_mid, scalars, left_part, *late_y.sent), d_gains
+    e_own, e_sent = embed_weight_call(patches, hot, d_embed, d_gains, [own_mid, *late_y.sent])
+    head_sum = tied(head_sum, e_own) / weight_sum
+    scalars = jnp.stack([weight_sum, jnp.sum(jnp.square(head_sum)), loss[0, 0]])
+    left_part = pick_index(
+        tied(left_roots, e_own).reshape(left_roots.shape[0], deep, size, part, width), me_s, 2
     )
     last_y = Sum(Sum(core_terms(e_own, e_sent), X).terms, Y)
     both_z = Sum(
@@ -1103,6 +1106,11 @@
     blocks_new = blocks_new.reshape(blocks.shape)
     block_grads = block_grads.reshape(blocks.shape)
     slotted = tied(slotted, back)
+    head_all = settled(
+        seq_parts(tied(head_sum, back)),
+        [(size, *head_sum.shape)],
+        [(j, (), 0, lambda f, s, j=j: j ^ s) for j in range(size)],
+    )[0].reshape(head.shape)
     gram_left = product("sij,skj->sik", slotted, slotted)
     gram_right = product("sji,sjk->sik", slotted, slotted)
     left_new = stat_decay * left_stats + ((1 - stat_decay) * factor * factor) * gram_left
@@ -1117,7 +1125,7 @@
     )
     gains_new, gain_first_new, gain_second_new = adam(gains, gain_grad, gain_first, gain_second, gain_rate, 0.0)
     head_new, head_first_new, head_second_new = adam(
-        head, tied(head_sum, back) * factor, head_first, head_second, adam_rate, decay_rate
+        head, head_all * factor, head_first, head_second, adam_rate, decay_rate
     )
     return (
         blocks_new, block_grads, left_new, right_new, pos_new, pos_first_new, pos_second_new,

time: 732 us -> 671 us (0.917)
  waiting for transfers between devices: 106 us -> 77.9 us
  other arithmetic: 51.2 us -> 30.1 us
    psum x1 -> x0, waiting for transfers between devices: 14.9 us -> none  [local(): head_sum = lax.psum(tied(head_sum, *rest_y.sent), 'seq')]
    ppermute x54 -> x51, waiting for transfers between devices: 91.2 us -> 77.5 us  [swap(): lax.ppermute(x, axis, [(i, i ^ bits) for i in range(lax.axis_size(axis))])]
    convert_element_type x7 -> x5, other arithmetic: 17.1 us -> 7.28 us  [__init__(): self.sent = [part(k).astype(narrow) for k in range(1, size)]]
    add x6 -> x4, other arithmetic: 11.5 us -> 2.46 us  [fold(): parts = [parts[i] + parts[i + 1] for i in range(0, len(parts), 2)]]
    ppermute x54 -> x51, starting transfers between devices: 68.6 us -> 61.4 us  [swap(): lax.ppermute(x, axis, [(i, i ^ bits) for i in range(lax.axis_size(axis))])]
    pallas_call x8 -> x7, Pallas kernels: 206 us -> 205 us  [the longest x2 108 us: attend_back_call(): pl.pallas_call(beside(attend_back_kernel, 12, len(first)), grid_spec=pltp...]
  transfers between devices with their start and end apart: 58 -> 55, of which waited for: 20 -> 18; matrix products, arithmetic and copies ran while one was open for 11% -> 9% of each run, Pallas kernels for 43% -> 60%
where the time goes in v3:
time: 671 us; the launch traced here: 666 us
  Pallas kernels  430 us (64%)
  waiting for transfers between devices  77.9 us (12%)
  starting transfers between devices  61.7 us (9%)
  local copies, waits for them, and re-layouts  32.9 us (5%)
  other arithmetic  30.1 us (4%)
  between operations  21.7 us (3%)
  matrix products  12.3 us (2%)
    pallas_call x2, Pallas kernels, attend_back_call(): pl.pallas_call(beside(attend_back_kernel, 12, len(first)), grid_spec=pltp...  108 us
    ppermute x51, waiting for transfers between devices, swap(): lax.ppermute(x, axis, [(i, i ^ bits) for i in range(lax.axis_size(axis))])  77.5 us
    ppermute x51, starting transfers between devices, swap(): lax.ppermute(x, axis, [(i, i ^ bits) for i in range(lax.axis_size(axis))])  61.4 us
    pallas_call x1, Pallas kernels, attend_call(): pl.pallas_call(attend_kernel, grid_spec=pltpu.PrefetchScalarGridSpec(num_...  52.4 us
    pallas_call x1, Pallas kernels, backward_call(): pl.pallas_call(backward_kernel, grid_spec=pltpu.PrefetchScalarGridSpec(nu...  52.3 us
    pallas_call x1, Pallas kernels, forward_call(): pl.pallas_call(forward_kernel, grid_spec=pltpu.PrefetchScalarGridSpec(num...  50.8 us
    pallas_call x1, Pallas kernels, weight_call(): pl.pallas_call(weight_kernel, grid=(8,), in_specs=[spec(one, lambda i: (j...  35.9 us
    pallas_call x2, Pallas kernels, one_weight_call(): pl.pallas_call(beside(functools.partial(one_weight_kernel, groups=[len(gr...  30.8 us
  transfers between devices with their start and end apart: 55, of which 18 were waited for; matrix products, arithmetic and copies ran while one was open for 9% of the time, Pallas kernels for 60%

profile of v3, /device:TPU:0, one launch (start us, length us, event | category | flops | bytes accessed | tf_op | source)
XLA Modules:
  0.0 666.5 jit_solution(14056337667916916204)
XLA Ops:
  31.2 9.4 %collective-permute-done.1 = bf16[2,24,3328]{2,1,0:T(8,128)(2,1)S(1)} collective-permute-done((bf16[2,24,3328]{2,1,0:T(8,128)(2,1)S(1)}, bf16[2,24,3328]{2,1,0:T(8,128)(2,1)S(1)}, u32[]{:S(2)}, u32[]{:S(2)}) %collective-permute-start.1) | collective-permute-done | bytes 319520 | tf_op jit(solution)/shard_map/ppermute | solution.py:696
  42.6 10.9 %collective-permute-done.2 = bf16[2,24,3328]{2,1,0:T(8,128)(2,1)S(1)} collective-permute-done((bf16[2,24,3328]{2,1,0:T(8,128)(2,1)S(1)}, bf16[2,24,3328]{2,1,0:T(8,128)(2,1)S(1)}, u32[]{:S(2)}, u32[]{:S(2)}) %collective-permute-start.2) | collective-permute-done | bytes 319520 | tf_op jit(solution)/shard_map/ppermute | solution.py:696
  55.8 6.3 collective-permute-done.5.refs_2_
  73.6 11.8 %shard_map.316 = (f32[2,1408,768]{2,1,0:T(8,128)}, bf16[2,1408,768]{2,1,0:T(8,128)(2,1)}) custom-call(bf16[2,1,1536,768]{3,2,1,0:T(8,128)(2,1)} %refs_1_.1, bf16[2,1408,128]{2,1,0:T(8,128)(2,1)} %add_convert_fusion.1.hot_ref.refs_2_, bf16[768,1024]{1,0:T(8,128)(2,1)} %bitcast.208, f32[8,768]{1,0:T(8,128)} %slice_convert_fusion.1.gain_ref.refs_10_.refs_9_), custom_call_target="tpu_custom_call" | custom-call | flops 3875536896 | bytes 20000000 | tf_op jit(solution)/shard_map/pallas_call | solution.py:88
  85.4 5.1 collective-permute-done.8.refs_2_
  97.1 22.7 %shard_map.318 = (bf16[2,1408,768]{2,1,0:T(8,128)(2,1)}, bf16[2,1408,768]{2,1,0:T(8,128)(2,1)}, bf16[2,1408,768]{2,1,0:T(8,128)(2,1)}, bf16[2,1408,768]{2,1,0:T(...) custom-call(bf16[2,1408,768]{2,1,0:T(8,128)(2,1)} %get-tuple-element.97.fir, ...), custom_call_target="tpu_custom_call" | custom-call | flops 9965666304 | bytes 30000000 | tf_op jit(solution)/shard_map/pallas_call | solution.py:134
  119.8 52.4 %shard_map.319 = (bf16[2,1408,768]{2,1,0:T(8,128)(2,1)}, f32[2,1408,128]{2,1,0:T(8,128)}) custom-call(s32[2,2]{1,0:T(2,128)} %bitcast.247, bf16[2,1408,768]{2,1,0:T(8,128)(2,1)} %get-tuple-element.100.q_ref.refs_1_, bf16[2,1408,768]{2,1,0:T(8,128)(2,1)} %get-tuple-element.101.k_ref.refs_2_, bf16[2,1408,768]{2,1,0:T(8,128)(2,1)} %get-tuple-element.102.v_ref.refs_3_), custom_call_target="tpu_custom_call" | custom-call | flops 34225520640 | bytes 17301504 | tf_op jit(solution)/shard_map/pallas_call | solution.py:196
  174.0 50.8 %shard_map.320 = (bf16[2,1408,768]{2,1,0:T(8,128)(2,1)}, bf16[4,2,1408,768]{3,2,1,0:T(8,128)(2,1)}, bf16[4,2,1408,768]{3,2,1,0:T(8,128)(2,1)}, bf16[2,1408,768]{...) custom-call(s32[2,2]{1,0:T(2,128)} %bitcast.248, ...), custom_call_target="tpu_custom_call" | custom-call | flops 29896998912 | bytes 80000000 | tf_op jit(solution)/shard_map/pallas_call | solution.py:260
  224.9 4.4 shard_map.321
  229.3 52.3 %shard_map.322 = (bf16[2,1408,768]{2,1,0:T(8,128)(2,1)}, bf16[4,2,1408,768]{3,2,1,0:T(8,128)(2,1)}, bf16[2,1408,768]{2,1,0:T(8,128)(2,1)}, bf16[2,1408,768]{2,1,...) custom-call(s32[2,2]{1,0:T(2,128)} %bitcast.249, f32[2,8,768]{2,1,0:T(8,128)} %bitcast.256, ...), custom_call_target="tpu_custom_call" | custom-call | flops 29896998912 | bytes 70000000 | tf_op jit(solution)/shard_map/pallas_call | solution.py:363
  284.6 35.9 %shard_map.323.refs_12_ = bf16[32,8,24,768]{3,2,1,0:T(8,128)(2,1)} custom-call(bf16[4,2,1408,768]{3,2,1,0:T(8,128)(2,1)} %get-tuple-element.120.act_ref, bf16[2,1408,768]{2,1,0:T(8,128)(2,1)} %get-tuple-element.121.dm_ref, bf16[2,1408,768]{2,1,0:T(8,128)(2,1)} %get-tuple-element.122.second_ref, bf16[4,2,1408,768]{3,2,1,0:T(8,128)(2,1)} %get-tuple-element.123.dup_ref), custom_call_target="tpu_custom_call" | custom-call | flops 26575110144 | bytes 60000000 | tf_op jit(solution)/shard_map/pallas_call | solution.py:566
  320.5 70.4 %shard_map.324 = (bf16[2,1408,512]{2,1,0:T(8,128)(2,1)}, bf16[2,1408,512]{2,1,0:T(8,128)(2,1)}, bf16[2,1408,512]{2,1,0:T(8,128)(2,1)}, f32[4,8,128]{2,1,0:T(8,128)}) custom-call(s32[2,2]{1,0:T(2,128)} %bitcast.250, bf16[2,1408,768]{2,1,0:T(8,128)(2,1)} %get-tuple-element.100.q_ref.refs_1_, bf16[2,1408,768]{2,1,0:T(8,128)(2,1)} %get-tuple-element.101.k_ref.refs_2_, ...), custom_call_target="tpu_custom_call" | custom-call | flops 57042534400 | bytes 25952256 | tf_op jit(solution)/shard_map/pallas_call | solution.py:461
  390.9 20.1 %shard_map.325 = (bf16[2,2,4,1,24,2304]{5,4,3,2,1,0:T(8,128)(2,1)}, bf16[2,2,4,1,24,2304]{5,4,3,2,1,0:T(8,128)(2,1)}) custom-call(s32[1]{0:T(128)} %bitcast.2.refs_0_, bf16[2,1408,768]{2,1,0:T(8,128)(2,1)} %get-tuple-element.104.mixed_ref.refs_1_, bf16[2,1408,768]{2,1,0:T(8,128)(2,1)} %get-tuple-element.127.refs_2_.refs_7_, ...), custom_call_target="tpu_custom_call" | custom-call | flops 9965666304 | bytes 12000000 | tf_op jit(solution)/shard_map/pallas_call | solution.py:617
  419.7 37.1 %shard_map.326 = (bf16[2,1408,256]{2,1,0:T(8,128)(2,1)}, bf16[2,1408,256]{2,1,0:T(8,128)(2,1)}, bf16[2,1408,256]{2,1,0:T(8,128)(2,1)}, f32[2,8,128]{2,1,0:T(8,128)}) custom-call(s32[2,2]{1,0:T(2,128)} %bitcast.251, bf16[2,1408,768]{2,1,0:T(8,128)(2,1)} %get-tuple-element.100.q_ref.refs_1_, bf16[2,1408,768]{2,1,0:T(8,128)(2,1)} %get-tuple-element.101.k_ref.refs_2_, ...), custom_call_target="tpu_custom_call" | custom-call | flops 28521267200 | bytes 12976128 | tf_op jit(solution)/shard_map/pallas_call | solution.py:461
  458.0 10.8 %shard_map.327 = (bf16[2,2,4,1,24,768]{5,4,3,2,1,0:T(8,128)(2,1)}, bf16[2,2,4,1,24,768]{5,4,3,2,1,0:T(8,128)(2,1)}) custom-call(s32[1]{0:T(128)} %bitcast.2.refs_0_, bf16[2,1408,768]{2,1,0:T(8,128)(2,1)} %get-tuple-element.97.first_ref.refs_3_.refs_1_, bf16[2,1408,256]{2,1,0:T(8,128)(2,1)} %get-tuple-element.131.refs_2_.refs_3_, ...), custom_call_target="tpu_custom_call" | custom-call | flops 3321888768 | bytes 12000000 | tf_op jit(solution)/shard_map/pallas_call | solution.py:617
  473.7 5.7 collective-permute-start.15
  482.1 21.2 %shard_map.328 = (bf16[2,1408,768]{2,1,0:T(8,128)(2,1)}, f32[8,768]{1,0:T(8,128)}) custom-call(bf16[2,1408,512]{2,1,0:T(8,128)(2,1)} %get-tuple-element.124.refs_4_.refs_0_, bf16[2,1408,512]{2,1,0:T(8,128)(2,1)} %get-tuple-element.125.refs_5_.refs_1_, bf16[2,1408,512]{2,1,0:T(8,128)(2,1)} %get-tuple-element.126.refs_6_.refs_2_, ...), custom_call_target="tpu_custom_call" | custom-call | flops 9965666304 | bytes 32000000 | tf_op jit(solution)/shard_map/pallas_call | solution.py:506
  506.7 9.7 %shard_map.329 = (bf16[2,2,4,1,24,1024]{5,4,3,2,1,0:T(8,128)(2,1)}, bf16[2,2,4,1,24,1024]{5,4,3,2,1,0:T(8,128)(2,1)}) custom-call(s32[1]{0:T(128)} %bitcast.2.refs_0_, bf16[2,1,1536,768]{3,2,1,0:T(8,128)(2,1)} %refs_1_.1, bf16[2,1408,128]{2,1,0:T(8,128)(2,1)} %add_convert_fusion.1.hot_ref.refs_2_, bf16[2,1408,768]{2,1,0:T(8,128)(2,1)} %get-tuple-element.138.refs_3_, ...), custom_call_target="tpu_custom_call" | custom-call | flops 3875536896 | bytes 12000000 | tf_op jit(solution)/shard_map/pallas_call | solution.py:666
  526.5 5.5 collective-permute-done.19
  572.0 12.7 %collective-permute-done.33.refs_2_ = bf16[8,56,768]{2,1,0:T(8,128)(2,1)S(1)} collective-permute-done((bf16[8,56,768]{2,1,0:T(8,128)(2,1)S(1)}, bf16[8,56,768]{2,1,0:T(8,128)(2,1)S(1)}, u32[]{:S(2)}, u32[]{:S(2)}) %collective-permute-start.33) | collective-permute-done | bytes 688160 | tf_op jit(solution)/shard_map/ppermute | solution.py:696
  589.0 8.5 %shard_map.331 = (bf16[2,768,768]{2,1,0:T(8,128)(2,1)}, bf16[8,4,8,768]{3,2,1,0:T(8,128)(2,1)}, bf16[2,24,768]{2,1,0:T(8,128)(2,1)}, bf16[2,24,768]{2,1,0:T(8,12...) custom-call(s32[2]{0:T(128)} %pad_add_fusion.at_ref, ...), custom_call_target="tpu_custom_call" | custom-call | flops 2264924160 | bytes 16000000 | tf_op jit(solution)/shard_map/pallas_call | solution.py:904
  598.6 4.9 collective-permute-start.36
  623.5 8.1 %multiply_add_fusion = f32[2,768,768]{2,1,0:T(8,128)} fusion(f32[2,768,768]{2,1,0:T(8,128)} %param.31, f32[]{:T(128)S(6)} %mul.152, bf16[2,768,768]{2,1,0:T(8,128)(2,1)} %get-tuple-element.171), kind=kOutput, calls=%fused_computation | convolution fusion | flops 1815478272 | bytes 11796484 | tf_op jit(solution)/shard_map/sji,sjk->sik/dot_general | solution.py:982
  652.2 5.3 shard_map.333
  (323 shorter events, 162.9 us)
Async XLA Ops:
  7.2 166.8 %all-gather.3.cloned.1.call-start = ((), (), s32[]{:S(2)}) async-start(), calls=%async_computation.2 | async-start | bytes 10948608 | tf_op jit(solution)/shard_map/all_gather | solution.py:1028
  25.9 14.6 %collective-permute-start.1 = (bf16[2,24,3328]{2,1,0:T(8,128)(2,1)S(1)}, bf16[2,24,3328]{2,1,0:T(8,128)(2,1)S(1)}, u32[]{:S(2)}, u32[]{:S(2)}) collective-permute-start(bf16[2,24,3328]{2,1,0:T(8,128)(2,1)S(1)} %pad_maximum_fusion.1), channel_id=1, source_target_pairs={{0,2},{1,3},{2,0},{3,1},{4,6},{5,7},{6,4},{7,5},{8,10},{9,11},{10,... | collective-permute-start | bytes 958472 | tf_op jit(solution)/shard_map/ppermute | solution.py:696
  28.3 25.1 %collective-permute-start.2 = (bf16[2,24,3328]{2,1,0:T(8,128)(2,1)S(1)}, bf16[2,24,3328]{2,1,0:T(8,128)(2,1)S(1)}, u32[]{:S(2)}, u32[]{:S(2)}) collective-permute-start(bf16[2,24,3328]{2,1,0:T(8,128)(2,1)S(1)} %pad_maximum_fusion.1), channel_id=1, source_target_pairs={{0,4},{1,5},{2,6},{3,7},{4,0},{5,1},{6,2},{7,3},{8,12},{9,13},{10,... | collective-permute-start | bytes 958472 | tf_op jit(solution)/shard_map/ppermute | solution.py:696
  30.9 23.2 %collective-permute-start.3 = (bf16[2,24,3328]{2,1,0:T(8,128)(2,1)S(1)}, bf16[2,24,3328]{2,1,0:T(8,128)(2,1)S(1)}, u32[]{:S(2)}, u32[]{:S(2)}) collective-permute-start(bf16[2,24,3328]{2,1,0:T(8,128)(2,1)S(1)} %pad_maximum_fusion.1), channel_id=1, source_target_pairs={{0,6},{1,7},{2,4},{3,5},{4,2},{5,3},{6,0},{7,1},{8,14},{9,15},{10,... | collective-permute-start | bytes 958472 | tf_op jit(solution)/shard_map/ppermute | solution.py:696
  63.8 161.0 %all-gather.5.cloned.1.call-start = ((), (), s32[]{:S(2)}) async-start(), calls=%async_computation.3 | async-start | bytes 1622016 | tf_op jit(solution)/shard_map/all_gather | solution.py:1029
  66.2 24.4 %collective-permute-start.8 = (bf16[8,24,2304]{2,1,0:T(8,128)(2,1)S(1)}, bf16[8,24,2304]{2,1,0:T(8,128)(2,1)S(1)}, u32[]{:S(2)}, u32[]{:S(2)}) collective-permute-start(bf16[8,24,2304]{2,1,0:T(8,128)(2,1)S(1)} %bitcast.203), channel_id=1, source_target_pairs={{0,16},{8,24},{16,0},{24,8},{1,17},{9,25},{17,1},{25,9},{2,18},{10... | collective-permute-start | bytes 2654216 | tf_op jit(solution)/shard_map/ppermute | solution.py:696
  72.7 18.1 %collective-permute-start.7 = (bf16[8,24,2304]{2,1,0:T(8,128)(2,1)S(1)}, bf16[8,24,2304]{2,1,0:T(8,128)(2,1)S(1)}, u32[]{:S(2)}, u32[]{:S(2)}) collective-permute-start(bf16[8,24,2304]{2,1,0:T(8,128)(2,1)S(1)} %bitcast.204), channel_id=1, source_target_pairs={{0,8},{8,0},{16,24},{24,16},{1,9},{9,1},{17,25},{25,17},{2,10},{10... | collective-permute-start | bytes 2654216 | tf_op jit(solution)/shard_map/ppermute | solution.py:696
  90.6 300.3 %reduce-scatter.3.cloned.1.call-start = ((), (), s32[]{:S(2)}) async-start(), calls=%async_computation.4 | async-start | bytes 3244032 | tf_op jit(solution)/shard_map/reduce_scatter | solution.py:1040
  229.3 252.8 %reduce-scatter.5.cloned.1.call-start = ((), (), s32[]{:S(2)}) async-start(), calls=%async_computation.5 | async-start | bytes 9732096 | tf_op jit(solution)/shard_map/reduce_scatter | solution.py:1046
  418.0 38.8 %collective-permute-start.11 = (bf16[2,4,1,24,2304]{4,3,1,2,0:T(8,128)(2,1)}, bf16[2,4,1,24,2304]{4,3,1,2,0:T(8,128)(2,1)S(1)}, u32[]{:S(2)}, u32[]{:S(2)}) collective-permute-start(bf16[2,4,1,24,2304]{4,3,1,2,0:T(8,128)(2,1)} %get-tuple-element.185), channel_id=1, source_target_pairs={{0,16},{8,24},{16,0},{24,8},{1,17},{9,25},{17,1},{25,9},{2,18},{10... | collective-permute-start | bytes 2654216 | tf_op jit(solution)/shard_map/ppermute | solution.py:696
  457.7 14.2 %collective-permute-start.13 = (bf16[4,1,24,2304]{3,2,1,0:T(8,128)(2,1)}, bf16[4,1,24,2304]{3,2,1,0:T(8,128)(2,1)S(1)}, u32[]{:S(2)}, u32[]{:S(2)}) collective-permute-start(bf16[4,1,24,2304]{3,2,1,0:T(8,128)(2,1)} %get-tuple-element.189.refs_5_), channel_id=1, source_target_pairs={{0,1},{1,0},{2,3},{3,2},{4,5},{5,4},{6,7},{7,6},{8,9},{9,8},{10,11... | collective-permute-start | bytes 1327112 | tf_op jit(solution)/shard_map/ppermute | solution.py:696
  472.1 33.9 %collective-permute-start.16 = (bf16[1,24,2304]{2,1,0:T(8,128)(2,1)S(1)}, bf16[1,24,2304]{2,1,0:T(8,128)(2,1)S(1)}, u32[]{:S(2)}, u32[]{:S(2)}) collective-permute-start(bf16[1,24,2304]{2,1,0:T(8,128)(2,1)S(1)} %get-tuple-element.197.refs_14_), channel_id=1, source_target_pairs={{0,6},{1,7},{2,4},{3,5},{4,2},{5,3},{6,0},{7,1},{8,14},{9,15},{10,... | collective-permute-start | bytes 331784 | tf_op jit(solution)/shard_map/ppermute | solution.py:696
  473.7 32.2 %collective-permute-start.15 = (bf16[1,24,2304]{2,1,0:T(8,128)(2,1)S(1)}, bf16[1,24,2304]{2,1,0:T(8,128)(2,1)S(1)}, u32[]{:S(2)}, u32[]{:S(2)}) collective-permute-start(bf16[1,24,2304]{2,1,0:T(8,128)(2,1)S(1)} %get-tuple-element.198.refs_13_), channel_id=1, source_target_pairs={{0,4},{1,5},{2,6},{3,7},{4,0},{5,1},{6,2},{7,3},{8,12},{9,13},{10,... | collective-permute-start | bytes 331784 | tf_op jit(solution)/shard_map/ppermute | solution.py:696
  479.5 26.5 %collective-permute-start.14 = (bf16[1,24,2304]{2,1,0:T(8,128)(2,1)S(1)}, bf16[1,24,2304]{2,1,0:T(8,128)(2,1)S(1)}, u32[]{:S(2)}, u32[]{:S(2)}) collective-permute-start(bf16[1,24,2304]{2,1,0:T(8,128)(2,1)S(1)} %get-tuple-element.199.refs_12_), channel_id=1, source_target_pairs={{0,2},{1,3},{2,0},{3,1},{4,6},{5,7},{6,4},{7,5},{8,10},{9,11},{10,... | collective-permute-start | bytes 331784 | tf_op jit(solution)/shard_map/ppermute | solution.py:696
  481.4 23.9 %collective-permute-start.17 = (bf16[2,4,1,24,768]{4,3,1,2,0:T(8,128)(2,1)S(1)}, bf16[2,4,1,24,768]{4,3,1,2,0:T(8,128)(2,1)S(1)}, u32[]{:S(2)}, u32[]{:S(2)}) collective-permute-start(bf16[2,4,1,24,768]{4,3,1,2,0:T(8,128)(2,1)S(1)} %get-tuple-element.202), channel_id=1, source_target_pairs={{0,16},{8,24},{16,0},{24,8},{1,17},{9,25},{17,1},{25,9},{2,18},{10... | collective-permute-start | bytes 884744 | tf_op jit(solution)/shard_map/ppermute | solution.py:696
  556.3 14.5 %collective-permute-start.29 = (bf16[56,768]{1,0:T(8,128)(2,1)}, bf16[56,768]{1,0:T(8,128)(2,1)S(1)}, u32[]{:S(2)}, u32[]{:S(2)}) collective-permute-start(bf16[56,768]{1,0:T(8,128)(2,1)} %get-tuple-element.155), channel_id=1, source_target_pairs={{0,5},{1,4},{2,7},{3,6},{4,1},{5,0},{6,3},{7,2},{8,13},{9,12},{10,... | collective-permute-start | bytes 258056 | tf_op jit(solution)/shard_map/ppermute | solution.py:696
  572.0 15.4 %collective-permute-start.32 = (bf16[8,56,768]{2,1,0:T(8,128)(2,1)S(1)}, bf16[8,56,768]{2,1,0:T(8,128)(2,1)S(1)}, u32[]{:S(2)}, u32[]{:S(2)}) collective-permute-start(bf16[8,56,768]{2,1,0:T(8,128)(2,1)S(1)} %bitcast_dynamic-update-slice_fusion.refs_0_), channel_id=1, source_target_pairs={{0,8},{8,0},{16,24},{24,16},{1,9},{9,1},{17,25},{25,17},{2,10},{10... | collective-permute-start | bytes 2064392 | tf_op jit(solution)/shard_map/ppermute | solution.py:696
  603.4 14.1 %collective-permute-start.37 = (bf16[2,24,768]{2,1,0:T(8,128)(2,1)}, bf16[2,24,768]{2,1,0:T(8,128)(2,1)S(1)}, u32[]{:S(2)}, u32[]{:S(2)}) collective-permute-start(bf16[2,24,768]{2,1,0:T(8,128)(2,1)} %get-tuple-element.162), channel_id=1, source_target_pairs={{0,3},{1,2},{2,1},{3,0},{4,7},{5,6},{6,5},{7,4},{8,11},{9,10},{10,... | collective-permute-start | bytes 221192 | tf_op jit(solution)/shard_map/ppermute | solution.py:696
  604.0 14.4 %collective-permute-start.38 = (bf16[2,24,768]{2,1,0:T(8,128)(2,1)}, bf16[2,24,768]{2,1,0:T(8,128)(2,1)S(1)}, u32[]{:S(2)}, u32[]{:S(2)}) collective-permute-start(bf16[2,24,768]{2,1,0:T(8,128)(2,1)} %get-tuple-element.163), channel_id=1, source_target_pairs={{0,4},{1,5},{2,6},{3,7},{4,0},{5,1},{6,2},{7,3},{8,12},{9,13},{10,... | collective-permute-start | bytes 221192 | tf_op jit(solution)/shard_map/ppermute | solution.py:696
  617.6 23.8 %collective-permute-start.46 = (bf16[320,768]{1,0:T(8,128)(2,1)S(1)}, bf16[320,768]{1,0:T(8,128)(2,1)S(1)}, u32[]{:S(2)}, u32[]{:S(2)}) collective-permute-start(bf16[320,768]{1,0:T(8,128)(2,1)S(1)} %copy-done.11), channel_id=1, source_target_pairs={{0,16},{8,24},{16,0},{24,8},{1,17},{9,25},{17,1},{25,9},{2,18},{10... | collective-permute-start | bytes 1474568 | tf_op jit(solution)/shard_map/ppermute | solution.py:696
  618.4 26.9 %collective-permute-start.45 = (bf16[320,768]{1,0:T(8,128)(2,1)S(1)}, bf16[320,768]{1,0:T(8,128)(2,1)S(1)}, u32[]{:S(2)}, u32[]{:S(2)}) collective-permute-start(bf16[320,768]{1,0:T(8,128)(2,1)S(1)} %copy-done.11), channel_id=1, source_target_pairs={{0,8},{8,0},{16,24},{24,16},{1,9},{9,1},{17,25},{25,17},{2,10},{10... | collective-permute-start | bytes 1474568 | tf_op jit(solution)/shard_map/ppermute | solution.py:696
  622.5 15.7 %collective-permute-start.48 = (f32[24,1000]{1,0:T(8,128)S(1)}, f32[24,1000]{1,0:T(8,128)S(1)}, u32[]{:S(2)}, u32[]{:S(2)}) collective-permute-start(f32[24,1000]{1,0:T(8,128)S(1)} %get-tuple-element.173.refs_0_), channel_id=1, source_target_pairs={{0,8},{8,0},{16,24},{24,16},{1,9},{9,1},{17,25},{25,17},{2,10},{10... | collective-permute-start | bytes 288008 | tf_op jit(solution)/shard_map/ppermute | solution.py:696
  622.7 22.4 %collective-permute-start.43 = (bf16[312,768]{1,0:T(8,128)(2,1)}, bf16[312,768]{1,0:T(8,128)(2,1)S(1)}, u32[]{:S(2)}, u32[]{:S(2)}) collective-permute-start(bf16[312,768]{1,0:T(8,128)(2,1)} %shard_map.332.refs_0_), channel_id=1, source_target_pairs={{0,16},{8,24},{16,0},{24,8},{1,17},{9,25},{17,1},{25,9},{2,18},{10... | collective-permute-start | bytes 1437704 | tf_op jit(solution)/shard_map/ppermute | solution.py:696
  638.3 14.0 %collective-permute-start.42 = (bf16[312,768]{1,0:T(8,128)(2,1)S(1)}, bf16[312,768]{1,0:T(8,128)(2,1)}, u32[]{:S(2)}, u32[]{:S(2)}) collective-permute-start(bf16[312,768]{1,0:T(8,128)(2,1)S(1)} %copy-done.2), channel_id=1, source_target_pairs={{0,8},{8,0},{16,24},{24,16},{1,9},{9,1},{17,25},{25,17},{2,10},{10... | collective-permute-start | bytes 1437704 | tf_op jit(solution)/shard_map/ppermute | solution.py:696
  (84 other events, 761.4 us)
Sparse Core Ops, SparseCore 0:
  63.9 93.4 all-gather.2
  160.8 53.3 all-gather.4
  229.4 105.4 reduce-scatter.2
  340.6 141.4 reduce-scatter.4

commit v4 on v3

--- a/solution.py
+++ b/solution.py
@@ -30,6 +30,7 @@
 wide = jnp.float32
 log2e = math.log2(math.e)
 VM = 60 * 1024 * 1024
+SMALL_VM = 20 * 1024 * 1024
 
 
 def params(limit=VM):
@@ -536,7 +537,7 @@
     return ref[...].reshape(-1, ref.shape[-1])
 
 
-def weight_kernel(act_ref, dm_ref, second_ref, dup_ref, out_ref):
+def weight_kernel(act_ref, dm_ref, second_ref, dup_ref, mixed_ref, dr_ref, out_ref):
     step = pl.program_id(0)
 
     def write(a_ref, b_ref):
@@ -545,8 +546,9 @@
         for to in range(out_ref.shape[0]):
             out_ref[to, 0] = value[to * part : (to + 1) * part].astype(narrow)
 
-    pl.when(step < 4)(lambda: write(second_ref, dup_ref))
-    pl.when(step >= 4)(lambda: write(act_ref, dm_ref))
+    pl.when(step == 0)(lambda: write(mixed_ref, dr_ref))
+    pl.when((step >= 1) & (step < 5))(lambda: write(second_ref, dup_ref))
+    pl.when(step >= 5)(lambda: write(act_ref, dm_ref))
 
 
 def split_shape(rows):
@@ -558,25 +560,27 @@
     return (lax.axis_index("seq") % 2).reshape(1).astype(jnp.int32)
 
 
-def weight_call(act, dm, second, dup):
+def weight_call(act, dm, second, dup, mixed, dr):
     width = dm.shape[2]
     parts = lax.axis_size("fsdp") * lax.axis_size("seq")
     rows = held(dm.shape)
     one = (1, *dm.shape)
     return pl.pallas_call(
         weight_kernel,
-        grid=(8,),
+        grid=(9,),
         in_specs=[
-            spec(one, lambda i: (jnp.maximum(i - 4, 0), 0, 0, 0)),
+            spec(one, lambda i: (jnp.maximum(i - 5, 0), 0, 0, 0)),
             rows,
             rows,
-            spec(one, lambda i: (jnp.minimum(i, 3), 0, 0, 0)),
+            spec(one, lambda i: (jnp.clip(i - 1, 0, 3), 0, 0, 0)),
+            rows,
+            rows,
         ],
         out_specs=spec((parts, 1, width // parts, width), lambda i: (0, i, 0, 0)),
-        out_shape=jax.ShapeDtypeStruct((parts, 8, width // parts, width), narrow),
-        compiler_params=params(),
-        cost_estimate=cost(2 * 8 * dm.size * width, 60e6),
-    )(act, dm, second, dup)
+        out_shape=jax.ShapeDtypeStruct((parts, 9, width // parts, width), narrow),
+        compiler_params=params(),
+        cost_estimate=cost(2 * 9 * dm.size * width, 70e6),
+    )(act, dm, second, dup, mixed, dr)
 
 
 def one_weight_kernel(at_ref, *refs, groups):
@@ -749,16 +753,16 @@
     return [pl.BlockSpec(memory_space=pltpu.VMEM)] * count
 
 
-def settled(parts, shapes, moves):
+def settled(parts, shapes, moves, first=()):
     size = sum(part.size for part in parts) * parts[0].dtype.itemsize
     return pl.pallas_call(
-        functools.partial(settle_kernel, count=len(parts), moves=moves),
-        in_specs=[pl.BlockSpec(memory_space=pltpu.SMEM)] + in_vmem(len(parts)),
+        beside(functools.partial(settle_kernel, count=len(parts), moves=moves), 1 + len(parts), len(first)),
+        in_specs=[pl.BlockSpec(memory_space=pltpu.SMEM)] + in_vmem(len(parts)) + anywhere(first),
         out_specs=in_vmem(len(shapes)),
         out_shape=[jax.ShapeDtypeStruct(shape, parts[0].dtype) for shape in shapes],
         compiler_params=params(),
         cost_estimate=cost(0, 2 * size),
-    )(mesh_at(), *parts)
+    )(mesh_at(), *parts, *first)
 
 
 def seq_parts(x, *after):
@@ -807,19 +811,18 @@
         small_ref[to] = ref[out_ref.shape[0] * part :].astype(wide) * factor
 
 
-def collect_kernel(at_ref, slot_ref, scalar_ref, rest_ref, mid_ref, *refs, count, deep, per, columns):
+def collect_kernel(at_ref, slot_ref, scalar_ref, rest_ref, *refs, count, deep, per, columns):
     terms, (own_ref, *out_refs) = refs[:count], refs[count : count + 1 + deep]
     blocks = refs[-1]
     part, width = rest_ref.shape[1:]
     scale = 1.0 / scalar_ref[0]
     both = fold([ref[0].astype(wide) for ref in terms])
-    late = both[:, width + 256 :]
     remain = width - columns
+    late, mid = both[:, width + 256 : width + 256 + 3 * remain], both[:, width + 256 + 3 * remain :]
     pieces = [both[:, :width]]
     for i in range(3):
-        first = mid_ref[:, width + i * columns : width + (i + 1) * columns]
+        first = mid[:, i * columns : (i + 1) * columns]
         pieces.append(jnp.concatenate([first, late[:, i * remain : (i + 1) * remain]], axis=1))
-    pieces.append(mid_ref[:, :width])
     pieces += [rest_ref[i].astype(wide) for i in range(rest_ref.shape[0])]
     squares = jnp.zeros((1, 1), wide)
     total = jnp.zeros((part, width), wide)
@@ -853,31 +856,30 @@
         out_ref[per * part :] = notes
 
 
-def collect_call(block_slot, scalars, rest, mid, terms, per, columns):
+def collect_call(block_slot, scalars, rest, terms, per, columns, first):
     part, width = rest.shape[1:]
     deep = lax.axis_size("fsdp")
     count = block_slot.shape[0]
     smem = pl.BlockSpec(memory_space=pltpu.SMEM)
     message = jax.ShapeDtypeStruct((per * part + 8, width), narrow)
     return pl.pallas_call(
-        functools.partial(collect_kernel, count=len(terms), deep=deep, per=per, columns=columns),
-        in_specs=[smem, smem, smem] + in_vmem(2 + len(terms)),
+        beside(
+            functools.partial(collect_kernel, count=len(terms), deep=deep, per=per, columns=columns),
+            4 + len(terms),
+            len(first),
+        ),
+        in_specs=[smem, smem, smem] + in_vmem(1 + len(terms)) + anywhere(first),
         out_specs=in_vmem(1 + deep),
         out_shape=[jax.ShapeDtypeStruct((count * part + part // 3, width), narrow)] + [message] * deep,
         scratch_shapes=[pltpu.VMEM((count + 1, part, width), narrow)],
         compiler_params=params(),
         cost_estimate=cost(0, 4e6),
-    )(mesh_at(), block_slot, scalars, rest, mid, *terms)
-
-
-def halves(x):
-    high = x.astype(narrow)
-    return high, (x - high.astype(wide)).astype(narrow)
+    )(mesh_at(), block_slot, scalars, rest, *terms, *first)
 
 
 def direction_kernel(at_ref, left_ref, right_ref, *refs, count, deep):
     parts, slotted_ref, notes_ref = refs[:count], refs[count], refs[count + 1]
-    out_refs, rows, result = refs[count + 2 : count + 2 + deep], refs[-2], refs[-1]
+    out_ref, rows = refs[count + 2 :]
     per, _, part, width = left_ref.shape
     for j, ref in enumerate(parts):
         for k in range(deep):
@@ -888,14 +890,9 @@
     for i in range(per):
         grad = rows[i].reshape(deep * count * part, width).astype(narrow)
         slotted_ref[i] = grad
-        left_high, left_low = halves(left_ref[i].reshape(deep * part, width))
-        inner_high, inner_low = halves(dot(left_high, grad) + dot(left_low, grad))
-        right_high, right_low = halves(right_ref[i])
-        value = dot(inner_high, right_high) + dot(inner_low, right_high) + dot(inner_high, right_low)
-        result[i] = value.reshape(deep, part, width)
-    for k, out_ref in enumerate(out_refs):
-        for i in range(per):
-            out_ref[i] = result[i, at_ref[0] ^ k].astype(narrow)
+        inner = dot(left_ref[i].astype(wide).reshape(deep * part, width).astype(narrow), grad)
+        value = dot(inner.astype(narrow), right_ref[i])
+        out_ref[:, i] = value.reshape(deep, part, width).astype(narrow)
 
 
 def direction_call(left, right, parts):
@@ -904,44 +901,56 @@
     return pl.pallas_call(
         functools.partial(direction_kernel, count=count, deep=deep),
         in_specs=[pl.BlockSpec(memory_space=pltpu.SMEM)] + in_vmem(2 + count),
-        out_specs=in_vmem(2 + deep),
+        out_specs=in_vmem(3),
         out_shape=[
             jax.ShapeDtypeStruct((per, width, width), narrow),
             jax.ShapeDtypeStruct((deep, count, 8, width), narrow),
-        ]
-        + [jax.ShapeDtypeStruct((per, part, width), narrow)] * deep,
-        scratch_shapes=[
-            pltpu.VMEM((per, deep * count, part, width), wide),
-            pltpu.VMEM((per, deep, part, width), wide),
+            jax.ShapeDtypeStruct((deep, per, part, width), narrow),
         ],
+        scratch_shapes=[pltpu.VMEM((per, deep * count, part, width), wide)],
         compiler_params=params(),
         cost_estimate=cost(10 * per * deep * part * width * width, 16e6),
     )(mesh_at(), left, right, *parts)
 
 
-def select_kernel(at_ref, slot_ref, *refs, deep):
-    parts, out_ref, slots = refs[:deep], refs[deep], refs[deep + 1]
-    per, part = parts[0].shape[:2]
-    for k, ref in enumerate(parts):
-        for i in range(per):
-            slots[(at_ref[0] ^ k) * per + i] = ref[i]
+def select_kernel(slot_ref, slots_ref, out_ref):
+    per, part = slots_ref.shape[1:3]
     for b in range(out_ref.shape[0] // part):
-        out_ref[b * part : (b + 1) * part] = slots[slot_ref[b]]
-
-
-def select_call(block_slot, parts):
-    per, part, width = parts[0].shape
-    deep = len(parts)
-    smem = pl.BlockSpec(memory_space=pltpu.SMEM)
-    return pl.pallas_call(
-        functools.partial(select_kernel, deep=deep),
-        in_specs=[smem, smem] + in_vmem(deep),
+        slot = slot_ref[b]
+        out_ref[b * part : (b + 1) * part] = slots_ref[slot // per, slot % per]
+
+
+def select_call(block_slot, slots, first):
+    part, width = slots.shape[2:]
+    return pl.pallas_call(
+        beside(select_kernel, 2, len(first)),
+        in_specs=[pl.BlockSpec(memory_space=pltpu.SMEM)] + in_vmem(1) + anywhere(first),
         out_specs=pl.BlockSpec(memory_space=pltpu.VMEM),
         out_shape=jax.ShapeDtypeStruct((block_slot.shape[0] * part, width), narrow),
-        scratch_shapes=[pltpu.VMEM((deep * per, part, width), narrow)],
         compiler_params=params(),
         cost_estimate=cost(0, 2e6),
-    )(mesh_at(), block_slot, *parts)
+    )(block_slot, slots, *first)
+
+
+def stats_kernel(factor_ref, grad_ref, left_ref, right_ref, left_out, right_out):
+    grad = grad_ref[0]
+    share = (1 - stat_decay) * factor_ref[0] * factor_ref[0]
+    left_out[0] = stat_decay * left_ref[0] + share * dot(grad, grad, 1, 1)
+    right_out[0] = stat_decay * right_ref[0] + share * dot(grad, grad, 0, 0)
+
+
+def stats_call(factor, grads, left, right, first):
+    per, width, _ = grads.shape
+    one = spec((1, width, width), lambda i: (i, 0, 0))
+    return pl.pallas_call(
+        beside(stats_kernel, 4, len(first)),
+        grid=(per,),
+        in_specs=[pl.BlockSpec(memory_space=pltpu.SMEM), one, one, one] + anywhere(first),
+        out_specs=[one, one],
+        out_shape=[jax.ShapeDtypeStruct(left.shape, wide)] * 2,
+        compiler_params=params(),
+        cost_estimate=cost(4 * per * width**3, 20e6),
+    )(factor.reshape(1), grads, left, right, *first)
 
 
 def update_kernel(at_ref, factor_ref, block_ref, *refs, count, part):
@@ -955,16 +964,16 @@
             out_ref[b, to] = old - shampoo_rate * (step + decay_rate * old)
 
 
-def finish_call(kernel, factor, arrays, parts, part, shapes):
+def finish_call(kernel, factor, arrays, parts, part, shapes, first=()):
     smem = pl.BlockSpec(memory_space=pltpu.SMEM)
     return pl.pallas_call(
-        functools.partial(kernel, count=len(parts), part=part),
-        in_specs=[smem, smem] + in_vmem(len(arrays) + len(parts)),
+        beside(functools.partial(kernel, count=len(parts), part=part), 2 + len(arrays) + len(parts), len(first)),
+        in_specs=[smem, smem] + in_vmem(len(arrays) + len(parts)) + anywhere(first),
         out_specs=in_vmem(len(shapes)),
         out_shape=[jax.ShapeDtypeStruct(shape, wide) for shape in shapes],
         compiler_params=params(),
         cost_estimate=cost(0, 12e6),
-    )(mesh_at(), factor.reshape(1), *arrays, *parts)
+    )(mesh_at(), factor.reshape(1), *arrays, *parts, *first)
 
 
 def adam(weight, grad, first, second, rate, decay):
@@ -1002,7 +1011,13 @@
     ).astype(narrow)
     opening = my_rows(jnp.concatenate([blocks[0].astype(narrow), small], axis=1)[None])[0]
     project = my_rows(blocks[1:4]).astype(narrow).transpose(1, 0, 2).reshape(part, 3 * width)
-    every = far_exchange(near_exchange(jnp.concatenate([opening, project], axis=1)))
+    near = near_exchange(jnp.concatenate([opening, project], axis=1))
+    every = far_exchange(near)
+    positions, lengths, res_weights, labels, later, later_head, left_part, right_part, _ = lax.optimization_barrier(
+        (positions, lengths, res_weights, labels, blocks, head, left_roots, right_roots, near)
+    )
+    left_part = pick_index(left_part.reshape(left_roots.shape[0], deep, size, part, width), me_s, 2).astype(narrow)
+    right_part = right_part.astype(narrow)
     places = positions[:, :, 0, :ROWS]
     grid = jnp.arange(grid_rows)
     hot = jnp.concatenate([places[i][:, :, None] == grid for i in range(2)], axis=2).astype(narrow)
@@ -1015,12 +1030,13 @@
         return jnp.broadcast_to(x, (8 * mb, 128))
 
     seq_columns = [column(1.0 / lengths.astype(wide)), column(res_weights), column(labels)]
-    rest_part = my_rows(blocks[4:13]).astype(narrow)
-    head_part = my_rows(head[None])[0].astype(narrow)
-    ahead = (hot, ones, pick, rest_part, head_part, *seq_columns)
+    rest_part = my_rows(later[4:13]).astype(narrow)
+    head_part = my_rows(later_head[None])[0].astype(narrow)
+    ahead = (hot, ones, pick, rest_part, head_part, left_part, right_part, *seq_columns)
     every = [every[0], tied(every[1], *ahead), *every[2:]]
-    opening = seq_parts(stacked([x[:, :, : width + 256] for x in every]))
-    project = stacked([x[:, :, width + 256 :] for x in every])
+    opening = stacked([x[:, :, : width + 256] for x in every])
+    project = tied(stacked([x[:, :, width + 256 :] for x in every]), opening)
+    opening = seq_parts(opening)
     w_embed = settle_rows(opening, [(0, part, 0, ())], [(deep, size, part, width + 256)])[0]
     w_embed = w_embed.reshape(width, width + 256)
     gains_full = w_embed[:, width + 128 :].T[:8].astype(wide)
@@ -1030,7 +1046,7 @@
 
     embed, first = embed_call(patches, hot, tied(w_embed, project), gains_full)
     w_project = settle_rows(
-        seq_parts(tied(project, opening[-1]), first), [(0, part, 0, ())], [(deep, size, part, 3 * width)]
+        seq_parts(project, first), [(0, part, 0, ())], [(deep, size, part, 3 * width)]
     )[0].reshape(width, 3 * width)
     query, keys, values, *kept = project_call(first, w_project, gains_full, ones)
     mixed, stat = attend_call(lengths, query, keys, values)
@@ -1042,7 +1058,7 @@
     dm, d_up, dr, d_mixed, delta, d_gain_rest = backward_call(
         lengths, d_pool.reshape(mb, 8, width), unit3, unit2, row_stat, slope, mixed, w_rest, gains_full, pick
     )
-    d_rest = weight_call(act, dm, second, d_up)
+    d_rest = weight_call(act, dm, second, d_up, mixed, dr)
     own_rest = lax.psum_scatter(d_rest, ("fsdp", "seq"), scatter_dimension=0, tiled=True)[0]
 
     pairs = HEADS // 2
@@ -1058,63 +1074,60 @@
         return out[:3], out[3]
 
     grads_one, gain_one = heads_back([d_rest], 0, early)
-    mid_core = core_terms(*one_weight_call((mixed, dr), (first, *grads_one), first=[head_sum]))
+    mid_core = core_terms(*one_weight_call((first, *grads_one), first=[head_sum]))
     mid_x = Sum(mid_core, X)
     grads_two, gain_two = heads_back(mid_x.sent, early, pairs - early)
     mid_y = Sum(mid_x.after(grads_two[0]), Y)
     late_core = core_terms(*one_weight_call((first, *grads_two), first=mid_y.sent))
     late_x = Sum(late_core, X)
-    mid_z = Sum(mid_y.after(late_core[0]), Z)
     d_embed, d_gain_first = first_call(
-        (*grads_one, *grads_two), embed, dr, w_project, gains_full, [own_rest, *late_x.sent, *mid_z.sent]
+        (*grads_one, *grads_two), embed, dr, w_project, gains_full, late_x.sent
     )
     late_y = Sum(late_x.after(d_embed), Y)
-    own_mid = fold([x.astype(wide) for x in mid_z.after(d_embed)])
     d_gain_heads = jnp.concatenate([gain_one, gain_two], axis=0).transpose(1, 0, 2).reshape(8, width)
     d_gains = jnp.concatenate(
         [d_gain_first[:1], d_gain_heads[:2], d_gain_rest[3:5], jnp.zeros((123, width), wide)], axis=0
     ).T
-    e_own, e_sent = embed_weight_call(patches, hot, d_embed, d_gains, [own_mid, *late_y.sent])
+    e_own, e_sent = embed_weight_call(patches, hot, d_embed, d_gains, [own_rest, *late_y.sent])
     head_sum = tied(head_sum, e_own) / weight_sum
     scalars = jnp.stack([weight_sum, jnp.sum(jnp.square(head_sum)), loss[0, 0]])
-    left_part = pick_index(
-        tied(left_roots, e_own).reshape(left_roots.shape[0], deep, size, part, width), me_s, 2
-    )
     last_y = Sum(Sum(core_terms(e_own, e_sent), X).terms, Y)
     both_z = Sum(
-        [jnp.concatenate([a.astype(wide), b.astype(wide)], axis=3) for a, b in zip(last_y.terms, late_y.terms)], Z
+        [
+            jnp.concatenate([x.astype(wide) for x in terms], axis=3)
+            for terms in zip(last_y.terms, late_y.terms, mid_y.terms)
+        ],
+        Z,
     )
 
     per = left_stats.shape[0]
     count = blocks.shape[0]
     own, *outgoing = collect_call(
-        block_slot, scalars, own_rest, own_mid[0], both_z.terms, per,
-        early * 2 * HEAD,
+        block_slot, scalars, own_rest, both_z.terms, per,
+        early * 2 * HEAD, [],
     )
     arrived = seq_parts(jnp.stack([swap(x, "fsdp", k) for k, x in enumerate(outgoing)]))
-    slotted, notes, *directions = direction_call(left_part, right_roots, arrived)
+    slotted, notes, directions = direction_call(left_part, right_part, arrived)
     notes = jnp.sum(notes[:, :, :, 0].astype(wide), axis=(0, 1))
     loss_sum = notes[3] + notes[4] + notes[5]
     clip_norm = jnp.sqrt(notes[0] + notes[1] + notes[2])
     factor = jnp.minimum(1.0, clip_bound / clip_norm)
-    back = select_call(block_slot, [swap(x, "fsdp", k) for k, x in enumerate(directions)])
+    came = lax.all_to_all(directions, "fsdp", split_axis=0, concat_axis=0, tiled=True)
+    own_parts = seq_parts(tied(own, slotted))
+    head_parts = seq_parts(tied(head_sum, slotted))
+    left_new, right_new = stats_call(factor, slotted, left_stats, right_stats, [])
+    back = select_call(block_slot, came, [own_parts[-1], head_parts[-1]])
+    back_parts = seq_parts(back)
     split = (count, size, part, width)
     block_grads, small_grad = finish_call(
-        grads_kernel, factor, [], seq_parts(tied(own, slotted)), part, [split, (size, part // 3, width)]
-    )
-    blocks_new = finish_call(update_kernel, factor, [blocks.reshape(split)], seq_parts(back), part, [split])[0]
-    blocks_new = blocks_new.reshape(blocks.shape)
-    block_grads = block_grads.reshape(blocks.shape)
-    slotted = tied(slotted, back)
+        grads_kernel, factor, [], own_parts, part, [split, (size, part // 3, width)], [back]
+    )
     head_all = settled(
-        seq_parts(tied(head_sum, back)),
+        head_parts,
         [(size, *head_sum.shape)],
         [(j, (), 0, lambda f, s, j=j: j ^ s) for j in range(size)],
+        [back],
     )[0].reshape(head.shape)
-    gram_left = product("sij,skj->sik", slotted, slotted)
-    gram_right = product("sji,sjk->sik", slotted, slotted)
-    left_new = stat_decay * left_stats + ((1 - stat_decay) * factor * factor) * gram_left
-    right_new = stat_decay * right_stats + ((1 - stat_decay) * factor * factor) * gram_right
 
     small_grad = jnp.concatenate([small_grad[:, :, i * 256 : (i + 1) * 256] for i in range(3)], axis=1)
     small_grad = small_grad.reshape(lanes, 256).T
@@ -1127,6 +1140,11 @@
     head_new, head_first_new, head_second_new = adam(
         head, head_all * factor, head_first, head_second, adam_rate, decay_rate
     )
+    blocks_new = finish_call(
+        update_kernel, factor, [blocks.reshape(split)], back_parts, part, [split],
+        [block_grads, right_new, pos_new, gains_new, head_new],
+    )[0].reshape(blocks.shape)
+    block_grads = block_grads.reshape(blocks.shape)
     return (
         blocks_new, block_grads, left_new, right_new, pos_new, pos_first_new, pos_second_new,
         gains_new, gain_first_new, gain_second_new, head_new, head_first_new, head_second_new,

time: 671 us -> 656 us (0.978)
  starting transfers between devices: 61.7 us -> 48.7 us
  matrix products: 12.3 us -> 0 us
    ppermute x51 -> x41, starting transfers between devices: 61.4 us -> 38.3 us  [swap(): lax.ppermute(x, axis, [(i, i ^ bits) for i in range(lax.axis_size(axis))])]
    pallas_call x8 -> x9, Pallas kernels: 57.7 us -> 72.5 us  [the longest x1 42.3 us: weight_call(): pl.pallas_call(weight_kernel, grid=(9,), in_specs=[spec(one, lambda i: (j...]
    dot_general x2 -> x0, matrix products: 12.3 us -> none  [product(): return jnp.einsum(spec_text, a, b, preferred_element_type=wide)]
    all_to_all x0 -> x1, starting transfers between devices: none -> 9.88 us  [local(): lax.all_to_all(directions, 'fsdp', split_axis=0, concat_axis=0, tiled=True)]
    ppermute x51 -> x41, waiting for transfers between devices: 77.5 us -> 82.1 us  [swap(): lax.ppermute(x, axis, [(i, i ^ bits) for i in range(lax.axis_size(axis))])]
  transfers between devices with their start and end apart: 55 -> 46, of which waited for: 18 -> 21; matrix products, arithmetic and copies ran while one was open for 9% -> 7% of each run, Pallas kernels for 60% -> 63%
where the time goes in v4:
time: 656 us; the launch traced here: 646 us
  Pallas kernels  435 us (66%)
  waiting for transfers between devices  82.2 us (13%)
  starting transfers between devices  48.7 us (7%)
  other arithmetic  29 us (4%)
  local copies, waits for them, and re-layouts  28.9 us (4%)
  between operations  21.7 us (3%)
    pallas_call x2, Pallas kernels, attend_back_call(): pl.pallas_call(beside(attend_back_kernel, 12, len(first)), grid_spec=pltp...  107 us
    ppermute x41, waiting for transfers between devices, swap(): lax.ppermute(x, axis, [(i, i ^ bits) for i in range(lax.axis_size(axis))])  82.1 us
    pallas_call x1, Pallas kernels, backward_call(): pl.pallas_call(backward_kernel, grid_spec=pltpu.PrefetchScalarGridSpec(nu...  52.4 us
    pallas_call x1, Pallas kernels, attend_call(): pl.pallas_call(attend_kernel, grid_spec=pltpu.PrefetchScalarGridSpec(num_...  52.1 us
    pallas_call x1, Pallas kernels, forward_call(): pl.pallas_call(forward_kernel, grid_spec=pltpu.PrefetchScalarGridSpec(num...  51 us
    pallas_call x1, Pallas kernels, weight_call(): pl.pallas_call(weight_kernel, grid=(9,), in_specs=[spec(one, lambda i: (j...  42.3 us
    ppermute x41, starting transfers between devices, swap(): lax.ppermute(x, axis, [(i, i ^ bits) for i in range(lax.axis_size(axis))])  38.3 us
    pallas_call x2, Pallas kernels, one_weight_call(): pl.pallas_call(beside(functools.partial(one_weight_kernel, groups=[len(gr...  24.3 us
  transfers between devices with their start and end apart: 46, of which 21 were waited for; matrix products, arithmetic and copies ran while one was open for 7% of the time, Pallas kernels for 63%

profile of v4, /device:TPU:0, one launch (start us, length us, event | category | flops | bytes accessed | tf_op | source)
XLA Modules:
  0.0 645.7 jit_solution(16517690467848888645)
XLA Ops:
  36.3 5.8 collective-permute-done.1
  44.2 4.6 collective-permute-done.2
  50.4 8.6 %collective-permute-done.5.refs_3_ = bf16[8,24,1024]{2,1,0:T(8,128)(2,1)S(1)} collective-permute-done((bf16[8,24,1024]{2,1,0:T(8,128)(2,1)S(1)}, bf16[8,24,1024]{2,1,0:T(8,128)(2,1)S(1)}, u32[]{:S(2)}, u32[]{:S(2)}) %collective-permute-start.5) | collective-permute-done | bytes 393248 | tf_op jit(solution)/shard_map/ppermute | solution.py:700
  68.9 11.8 %shard_map.316 = (f32[2,1408,768]{2,1,0:T(8,128)}, bf16[2,1408,768]{2,1,0:T(8,128)(2,1)}) custom-call(bf16[2,1,1536,768]{3,2,1,0:T(8,128)(2,1)} %refs_1_.2, bf16[2,1408,128]{2,1,0:T(8,128)(2,1)} %add_convert_fusion.hot_ref.refs_2_, bf16[768,1024]{1,0:T(8,128)(2,1)} %bitcast.195, f32[8,768]{1,0:T(8,128)} %slice_convert_fusion.1.gain_ref.refs_10_.refs_9_), custom_call_target="tpu_custom_call" | custom-call | flops 3875536896 | bytes 20000000 | tf_op jit(solution)/shard_map/pallas_call | solution.py:89
  80.7 5.9 collective-permute-done.8.refs_3_
  93.2 22.7 %shard_map.318 = (bf16[2,1408,768]{2,1,0:T(8,128)(2,1)}, bf16[2,1408,768]{2,1,0:T(8,128)(2,1)}, bf16[2,1408,768]{2,1,0:T(8,128)(2,1)}, bf16[2,1408,768]{2,1,0:T(...) custom-call(bf16[2,1408,768]{2,1,0:T(8,128)(2,1)} %get-tuple-element.106.fi, ...), custom_call_target="tpu_custom_call" | custom-call | flops 9965666304 | bytes 30000000 | tf_op jit(solution)/shard_map/pallas_call | solution.py:135
  115.9 52.1 %shard_map.319 = (bf16[2,1408,768]{2,1,0:T(8,128)(2,1)}, f32[2,1408,128]{2,1,0:T(8,128)}) custom-call(s32[2,2]{1,0:T(2,128)} %bitcast.234, bf16[2,1408,768]{2,1,0:T(8,128)(2,1)} %get-tuple-element.108.q_ref.refs_1_, bf16[2,1408,768]{2,1,0:T(8,128)(2,1)} %get-tuple-element.109.k_ref.refs_2_, bf16[2,1408,768]{2,1,0:T(8,128)(2,1)} %get-tuple-element.110.v_ref.refs_3_), custom_call_target="tpu_custom_call" | custom-call | flops 34225520640 | bytes 17301504 | tf_op jit(solution)/shard_map/pallas_call | solution.py:197
  168.0 51.0 %shard_map.320 = (bf16[2,1408,768]{2,1,0:T(8,128)(2,1)}, bf16[4,2,1408,768]{3,2,1,0:T(8,128)(2,1)}, bf16[4,2,1408,768]{3,2,1,0:T(8,128)(2,1)}, bf16[2,1408,768]{...) custom-call(s32[2,2]{1,0:T(2,128)} %bitcast.235, ...), custom_call_target="tpu_custom_call" | custom-call | flops 29896998912 | bytes 80000000 | tf_op jit(solution)/shard_map/pallas_call | solution.py:261
  223.4 52.4 %shard_map.322 = (bf16[2,1408,768]{2,1,0:T(8,128)(2,1)}, bf16[4,2,1408,768]{3,2,1,0:T(8,128)(2,1)}, bf16[2,1408,768]{2,1,0:T(8,128)(2,1)}, bf16[2,1408,768]{2,1,...) custom-call(s32[2,2]{1,0:T(2,128)} %bitcast.236, f32[2,8,768]{2,1,0:T(8,128)} %bitcast.243, ...), custom_call_target="tpu_custom_call" | custom-call | flops 29896998912 | bytes 70000000 | tf_op jit(solution)/shard_map/pallas_call | solution.py:364
  275.8 42.3 %shard_map.323.refs_12_ = bf16[32,9,24,768]{3,2,1,0:T(8,128)(2,1)} custom-call(bf16[4,2,1408,768]{3,2,1,0:T(8,128)(2,1)} %get-tuple-element.128.act_ref, bf16[2,1408,768]{2,1,0:T(8,128)(2,1)} %get-tuple-element.129.dm_ref, bf16[2,1408,768]{2,1,0:T(8,128)(2,1)} %get-tuple-element.130.second_ref, bf16[4,2,1408,768]{3,2,1,0:T(8,128)(2,1)} %get-tuple-element.131.dup_ref, ...), custom_call_target="tpu_custom_call" | custom-call | flops 29896998912 | bytes 70000000 | tf_op jit(solution)/shard_map/pallas_call | solution.py:568
  321.4 70.4 %shard_map.324 = (bf16[2,1408,512]{2,1,0:T(8,128)(2,1)}, bf16[2,1408,512]{2,1,0:T(8,128)(2,1)}, bf16[2,1408,512]{2,1,0:T(8,128)(2,1)}, f32[4,8,128]{2,1,0:T(8,128)}) custom-call(s32[2,2]{1,0:T(2,128)} %bitcast.237, bf16[2,1408,768]{2,1,0:T(8,128)(2,1)} %get-tuple-element.108.q_ref.refs_1_, bf16[2,1408,768]{2,1,0:T(8,128)(2,1)} %get-tuple-element.109.k_ref.refs_2_, ...), custom_call_target="tpu_custom_call" | custom-call | flops 57042534400 | bytes 25952256 | tf_op jit(solution)/shard_map/pallas_call | solution.py:462
  391.9 13.3 %shard_map.325 = (bf16[2,2,4,1,24,1536]{5,4,3,2,1,0:T(8,128)(2,1)}, bf16[2,2,4,1,24,1536]{5,4,3,2,1,0:T(8,128)(2,1)}) custom-call(s32[1]{0:T(128)} %bitcast.38.refs_0_, bf16[2,1408,768]{2,1,0:T(8,128)(2,1)} %get-tuple-element.106.first_ref.refs_1_, bf16[2,1408,512]{2,1,0:T(8,128)(2,1)} %get-tuple-element.133.refs_2_.refs_0_, ...), custom_call_target="tpu_custom_call" | custom-call | flops 6643777536 | bytes 12000000 | tf_op jit(solution)/shard_map/pallas_call | solution.py:621
  412.2 36.8 %shard_map.326 = (bf16[2,1408,256]{2,1,0:T(8,128)(2,1)}, bf16[2,1408,256]{2,1,0:T(8,128)(2,1)}, bf16[2,1408,256]{2,1,0:T(8,128)(2,1)}, f32[2,8,128]{2,1,0:T(8,128)}) custom-call(s32[2,2]{1,0:T(2,128)} %bitcast.238, bf16[2,1408,768]{2,1,0:T(8,128)(2,1)} %get-tuple-element.108.q_ref.refs_1_, bf16[2,1408,768]{2,1,0:T(8,128)(2,1)} %get-tuple-element.109.k_ref.refs_2_, ...), custom_call_target="tpu_custom_call" | custom-call | flops 28521267200 | bytes 12976128 | tf_op jit(solution)/shard_map/pallas_call | solution.py:462
  449.9 10.9 %shard_map.327 = (bf16[2,2,4,1,24,768]{5,4,3,2,1,0:T(8,128)(2,1)}, bf16[2,2,4,1,24,768]{5,4,3,2,1,0:T(8,128)(2,1)}) custom-call(s32[1]{0:T(128)} %bitcast.38.refs_0_, bf16[2,1408,768]{2,1,0:T(8,128)(2,1)} %get-tuple-element.106.first_ref.refs_1_, bf16[2,1408,256]{2,1,0:T(8,128)(2,1)} %get-tuple-element.138.refs_2_.refs_3_, ...), custom_call_target="tpu_custom_call" | custom-call | flops 3321888768 | bytes 12000000 | tf_op jit(solution)/shard_map/pallas_call | solution.py:621
  465.5 21.4 %shard_map.328 = (bf16[2,1408,768]{2,1,0:T(8,128)(2,1)}, f32[8,768]{1,0:T(8,128)}) custom-call(bf16[2,1408,512]{2,1,0:T(8,128)(2,1)} %get-tuple-element.133.refs_2_.refs_0_, bf16[2,1408,512]{2,1,0:T(8,128)(2,1)} %get-tuple-element.134.refs_3_.refs_1_, bf16[2,1408,512]{2,1,0:T(8,128)(2,1)} %get-tuple-element.135.refs_4_.refs_2_, ...), custom_call_target="tpu_custom_call" | custom-call | flops 9965666304 | bytes 32000000 | tf_op jit(solution)/shard_map/pallas_call | solution.py:507
  489.6 9.6 %shard_map.329 = (bf16[2,2,4,1,24,1024]{5,4,3,2,1,0:T(8,128)(2,1)}, bf16[2,2,4,1,24,1024]{5,4,3,2,1,0:T(8,128)(2,1)}) custom-call(s32[1]{0:T(128)} %bitcast.38.refs_0_, bf16[2,1,1536,768]{3,2,1,0:T(8,128)(2,1)} %refs_1_.2, bf16[2,1408,128]{2,1,0:T(8,128)(2,1)} %add_convert_fusion.hot_ref.refs_2_, bf16[2,1408,768]{2,1,0:T(8,128)(2,1)} %get-tuple-element.144.refs_3_, ...), custom_call_target="tpu_custom_call" | custom-call | flops 3875536896 | bytes 12000000 | tf_op jit(solution)/shard_map/pallas_call | solution.py:670
  509.4 4.9 collective-permute-done.15
  532.7 6.2 collective-permute-done.20.refs_6_
  554.7 5.0 collective-permute-done.25
  563.4 11.3 %collective-permute-done.30.refs_2_ = bf16[8,56,768]{2,1,0:T(8,128)(2,1)S(1)} collective-permute-done((bf16[8,56,768]{2,1,0:T(8,128)(2,1)S(1)}, bf16[8,56,768]{2,1,0:T(8,128)(2,1)S(1)}, u32[]{:S(2)}, u32[]{:S(2)}) %collective-permute-start.30) | collective-permute-done | bytes 688160 | tf_op jit(solution)/shard_map/ppermute | solution.py:700
  577.6 5.8 shard_map.331
  583.8 9.9 %all-to-all-start = ((bf16[8,2,24,768]{3,2,1,0:T(8,128)(2,1)}), bf16[8,2,24,768]{3,2,1,0:T(8,128)(2,1)S(1)}, u32[]{:S(2)}, u32[]{:S(2)}) async-start(bf16[8,2,24,768]{3,2,1,0:T(8,128)(2,1)} %get-tuple-element.163), calls=%async_computation.2 | async-start | bytes 1179648 | tf_op jit(solution)/shard_map/all_to_all | solution.py:1115
  601.0 8.4 %shard_map.334 = (f32[2,768,768]{2,1,0:T(8,128)}, f32[2,768,768]{2,1,0:T(8,128)}) custom-call(f32[1]{0:T(128)} %bitcast.92.refs_1_.refs_0_, bf16[2,768,768]{2,1,0:T(8,128)(2,1)} %get-tuple-element.165.refs_1_, f32[2,768,768]{2,1,0:T(8,128)} %refs_2_.1, f32[2,768,768]{2,1,0:T(8,128)} %refs_3_.1), custom_call_target="tpu_custom_call" | custom-call | flops 3623878656 | bytes 20000000 | tf_op jit(solution)/shard_map/pallas_call | solution.py:945
  631.4 5.3 shard_map.336
  (297 shorter events, 147.5 us)
Async XLA Ops:
  7.2 160.8 %all-gather.3.cloned.1.call-start = ((), (), s32[]{:S(2)}) async-start(), calls=%async_computation.3 | async-start | bytes 10948608 | tf_op jit(solution)/shard_map/all_gather | solution.py:1044
  18.5 25.6 %collective-permute-start.3 = (bf16[2,24,3328]{2,1,0:T(8,128)(2,1)S(1)}, bf16[2,24,3328]{2,1,0:T(8,128)(2,1)S(1)}, u32[]{:S(2)}, u32[]{:S(2)}) collective-permute-start(bf16[2,24,3328]{2,1,0:T(8,128)(2,1)S(1)} %pad_maximum_fusion.2), channel_id=1, source_target_pairs={{0,6},{1,7},{2,4},{3,5},{4,2},{5,3},{6,0},{7,1},{8,14},{9,15},{10,... | collective-permute-start | bytes 958472 | tf_op jit(solution)/shard_map/ppermute | solution.py:700
  22.4 26.4 %collective-permute-start.2 = (bf16[2,24,3328]{2,1,0:T(8,128)(2,1)S(1)}, bf16[2,24,3328]{2,1,0:T(8,128)(2,1)S(1)}, u32[]{:S(2)}, u32[]{:S(2)}) collective-permute-start(bf16[2,24,3328]{2,1,0:T(8,128)(2,1)S(1)} %pad_maximum_fusion.2), channel_id=1, source_target_pairs={{0,4},{1,5},{2,6},{3,7},{4,0},{5,1},{6,2},{7,3},{8,12},{9,13},{10,... | collective-permute-start | bytes 958472 | tf_op jit(solution)/shard_map/ppermute | solution.py:700
  22.4 19.7 %collective-permute-start.1 = (bf16[2,24,3328]{2,1,0:T(8,128)(2,1)S(1)}, bf16[2,24,3328]{2,1,0:T(8,128)(2,1)S(1)}, u32[]{:S(2)}, u32[]{:S(2)}) collective-permute-start(bf16[2,24,3328]{2,1,0:T(8,128)(2,1)S(1)} %pad_maximum_fusion.2), channel_id=1, source_target_pairs={{0,2},{1,3},{2,0},{3,1},{4,6},{5,7},{6,4},{7,5},{8,10},{9,11},{10,... | collective-permute-start | bytes 958472 | tf_op jit(solution)/shard_map/ppermute | solution.py:700
  60.8 158.2 %all-gather.5.cloned.1.call-start = ((), (), s32[]{:S(2)}) async-start(), calls=%async_computation.4 | async-start | bytes 1622016 | tf_op jit(solution)/shard_map/all_gather | solution.py:1045
  62.2 24.4 %collective-permute-start.8 = (bf16[8,24,2304]{2,1,0:T(8,128)(2,1)S(1)}, bf16[8,24,2304]{2,1,0:T(8,128)(2,1)S(1)}, u32[]{:S(2)}, u32[]{:S(2)}) collective-permute-start(bf16[8,24,2304]{2,1,0:T(8,128)(2,1)S(1)} %bitcast.190), channel_id=1, source_target_pairs={{0,16},{8,24},{16,0},{24,8},{1,17},{9,25},{17,1},{25,9},{2,18},{10... | collective-permute-start | bytes 2654216 | tf_op jit(solution)/shard_map/ppermute | solution.py:700
  64.4 22.5 %collective-permute-start.7 = (bf16[8,24,2304]{2,1,0:T(8,128)(2,1)S(1)}, bf16[8,24,2304]{2,1,0:T(8,128)(2,1)S(1)}, u32[]{:S(2)}, u32[]{:S(2)}) collective-permute-start(bf16[8,24,2304]{2,1,0:T(8,128)(2,1)S(1)} %bitcast.191), channel_id=1, source_target_pairs={{0,8},{8,0},{16,24},{24,16},{1,9},{9,1},{17,25},{25,17},{2,10},{10... | collective-permute-start | bytes 2654216 | tf_op jit(solution)/shard_map/ppermute | solution.py:700
  86.6 305.3 %reduce-scatter.3.cloned.1.call-start = ((), (), s32[]{:S(2)}) async-start(), calls=%async_computation.5 | async-start | bytes 3244032 | tf_op jit(solution)/shard_map/reduce_scatter | solution.py:1056
  223.4 266.2 %reduce-scatter.5.cloned.1.call-start = ((), (), s32[]{:S(2)}) async-start(), calls=%async_computation.6 | async-start | bytes 10948608 | tf_op jit(solution)/shard_map/reduce_scatter | solution.py:1062
  410.7 38.3 %collective-permute-start.11 = (bf16[2,4,1,24,1536]{4,3,1,2,0:T(8,128)(2,1)S(1)}, bf16[2,4,1,24,1536]{4,3,1,2,0:T(8,128)(2,1)S(1)}, u32[]{:S(2)}, u32[]{:S(2)}) collective-permute-start(bf16[2,4,1,24,1536]{4,3,1,2,0:T(8,128)(2,1)S(1)} %get-tuple-element.187), channel_id=1, source_target_pairs={{0,16},{8,24},{16,0},{24,8},{1,17},{9,25},{17,1},{25,9},{2,18},{10... | collective-permute-start | bytes 1769480 | tf_op jit(solution)/shard_map/ppermute | solution.py:700
  465.0 23.8 %collective-permute-start.13 = (bf16[2,4,1,24,768]{4,3,1,2,0:T(8,128)(2,1)S(1)}, bf16[2,4,1,24,768]{4,3,1,2,0:T(8,128)(2,1)S(1)}, u32[]{:S(2)}, u32[]{:S(2)}) collective-permute-start(bf16[2,4,1,24,768]{4,3,1,2,0:T(8,128)(2,1)S(1)} %get-tuple-element.196), channel_id=1, source_target_pairs={{0,16},{8,24},{16,0},{24,8},{1,17},{9,25},{17,1},{25,9},{2,18},{10... | collective-permute-start | bytes 884744 | tf_op jit(solution)/shard_map/ppermute | solution.py:700
  524.5 14.4 %collective-permute-start.20 = (bf16[1,24,3328]{2,1,0:T(8,128)(2,1)S(1)}, bf16[1,24,3328]{2,1,0:T(8,128)(2,1)S(1)}, u32[]{:S(2)}, u32[]{:S(2)}) collective-permute-start(bf16[1,24,3328]{2,1,0:T(8,128)(2,1)S(1)} %get-tuple-element.184), channel_id=1, source_target_pairs={{0,4},{1,5},{2,6},{3,7},{4,0},{5,1},{6,2},{7,3},{8,12},{9,13},{10,... | collective-permute-start | bytes 479240 | tf_op jit(solution)/shard_map/ppermute | solution.py:700
  526.3 12.6 %collective-permute-start.21 = (bf16[1,24,3328]{2,1,0:T(8,128)(2,1)S(1)}, bf16[1,24,3328]{2,1,0:T(8,128)(2,1)S(1)}, u32[]{:S(2)}, u32[]{:S(2)}) collective-permute-start(bf16[1,24,3328]{2,1,0:T(8,128)(2,1)S(1)} %get-tuple-element.183), channel_id=1, source_target_pairs={{0,6},{1,7},{2,4},{3,5},{4,2},{5,3},{6,0},{7,1},{8,14},{9,15},{10,... | collective-permute-start | bytes 479240 | tf_op jit(solution)/shard_map/ppermute | solution.py:700
  546.9 12.8 %collective-permute-start.25 = (bf16[56,768]{1,0:T(8,128)(2,1)}, bf16[56,768]{1,0:T(8,128)(2,1)S(1)}, u32[]{:S(2)}, u32[]{:S(2)}) collective-permute-start(bf16[56,768]{1,0:T(8,128)(2,1)} %get-tuple-element.158), channel_id=1, source_target_pairs={{0,4},{1,5},{2,6},{3,7},{4,0},{5,1},{6,2},{7,3},{8,12},{9,13},{10,... | collective-permute-start | bytes 258056 | tf_op jit(solution)/shard_map/ppermute | solution.py:700
  548.9 13.7 %collective-permute-start.26 = (bf16[56,768]{1,0:T(8,128)(2,1)}, bf16[56,768]{1,0:T(8,128)(2,1)S(1)}, u32[]{:S(2)}, u32[]{:S(2)}) collective-permute-start(bf16[56,768]{1,0:T(8,128)(2,1)} %get-tuple-element.159), channel_id=1, source_target_pairs={{0,5},{1,4},{2,7},{3,6},{4,1},{5,0},{6,3},{7,2},{8,13},{9,12},{10,... | collective-permute-start | bytes 258056 | tf_op jit(solution)/shard_map/ppermute | solution.py:700
  550.7 11.9 %collective-permute-start.27 = (bf16[56,768]{1,0:T(8,128)(2,1)}, bf16[56,768]{1,0:T(8,128)(2,1)S(1)}, u32[]{:S(2)}, u32[]{:S(2)}) collective-permute-start(bf16[56,768]{1,0:T(8,128)(2,1)} %get-tuple-element.160), channel_id=1, source_target_pairs={{0,6},{1,7},{2,4},{3,5},{4,2},{5,3},{6,0},{7,1},{8,14},{9,15},{10,... | collective-permute-start | bytes 258056 | tf_op jit(solution)/shard_map/ppermute | solution.py:700
  562.7 12.0 %collective-permute-start.30 = (bf16[8,56,768]{2,1,0:T(8,128)(2,1)S(1)}, bf16[8,56,768]{2,1,0:T(8,128)(2,1)S(1)}, u32[]{:S(2)}, u32[]{:S(2)}) collective-permute-start(bf16[8,56,768]{2,1,0:T(8,128)(2,1)S(1)} %bitcast_dynamic-update-slice_fusion.refs_0_), channel_id=1, source_target_pairs={{0,16},{8,24},{16,0},{24,8},{1,17},{9,25},{17,1},{25,9},{2,18},{10... | collective-permute-start | bytes 2064392 | tf_op jit(solution)/shard_map/ppermute | solution.py:700
  583.5 13.3 %collective-permute-start.32 = (bf16[320,768]{1,0:T(8,128)(2,1)S(1)}, bf16[320,768]{1,0:T(8,128)(2,1)S(1)}, u32[]{:S(2)}, u32[]{:S(2)}) collective-permute-start(bf16[320,768]{1,0:T(8,128)(2,1)S(1)} %copy-done.9), channel_id=1, source_target_pairs={{0,16},{8,24},{16,0},{24,8},{1,17},{9,25},{17,1},{25,9},{2,18},{10... | collective-permute-start | bytes 1474568 | tf_op jit(solution)/shard_map/ppermute | solution.py:700
  583.8 27.6 %all-to-all-start = ((bf16[8,2,24,768]{3,2,1,0:T(8,128)(2,1)}), bf16[8,2,24,768]{3,2,1,0:T(8,128)(2,1)S(1)}, u32[]{:S(2)}, u32[]{:S(2)}) async-start(bf16[8,2,24,768]{3,2,1,0:T(8,128)(2,1)} %get-tuple-element.163), calls=%async_computation.2 | async-start | bytes 1179648 | tf_op jit(solution)/shard_map/all_to_all | solution.py:1115
  593.6 21.6 %collective-permute-start.39 = (bf16[320,768]{1,0:T(8,128)(2,1)S(1)}, bf16[320,768]{1,0:T(8,128)(2,1)S(1)}, u32[]{:S(2)}, u32[]{:S(2)}) collective-permute-start(bf16[320,768]{1,0:T(8,128)(2,1)S(1)} %copy-done.9), channel_id=1, source_target_pairs={{0,8},{8,0},{16,24},{24,16},{1,9},{9,1},{17,25},{25,17},{2,10},{10... | collective-permute-start | bytes 1474568 | tf_op jit(solution)/shard_map/ppermute | solution.py:700
  595.1 25.6 %collective-permute-start.40 = (f32[24,1000]{1,0:T(8,128)S(1)}, f32[24,1000]{1,0:T(8,128)S(1)}, u32[]{:S(2)}, u32[]{:S(2)}) collective-permute-start(f32[24,1000]{1,0:T(8,128)S(1)} %get-tuple-element.167.refs_1_), channel_id=1, source_target_pairs={{0,8},{8,0},{16,24},{24,16},{1,9},{9,1},{17,25},{25,17},{2,10},{10... | collective-permute-start | bytes 288008 | tf_op jit(solution)/shard_map/ppermute | solution.py:700
  596.7 14.6 %collective-permute-start.33 = (bf16[320,768]{1,0:T(8,128)(2,1)S(1)}, bf16[320,768]{1,0:T(8,128)(2,1)S(1)}, u32[]{:S(2)}, u32[]{:S(2)}) collective-permute-start(bf16[320,768]{1,0:T(8,128)(2,1)S(1)} %collective-permute-done.32.refs_4_), channel_id=1, source_target_pairs={{0,8},{8,0},{16,24},{24,16},{1,9},{9,1},{17,25},{25,17},{2,10},{10... | collective-permute-start | bytes 1474568 | tf_op jit(solution)/shard_map/ppermute | solution.py:700
  614.9 15.5 %collective-permute-start.36 = (bf16[312,768]{1,0:T(8,128)(2,1)}, bf16[312,768]{1,0:T(8,128)(2,1)S(1)}, u32[]{:S(2)}, u32[]{:S(2)}) collective-permute-start(bf16[312,768]{1,0:T(8,128)(2,1)} %shard_map.332.refs_6_.refs_5_.refs_3_), channel_id=1, source_target_pairs={{0,8},{8,0},{16,24},{24,16},{1,9},{9,1},{17,25},{25,17},{2,10},{10... | collective-permute-start | bytes 1437704 | tf_op jit(solution)/shard_map/ppermute | solution.py:700
  614.9 13.5 %collective-permute-start.37 = (bf16[312,768]{1,0:T(8,128)(2,1)}, bf16[312,768]{1,0:T(8,128)(2,1)S(1)}, u32[]{:S(2)}, u32[]{:S(2)}) collective-permute-start(bf16[312,768]{1,0:T(8,128)(2,1)} %shard_map.332.refs_6_.refs_5_.refs_3_), channel_id=1, source_target_pairs={{0,16},{8,24},{16,0},{24,8},{1,17},{9,25},{17,1},{25,9},{2,18},{10... | collective-permute-start | bytes 1437704 | tf_op jit(solution)/shard_map/ppermute | solution.py:700
  (72 other events, 479.3 us)
Sparse Core Ops, SparseCore 0:
  60.9 88.2 all-gather.2
  152.6 53.4 all-gather.4
  223.5 100.9 reduce-scatter.2
  330.4 149.5 reduce-scatter.4

commit v5 on v4

--- a/solution.py
+++ b/solution.py
@@ -811,14 +811,46 @@
         small_ref[to] = ref[out_ref.shape[0] * part :].astype(wide) * factor
 
 
+def join_kernel(at_ref, *refs, counts, size):
+    ins, outs = refs[: sum(counts)], refs[sum(counts) :]
+    for k in range(size):
+        at = 0
+        ref = 0
+        for count in counts:
+            value = fold([r[at_ref[0] ^ k].astype(wide) for r in ins[ref : ref + count]])
+            ref += count
+            lanes = value.shape[-1]
+            outs[k][:, :, at : at + lanes] = value.astype(outs[k].dtype)
+            at += lanes
+
+
+def join_call(groups, first):
+    axis, stride, size = levels()[Z]
+    at = (lax.axis_index(axis) // stride % size).reshape(1).astype(jnp.int32)
+    arrays = [term for terms in groups for term in terms]
+    counts = [len(terms) for terms in groups]
+    shape = (*arrays[0].shape[1:-1], sum(terms[0].shape[-1] for terms in groups))
+    own, *sent = pl.pallas_call(
+        beside(functools.partial(join_kernel, counts=counts, size=size), 1 + len(arrays), len(first)),
+        in_specs=[pl.BlockSpec(memory_space=pltpu.SMEM)] + in_vmem(len(arrays)) + anywhere(first),
+        out_specs=in_vmem(size),
+        out_shape=[jax.ShapeDtypeStruct(shape, wide)] + [jax.ShapeDtypeStruct(shape, narrow)] * (size - 1),
+        compiler_params=params(),
+        cost_estimate=cost(0, 3e6),
+    )(at, *arrays, *first)
+    return [own] + [swap(x, axis, (k + 1) * stride) for k, x in enumerate(sent)]
+
+
 def collect_kernel(at_ref, slot_ref, scalar_ref, rest_ref, *refs, count, deep, per, columns):
-    terms, (own_ref, *out_refs) = refs[:count], refs[count : count + 1 + deep]
+    terms, mid_terms = refs[:count], refs[count : 2 * count]
+    own_ref, *out_refs = refs[2 * count : 2 * count + 1 + deep]
     blocks = refs[-1]
     part, width = rest_ref.shape[1:]
     scale = 1.0 / scalar_ref[0]
     both = fold([ref[0].astype(wide) for ref in terms])
     remain = width - columns
-    late, mid = both[:, width + 256 : width + 256 + 3 * remain], both[:, width + 256 + 3 * remain :]
+    late = both[:, width + 256 :]
+    mid = fold([ref[0].astype(wide) for ref in mid_terms])
     pieces = [both[:, :width]]
     for i in range(3):
         first = mid[:, i * columns : (i + 1) * columns]
@@ -856,7 +888,7 @@
         out_ref[per * part :] = notes
 
 
-def collect_call(block_slot, scalars, rest, terms, per, columns, first):
+def collect_call(block_slot, scalars, rest, terms, mid_terms, per, columns, first):
     part, width = rest.shape[1:]
     deep = lax.axis_size("fsdp")
     count = block_slot.shape[0]
@@ -865,16 +897,16 @@
     return pl.pallas_call(
         beside(
             functools.partial(collect_kernel, count=len(terms), deep=deep, per=per, columns=columns),
-            4 + len(terms),
+            4 + 2 * len(terms),
             len(first),
         ),
-        in_specs=[smem, smem, smem] + in_vmem(1 + len(terms)) + anywhere(first),
+        in_specs=[smem, smem, smem] + in_vmem(1 + 2 * len(terms)) + anywhere(first),
         out_specs=in_vmem(1 + deep),
         out_shape=[jax.ShapeDtypeStruct((count * part + part // 3, width), narrow)] + [message] * deep,
         scratch_shapes=[pltpu.VMEM((count + 1, part, width), narrow)],
         compiler_params=params(),
         cost_estimate=cost(0, 4e6),
-    )(mesh_at(), block_slot, scalars, rest, *terms, *first)
+    )(mesh_at(), block_slot, scalars, rest, *terms, *mid_terms, *first)
 
 
 def direction_kernel(at_ref, left_ref, right_ref, *refs, count, deep):
@@ -1088,22 +1120,19 @@
     d_gains = jnp.concatenate(
         [d_gain_first[:1], d_gain_heads[:2], d_gain_rest[3:5], jnp.zeros((123, width), wide)], axis=0
     ).T
-    e_own, e_sent = embed_weight_call(patches, hot, d_embed, d_gains, [own_rest, *late_y.sent])
+    e_own, e_sent = embed_weight_call(
+        patches, hot, d_embed, d_gains, [own_rest, *late_y.sent, *mid_y.terms[1:]]
+    )
     head_sum = tied(head_sum, e_own) / weight_sum
     scalars = jnp.stack([weight_sum, jnp.sum(jnp.square(head_sum)), loss[0, 0]])
     last_y = Sum(Sum(core_terms(e_own, e_sent), X).terms, Y)
-    both_z = Sum(
-        [
-            jnp.concatenate([x.astype(wide) for x in terms], axis=3)
-            for terms in zip(last_y.terms, late_y.terms, mid_y.terms)
-        ],
-        Z,
-    )
+    mid_z = Sum(mid_y.after(e_own), Z)
+    z_terms = join_call([last_y.terms, late_y.terms], mid_z.terms[1:])
 
     per = left_stats.shape[0]
     count = blocks.shape[0]
     own, *outgoing = collect_call(
-        block_slot, scalars, own_rest, both_z.terms, per,
+        block_slot, scalars, own_rest, z_terms, mid_z.terms, per,
         early * 2 * HEAD, [],
     )
     arrived = seq_parts(jnp.stack([swap(x, "fsdp", k) for k, x in enumerate(outgoing)]))

time: 656 us -> 650 us (level)
  waiting for transfers between devices: 82.2 us -> 65.6 us
    ppermute x41 -> x44, waiting for transfers between devices: 82.1 us -> 65.4 us  [swap(): lax.ppermute(x, axis, [(i, i ^ bits) for i in range(lax.axis_size(axis))])]
    ppermute x41 -> x44, starting transfers between devices: 38.3 us -> 45 us  [swap(): lax.ppermute(x, axis, [(i, i ^ bits) for i in range(lax.axis_size(axis))])]
  transfers between devices with their start and end apart: 46 -> 49, of which waited for: 21 -> 19; matrix products, arithmetic and copies ran while one was open for 7% -> 8% of each run, Pallas kernels for 63% -> 64%
where the time goes in v5:
time: 650 us; the launch traced here: 641 us
  Pallas kernels  438 us (67%)
  waiting for transfers between devices  65.6 us (10%)
  starting transfers between devices  53.5 us (8%)
  other arithmetic  34.5 us (5%)
  local copies, waits for them, and re-layouts  28.3 us (4%)
  between operations  21.7 us (3%)
    pallas_call x2, Pallas kernels, attend_back_call(): pl.pallas_call(beside(attend_back_kernel, 12, len(first)), grid_spec=pltp...  107 us
    ppermute x44, waiting for transfers between devices, swap(): lax.ppermute(x, axis, [(i, i ^ bits) for i in range(lax.axis_size(axis))])  65.4 us
    pallas_call x1, Pallas kernels, backward_call(): pl.pallas_call(backward_kernel, grid_spec=pltpu.PrefetchScalarGridSpec(nu...  52.4 us
    pallas_call x1, Pallas kernels, attend_call(): pl.pallas_call(attend_kernel, grid_spec=pltpu.PrefetchScalarGridSpec(num_...  52.1 us
    pallas_call x1, Pallas kernels, forward_call(): pl.pallas_call(forward_kernel, grid_spec=pltpu.PrefetchScalarGridSpec(num...  51 us
    ppermute x44, starting transfers between devices, swap(): lax.ppermute(x, axis, [(i, i ^ bits) for i in range(lax.axis_size(axis))])  45 us
    pallas_call x1, Pallas kernels, weight_call(): pl.pallas_call(weight_kernel, grid=(9,), in_specs=[spec(one, lambda i: (j...  42.3 us
    pallas_call x2, Pallas kernels, one_weight_call(): pl.pallas_call(beside(functools.partial(one_weight_kernel, groups=[len(gr...  24.3 us
  transfers between devices with their start and end apart: 49, of which 19 were waited for; matrix products, arithmetic and copies ran while one was open for 8% of the time, Pallas kernels for 64%

profile of v5, /device:TPU:0, one launch (start us, length us, event | category | flops | bytes accessed | tf_op | source)
XLA Modules:
  0.0 641.3 jit_solution(14497848631132926998)
XLA Ops:
  27.4 4.0 convert_element_type.441.right_ref
  38.5 5.8 collective-permute-done.1
  46.3 4.6 collective-permute-done.2
  52.6 8.6 %collective-permute-done.5.refs_3_ = bf16[8,24,1024]{2,1,0:T(8,128)(2,1)S(1)} collective-permute-done((bf16[8,24,1024]{2,1,0:T(8,128)(2,1)S(1)}, bf16[8,24,1024]{2,1,0:T(8,128)(2,1)S(1)}, u32[]{:S(2)}, u32[]{:S(2)}) %collective-permute-start.5) | collective-permute-done | bytes 393248 | tf_op jit(solution)/shard_map/ppermute | solution.py:700
  70.8 11.8 %shard_map.316 = (f32[2,1408,768]{2,1,0:T(8,128)}, bf16[2,1408,768]{2,1,0:T(8,128)(2,1)}) custom-call(bf16[2,1,1536,768]{3,2,1,0:T(8,128)(2,1)} %refs_1_.2, bf16[2,1408,128]{2,1,0:T(8,128)(2,1)} %add_convert_fusion.hot_ref.refs_2_, bf16[768,1024]{1,0:T(8,128)(2,1)} %bitcast.192, f32[8,768]{1,0:T(8,128)} %slice_convert_fusion.1.gain_ref.refs_10_.refs_9_), custom_call_target="tpu_custom_call" | custom-call | flops 3875536896 | bytes 20000000 | tf_op jit(solution)/shard_map/pallas_call | solution.py:89
  82.7 6.0 collective-permute-done.8.refs_3_
  91.2 4.3 shard_map.317
  95.5 22.7 %shard_map.318 = (bf16[2,1408,768]{2,1,0:T(8,128)(2,1)}, bf16[2,1408,768]{2,1,0:T(8,128)(2,1)}, bf16[2,1408,768]{2,1,0:T(8,128)(2,1)}, bf16[2,1408,768]{2,1,0:T(...) custom-call(bf16[2,1408,768]{2,1,0:T(8,128)(2,1)} %get-tuple-element.111.fi, ...), custom_call_target="tpu_custom_call" | custom-call | flops 9965666304 | bytes 30000000 | tf_op jit(solution)/shard_map/pallas_call | solution.py:135
  118.2 52.1 %shard_map.319 = (bf16[2,1408,768]{2,1,0:T(8,128)(2,1)}, f32[2,1408,128]{2,1,0:T(8,128)}) custom-call(s32[2,2]{1,0:T(2,128)} %bitcast.227, bf16[2,1408,768]{2,1,0:T(8,128)(2,1)} %get-tuple-element.113.q_ref.refs_1_, bf16[2,1408,768]{2,1,0:T(8,128)(2,1)} %get-tuple-element.114.k_ref.refs_2_, bf16[2,1408,768]{2,1,0:T(8,128)(2,1)} %get-tuple-element.115.v_ref.refs_3_), custom_call_target="tpu_custom_call" | custom-call | flops 34225520640 | bytes 17301504 | tf_op jit(solution)/shard_map/pallas_call | solution.py:197
  170.3 51.0 %shard_map.320 = (bf16[2,1408,768]{2,1,0:T(8,128)(2,1)}, bf16[4,2,1408,768]{3,2,1,0:T(8,128)(2,1)}, bf16[4,2,1408,768]{3,2,1,0:T(8,128)(2,1)}, bf16[2,1408,768]{...) custom-call(s32[2,2]{1,0:T(2,128)} %bitcast.228, ...), custom_call_target="tpu_custom_call" | custom-call | flops 29896998912 | bytes 80000000 | tf_op jit(solution)/shard_map/pallas_call | solution.py:261
  221.3 4.4 shard_map.321
  225.7 52.4 %shard_map.322 = (bf16[2,1408,768]{2,1,0:T(8,128)(2,1)}, bf16[4,2,1408,768]{3,2,1,0:T(8,128)(2,1)}, bf16[2,1408,768]{2,1,0:T(8,128)(2,1)}, bf16[2,1408,768]{2,1,...) custom-call(s32[2,2]{1,0:T(2,128)} %bitcast.229, f32[2,8,768]{2,1,0:T(8,128)} %bitcast.236, ...), custom_call_target="tpu_custom_call" | custom-call | flops 29896998912 | bytes 70000000 | tf_op jit(solution)/shard_map/pallas_call | solution.py:364
  278.1 42.3 %shard_map.323.refs_12_ = bf16[32,9,24,768]{3,2,1,0:T(8,128)(2,1)} custom-call(bf16[4,2,1408,768]{3,2,1,0:T(8,128)(2,1)} %get-tuple-element.133.act_ref, bf16[2,1408,768]{2,1,0:T(8,128)(2,1)} %get-tuple-element.134.dm_ref, bf16[2,1408,768]{2,1,0:T(8,128)(2,1)} %get-tuple-element.135.second_ref, bf16[4,2,1408,768]{3,2,1,0:T(8,128)(2,1)} %get-tuple-element.136.dup_ref, ...), custom_call_target="tpu_custom_call" | custom-call | flops 29896998912 | bytes 70000000 | tf_op jit(solution)/shard_map/pallas_call | solution.py:568
  323.8 70.5 %shard_map.324 = (bf16[2,1408,512]{2,1,0:T(8,128)(2,1)}, bf16[2,1408,512]{2,1,0:T(8,128)(2,1)}, bf16[2,1408,512]{2,1,0:T(8,128)(2,1)}, f32[4,8,128]{2,1,0:T(8,128)}) custom-call(s32[2,2]{1,0:T(2,128)} %bitcast.230, bf16[2,1408,768]{2,1,0:T(8,128)(2,1)} %get-tuple-element.113.q_ref.refs_1_, bf16[2,1408,768]{2,1,0:T(8,128)(2,1)} %get-tuple-element.114.k_ref.refs_2_, ...), custom_call_target="tpu_custom_call" | custom-call | flops 57042534400 | bytes 25952256 | tf_op jit(solution)/shard_map/pallas_call | solution.py:462
  394.3 13.3 %shard_map.325 = (bf16[2,2,4,1,24,1536]{5,4,3,2,1,0:T(8,128)(2,1)}, bf16[2,2,4,1,24,1536]{5,4,3,2,1,0:T(8,128)(2,1)}) custom-call(s32[1]{0:T(128)} %bitcast.38.refs_0_, bf16[2,1408,768]{2,1,0:T(8,128)(2,1)} %get-tuple-element.111.first_ref.refs_1_, bf16[2,1408,512]{2,1,0:T(8,128)(2,1)} %get-tuple-element.138.refs_2_.refs_0_, ...), custom_call_target="tpu_custom_call" | custom-call | flops 6643777536 | bytes 12000000 | tf_op jit(solution)/shard_map/pallas_call | solution.py:621
  414.7 36.9 %shard_map.326 = (bf16[2,1408,256]{2,1,0:T(8,128)(2,1)}, bf16[2,1408,256]{2,1,0:T(8,128)(2,1)}, bf16[2,1408,256]{2,1,0:T(8,128)(2,1)}, f32[2,8,128]{2,1,0:T(8,128)}) custom-call(s32[2,2]{1,0:T(2,128)} %bitcast.231, bf16[2,1408,768]{2,1,0:T(8,128)(2,1)} %get-tuple-element.113.q_ref.refs_1_, bf16[2,1408,768]{2,1,0:T(8,128)(2,1)} %get-tuple-element.114.k_ref.refs_2_, ...), custom_call_target="tpu_custom_call" | custom-call | flops 28521267200 | bytes 12976128 | tf_op jit(solution)/shard_map/pallas_call | solution.py:462
  452.5 11.0 %shard_map.327 = (bf16[2,2,4,1,24,768]{5,4,3,2,1,0:T(8,128)(2,1)}, bf16[2,2,4,1,24,768]{5,4,3,2,1,0:T(8,128)(2,1)}) custom-call(s32[1]{0:T(128)} %bitcast.38.refs_0_, bf16[2,1408,768]{2,1,0:T(8,128)(2,1)} %get-tuple-element.111.first_ref.refs_1_, bf16[2,1408,256]{2,1,0:T(8,128)(2,1)} %get-tuple-element.143.refs_2_.refs_3_, ...), custom_call_target="tpu_custom_call" | custom-call | flops 3321888768 | bytes 12000000 | tf_op jit(solution)/shard_map/pallas_call | solution.py:621
  468.9 21.4 %shard_map.328 = (bf16[2,1408,768]{2,1,0:T(8,128)(2,1)}, f32[8,768]{1,0:T(8,128)}) custom-call(bf16[2,1408,512]{2,1,0:T(8,128)(2,1)} %get-tuple-element.138.refs_2_.refs_0_, bf16[2,1408,512]{2,1,0:T(8,128)(2,1)} %get-tuple-element.139.refs_3_.refs_1_, bf16[2,1408,512]{2,1,0:T(8,128)(2,1)} %get-tuple-element.140.refs_4_.refs_2_, ...), custom_call_target="tpu_custom_call" | custom-call | flops 9965666304 | bytes 32000000 | tf_op jit(solution)/shard_map/pallas_call | solution.py:507
  493.8 9.7 %shard_map.329 = (bf16[2,2,4,1,24,1024]{5,4,3,2,1,0:T(8,128)(2,1)}, bf16[2,2,4,1,24,1024]{5,4,3,2,1,0:T(8,128)(2,1)}) custom-call(s32[1]{0:T(128)} %bitcast.38.refs_0_, bf16[2,1,1536,768]{3,2,1,0:T(8,128)(2,1)} %refs_1_.2, bf16[2,1408,128]{2,1,0:T(8,128)(2,1)} %add_convert_fusion.hot_ref.refs_2_, bf16[2,1408,768]{2,1,0:T(8,128)(2,1)} %get-tuple-element.149.refs_3_, ...), custom_call_target="tpu_custom_call" | custom-call | flops 3875536896 | bytes 12000000 | tf_op jit(solution)/shard_map/pallas_call | solution.py:670
  559.1 10.4 %collective-permute-done.33.refs_2_ = bf16[8,56,768]{2,1,0:T(8,128)(2,1)S(1)} collective-permute-done((bf16[8,56,768]{2,1,0:T(8,128)(2,1)S(1)}, bf16[8,56,768]{2,1,0:T(8,128)(2,1)S(1)}, u32[]{:S(2)}, u32[]{:S(2)}) %collective-permute-start.33) | collective-permute-done | bytes 688160 | tf_op jit(solution)/shard_map/ppermute | solution.py:700
  571.8 5.8 shard_map.332
  579.1 8.0 %all-to-all-start = ((bf16[8,2,24,768]{3,2,1,0:T(8,128)(2,1)}), bf16[8,2,24,768]{3,2,1,0:T(8,128)(2,1)S(1)}, u32[]{:S(2)}, u32[]{:S(2)}) async-start(bf16[8,2,24,768]{3,2,1,0:T(8,128)(2,1)} %get-tuple-element.173), calls=%async_computation.2 | async-start | bytes 1179648 | tf_op jit(solution)/shard_map/all_to_all | solution.py:1144
  595.6 8.4 %shard_map.335 = (f32[2,768,768]{2,1,0:T(8,128)}, f32[2,768,768]{2,1,0:T(8,128)}) custom-call(f32[1]{0:T(128)} %bitcast.92.refs_1_.refs_0_, bf16[2,768,768]{2,1,0:T(8,128)(2,1)} %get-tuple-element.175.refs_1_, f32[2,768,768]{2,1,0:T(8,128)} %refs_2_.1, f32[2,768,768]{2,1,0:T(8,128)} %refs_3_.1), custom_call_target="tpu_custom_call" | custom-call | flops 3623878656 | bytes 20000000 | tf_op jit(solution)/shard_map/pallas_call | solution.py:977
  627.1 5.3 shard_map.337
  (288 shorter events, 149.1 us)
Async XLA Ops:
  7.2 163.1 %all-gather.3.cloned.1.call-start = ((), (), s32[]{:S(2)}) async-start(), calls=%async_computation.3 | async-start | bytes 10948608 | tf_op jit(solution)/shard_map/all_gather | solution.py:1076
  20.7 25.6 %collective-permute-start.3 = (bf16[2,24,3328]{2,1,0:T(8,128)(2,1)S(1)}, bf16[2,24,3328]{2,1,0:T(8,128)(2,1)S(1)}, u32[]{:S(2)}, u32[]{:S(2)}) collective-permute-start(bf16[2,24,3328]{2,1,0:T(8,128)(2,1)S(1)} %pad_maximum_fusion.1), channel_id=1, source_target_pairs={{0,6},{1,7},{2,4},{3,5},{4,2},{5,3},{6,0},{7,1},{8,14},{9,15},{10,... | collective-permute-start | bytes 958472 | tf_op jit(solution)/shard_map/ppermute | solution.py:700
  24.6 26.4 %collective-permute-start.2 = (bf16[2,24,3328]{2,1,0:T(8,128)(2,1)S(1)}, bf16[2,24,3328]{2,1,0:T(8,128)(2,1)S(1)}, u32[]{:S(2)}, u32[]{:S(2)}) collective-permute-start(bf16[2,24,3328]{2,1,0:T(8,128)(2,1)S(1)} %pad_maximum_fusion.1), channel_id=1, source_target_pairs={{0,4},{1,5},{2,6},{3,7},{4,0},{5,1},{6,2},{7,3},{8,12},{9,13},{10,... | collective-permute-start | bytes 958472 | tf_op jit(solution)/shard_map/ppermute | solution.py:700
  24.6 19.7 %collective-permute-start.1 = (bf16[2,24,3328]{2,1,0:T(8,128)(2,1)S(1)}, bf16[2,24,3328]{2,1,0:T(8,128)(2,1)S(1)}, u32[]{:S(2)}, u32[]{:S(2)}) collective-permute-start(bf16[2,24,3328]{2,1,0:T(8,128)(2,1)S(1)} %pad_maximum_fusion.1), channel_id=1, source_target_pairs={{0,2},{1,3},{2,0},{3,1},{4,6},{5,7},{6,4},{7,5},{8,10},{9,11},{10,... | collective-permute-start | bytes 958472 | tf_op jit(solution)/shard_map/ppermute | solution.py:700
  63.8 157.5 %all-gather.5.cloned.1.call-start = ((), (), s32[]{:S(2)}) async-start(), calls=%async_computation.4 | async-start | bytes 1622016 | tf_op jit(solution)/shard_map/all_gather | solution.py:1077
  64.3 24.4 %collective-permute-start.8 = (bf16[8,24,2304]{2,1,0:T(8,128)(2,1)S(1)}, bf16[8,24,2304]{2,1,0:T(8,128)(2,1)S(1)}, u32[]{:S(2)}, u32[]{:S(2)}) collective-permute-start(bf16[8,24,2304]{2,1,0:T(8,128)(2,1)S(1)} %bitcast.187), channel_id=1, source_target_pairs={{0,16},{8,24},{16,0},{24,8},{1,17},{9,25},{17,1},{25,9},{2,18},{10... | collective-permute-start | bytes 2654216 | tf_op jit(solution)/shard_map/ppermute | solution.py:700
  66.4 22.6 %collective-permute-start.7 = (bf16[8,24,2304]{2,1,0:T(8,128)(2,1)S(1)}, bf16[8,24,2304]{2,1,0:T(8,128)(2,1)S(1)}, u32[]{:S(2)}, u32[]{:S(2)}) collective-permute-start(bf16[8,24,2304]{2,1,0:T(8,128)(2,1)S(1)} %bitcast.188), channel_id=1, source_target_pairs={{0,8},{8,0},{16,24},{24,16},{1,9},{9,1},{17,25},{25,17},{2,10},{10... | collective-permute-start | bytes 2654216 | tf_op jit(solution)/shard_map/ppermute | solution.py:700
  88.7 305.6 %reduce-scatter.3.cloned.1.call-start = ((), (), s32[]{:S(2)}) async-start(), calls=%async_computation.5 | async-start | bytes 3244032 | tf_op jit(solution)/shard_map/reduce_scatter | solution.py:1088
  225.7 267.4 %reduce-scatter.5.cloned.1.call-start = ((), (), s32[]{:S(2)}) async-start(), calls=%async_computation.6 | async-start | bytes 10948608 | tf_op jit(solution)/shard_map/reduce_scatter | solution.py:1094
  413.0 38.6 %collective-permute-start.11 = (bf16[2,4,1,24,1536]{4,3,1,2,0:T(8,128)(2,1)S(1)}, bf16[2,4,1,24,1536]{4,3,1,2,0:T(8,128)(2,1)S(1)}, u32[]{:S(2)}, u32[]{:S(2)}) collective-permute-start(bf16[2,4,1,24,1536]{4,3,1,2,0:T(8,128)(2,1)S(1)} %get-tuple-element.193), channel_id=1, source_target_pairs={{0,16},{8,24},{16,0},{24,8},{1,17},{9,25},{17,1},{25,9},{2,18},{10... | collective-permute-start | bytes 1769480 | tf_op jit(solution)/shard_map/ppermute | solution.py:700
  464.7 28.4 %collective-permute-start.14 = (bf16[4,1,24,1536]{3,2,1,0:T(8,128)(2,1)S(1)}, bf16[4,1,24,1536]{3,2,1,0:T(8,128)(2,1)S(1)}, u32[]{:S(2)}, u32[]{:S(2)}) collective-permute-start(bf16[4,1,24,1536]{3,2,1,0:T(8,128)(2,1)S(1)} %copy-done.19), channel_id=1, source_target_pairs={{0,1},{1,0},{2,3},{3,2},{4,5},{5,4},{6,7},{7,6},{8,9},{9,8},{10,11... | collective-permute-start | bytes 884744 | tf_op jit(solution)/shard_map/ppermute | solution.py:700
  468.2 24.1 %collective-permute-start.13 = (bf16[2,4,1,24,768]{4,3,1,2,0:T(8,128)(2,1)}, bf16[2,4,1,24,768]{4,3,1,2,0:T(8,128)(2,1)S(1)}, u32[]{:S(2)}, u32[]{:S(2)}) collective-permute-start(bf16[2,4,1,24,768]{4,3,1,2,0:T(8,128)(2,1)} %get-tuple-element.202), channel_id=1, source_target_pairs={{0,16},{8,24},{16,0},{24,8},{1,17},{9,25},{17,1},{25,9},{2,18},{10... | collective-permute-start | bytes 884744 | tf_op jit(solution)/shard_map/ppermute | solution.py:700
  507.4 11.2 %collective-permute-start.16 = (bf16[2,4,1,24,1024]{4,3,1,2,0:T(8,128)(2,1)S(1)}, bf16[2,4,1,24,1024]{4,3,1,2,0:T(8,128)(2,1)S(1)}, u32[]{:S(2)}, u32[]{:S(2)}) collective-permute-start(bf16[2,4,1,24,1024]{4,3,1,2,0:T(8,128)(2,1)S(1)} %get-tuple-element.198), channel_id=1, source_target_pairs={{0,16},{8,24},{16,0},{24,8},{1,17},{9,25},{17,1},{25,9},{2,18},{10... | collective-permute-start | bytes 1179656 | tf_op jit(solution)/shard_map/ppermute | solution.py:700
  545.4 12.2 %collective-permute-start.29 = (bf16[56,768]{1,0:T(8,128)(2,1)}, bf16[56,768]{1,0:T(8,128)(2,1)S(1)}, u32[]{:S(2)}, u32[]{:S(2)}) collective-permute-start(bf16[56,768]{1,0:T(8,128)(2,1)} %get-tuple-element.169), channel_id=1, source_target_pairs={{0,5},{1,4},{2,7},{3,6},{4,1},{5,0},{6,3},{7,2},{8,13},{9,12},{10,... | collective-permute-start | bytes 258056 | tf_op jit(solution)/shard_map/ppermute | solution.py:700
  557.6 11.9 %collective-permute-start.33 = (bf16[8,56,768]{2,1,0:T(8,128)(2,1)S(1)}, bf16[8,56,768]{2,1,0:T(8,128)(2,1)S(1)}, u32[]{:S(2)}, u32[]{:S(2)}) collective-permute-start(bf16[8,56,768]{2,1,0:T(8,128)(2,1)S(1)} %bitcast_dynamic-update-slice_fusion.refs_0_), channel_id=1, source_target_pairs={{0,16},{8,24},{16,0},{24,8},{1,17},{9,25},{17,1},{25,9},{2,18},{10... | collective-permute-start | bytes 2064392 | tf_op jit(solution)/shard_map/ppermute | solution.py:700
  559.1 10.4 %collective-permute-start.32 = (bf16[8,56,768]{2,1,0:T(8,128)(2,1)S(1)}, bf16[8,56,768]{2,1,0:T(8,128)(2,1)S(1)}, u32[]{:S(2)}, u32[]{:S(2)}) collective-permute-start(bf16[8,56,768]{2,1,0:T(8,128)(2,1)S(1)} %bitcast_dynamic-update-slice_fusion.refs_0_), channel_id=1, source_target_pairs={{0,8},{8,0},{16,24},{24,16},{1,9},{9,1},{17,25},{25,17},{2,10},{10... | collective-permute-start | bytes 2064392 | tf_op jit(solution)/shard_map/ppermute | solution.py:700
  577.6 13.8 %collective-permute-start.35 = (bf16[320,768]{1,0:T(8,128)(2,1)S(1)}, bf16[320,768]{1,0:T(8,128)(2,1)S(1)}, u32[]{:S(2)}, u32[]{:S(2)}) collective-permute-start(bf16[320,768]{1,0:T(8,128)(2,1)S(1)} %copy-done.9), channel_id=1, source_target_pairs={{0,16},{8,24},{16,0},{24,8},{1,17},{9,25},{17,1},{25,9},{2,18},{10... | collective-permute-start | bytes 1474568 | tf_op jit(solution)/shard_map/ppermute | solution.py:700
  579.1 27.0 %all-to-all-start = ((bf16[8,2,24,768]{3,2,1,0:T(8,128)(2,1)}), bf16[8,2,24,768]{3,2,1,0:T(8,128)(2,1)S(1)}, u32[]{:S(2)}, u32[]{:S(2)}) async-start(bf16[8,2,24,768]{3,2,1,0:T(8,128)(2,1)} %get-tuple-element.173), calls=%async_computation.2 | async-start | bytes 1179648 | tf_op jit(solution)/shard_map/all_to_all | solution.py:1144
  587.1 24.3 %collective-permute-start.42 = (bf16[320,768]{1,0:T(8,128)(2,1)S(1)}, bf16[320,768]{1,0:T(8,128)(2,1)S(1)}, u32[]{:S(2)}, u32[]{:S(2)}) collective-permute-start(bf16[320,768]{1,0:T(8,128)(2,1)S(1)} %copy-done.9), channel_id=1, source_target_pairs={{0,8},{8,0},{16,24},{24,16},{1,9},{9,1},{17,25},{25,17},{2,10},{10... | collective-permute-start | bytes 1474568 | tf_op jit(solution)/shard_map/ppermute | solution.py:700
  588.4 28.3 %collective-permute-start.43 = (f32[24,1000]{1,0:T(8,128)S(1)}, f32[24,1000]{1,0:T(8,128)}, u32[]{:S(2)}, u32[]{:S(2)}) collective-permute-start(f32[24,1000]{1,0:T(8,128)S(1)} %get-tuple-element.177.refs_1_), channel_id=1, source_target_pairs={{0,8},{8,0},{16,24},{24,16},{1,9},{9,1},{17,25},{25,17},{2,10},{10... | collective-permute-start | bytes 288008 | tf_op jit(solution)/shard_map/ppermute | solution.py:700
  591.4 14.6 %collective-permute-start.36 = (bf16[320,768]{1,0:T(8,128)(2,1)S(1)}, bf16[320,768]{1,0:T(8,128)(2,1)S(1)}, u32[]{:S(2)}, u32[]{:S(2)}) collective-permute-start(bf16[320,768]{1,0:T(8,128)(2,1)S(1)} %collective-permute-done.35.refs_4_), channel_id=1, source_target_pairs={{0,8},{8,0},{16,24},{24,16},{1,9},{9,1},{17,25},{25,17},{2,10},{10... | collective-permute-start | bytes 1474568 | tf_op jit(solution)/shard_map/ppermute | solution.py:700
  595.1 10.9 %collective-permute-start.38 = (f32[24,1000]{1,0:T(8,128)}, f32[24,1000]{1,0:T(8,128)S(1)}, u32[]{:S(2)}, u32[]{:S(2)}) collective-permute-start(f32[24,1000]{1,0:T(8,128)} %collective-permute-done.37.refs_3_), channel_id=1, source_target_pairs={{0,8},{8,0},{16,24},{24,16},{1,9},{9,1},{17,25},{25,17},{2,10},{10... | collective-permute-start | bytes 288008 | tf_op jit(solution)/shard_map/ppermute | solution.py:700
  609.6 16.5 %collective-permute-start.39 = (bf16[312,768]{1,0:T(8,128)(2,1)}, bf16[312,768]{1,0:T(8,128)(2,1)S(1)}, u32[]{:S(2)}, u32[]{:S(2)}) collective-permute-start(bf16[312,768]{1,0:T(8,128)(2,1)} %shard_map.333.refs_6_.refs_5_.refs_3_), channel_id=1, source_target_pairs={{0,8},{8,0},{16,24},{24,16},{1,9},{9,1},{17,25},{25,17},{2,10},{10... | collective-permute-start | bytes 1437704 | tf_op jit(solution)/shard_map/ppermute | solution.py:700
  609.7 13.5 %collective-permute-start.40 = (bf16[312,768]{1,0:T(8,128)(2,1)}, bf16[312,768]{1,0:T(8,128)(2,1)S(1)}, u32[]{:S(2)}, u32[]{:S(2)}) collective-permute-start(bf16[312,768]{1,0:T(8,128)(2,1)} %shard_map.333.refs_6_.refs_5_.refs_3_), channel_id=1, source_target_pairs={{0,16},{8,24},{16,0},{24,8},{1,17},{9,25},{17,1},{25,9},{2,18},{10... | collective-permute-start | bytes 1437704 | tf_op jit(solution)/shard_map/ppermute | solution.py:700
  (68 other events, 521.9 us)
Sparse Core Ops, SparseCore 0:
  63.9 88.2 all-gather.2
  155.7 53.3 all-gather.4
  225.8 100.7 reduce-scatter.2
  332.5 149.8 reduce-scatter.4

commit v6 on v5

--- a/solution.py
+++ b/solution.py
@@ -638,7 +638,7 @@
     )(core_at(), *arrays, *first)
 
 
-def embed_weight_kernel(at_ref, patch_ref, hot_ref, grad_ref, gain_ref, own_ref, sent_ref, total):
+def embed_weight_kernel(at_ref, patch_ref, hot_ref, grad_ref, norm_ref, gain_ref, own_ref, sent_ref, total):
     step = pl.program_id(0)
     grad = grad_ref[0]
     width = grad.shape[1]
@@ -657,18 +657,19 @@
 
     @pl.when(step == pl.num_programs(0) - 1)
     def _():
-        total[:, width + 128 :] = gain_ref[...]
+        gains = norm_ref[...] + gain_ref[...]
+        total[:, width + 128 :] = jnp.concatenate([gains, jnp.zeros((120, width), wide)], axis=0).T
         split_rows(total[...], own_ref, sent_ref, at_ref[0], 0)
 
 
-def embed_weight_call(patches, hot, grad, gain_columns, first=()):
+def embed_weight_call(patches, hot, grad, norm_gain, gain_rows, first=()):
     mb, _, width = grad.shape
     pixels = patches.shape[3]
     (x, y, z), part = split_shape(pixels)
     shape = (x, y, z, 1, part, width + 256)
     out = pl.BlockSpec(shape, lambda m, *_: (0,) * 6)
     return pl.pallas_call(
-        beside(embed_weight_kernel, 5, len(first)),
+        beside(embed_weight_kernel, 6, len(first)),
         grid_spec=pltpu.PrefetchScalarGridSpec(
             num_scalar_prefetch=1,
             grid=(mb,),
@@ -676,7 +677,8 @@
                 pl.BlockSpec((1, 1, ROWS, pixels), lambda m, *_: (m, 0, 0, 0)),
                 pl.BlockSpec((1, ROWS, hot.shape[2]), lambda m, *_: (m, 0, 0)),
                 pl.BlockSpec((1, ROWS, width), lambda m, *_: (m, 0, 0)),
-                pl.BlockSpec((width, 128), lambda m, *_: (0, 0)),
+                pl.BlockSpec((8, width), lambda m, *_: (0, 0)),
+                pl.BlockSpec((8, width), lambda m, *_: (0, 0)),
                 *anywhere(first),
             ],
             out_specs=[out, out],
@@ -685,7 +687,7 @@
         out_shape=[jax.ShapeDtypeStruct(shape, narrow)] * 2,
         compiler_params=params(),
         cost_estimate=cost(2 * grad.size * (pixels + 128), 12e6),
-    )(core_at(), patches, hot, grad, gain_columns, *first)
+    )(core_at(), patches, hot, grad, norm_gain, gain_rows, *first)
 
 
 def fold(parts):
@@ -985,6 +987,17 @@
     )(factor.reshape(1), grads, left, right, *first)
 
 
+def classifier_kernel(at_ref, factor_ref, weight_ref, first_ref, second_ref, *refs, count, part):
+    parts, outs = refs[:count], refs[count:]
+    for j, ref in enumerate(parts):
+        to = at_ref[1] ^ j
+        new = adam(
+            weight_ref[to], ref[...] * factor_ref[0], first_ref[to], second_ref[to], adam_rate, decay_rate
+        )
+        for out_ref, value in zip(outs, new):
+            out_ref[to] = value
+
+
 def update_kernel(at_ref, factor_ref, block_ref, *refs, count, part):
     parts, out_ref = refs[:count], refs[count]
     factor = factor_ref[0]
@@ -1118,10 +1131,10 @@
     late_y = Sum(late_x.after(d_embed), Y)
     d_gain_heads = jnp.concatenate([gain_one, gain_two], axis=0).transpose(1, 0, 2).reshape(8, width)
     d_gains = jnp.concatenate(
-        [d_gain_first[:1], d_gain_heads[:2], d_gain_rest[3:5], jnp.zeros((123, width), wide)], axis=0
-    ).T
+        [jnp.zeros((1, width), wide), d_gain_heads[:2], d_gain_rest[3:5], jnp.zeros((3, width), wide)], axis=0
+    )
     e_own, e_sent = embed_weight_call(
-        patches, hot, d_embed, d_gains, [own_rest, *late_y.sent, *mid_y.terms[1:]]
+        patches, hot, d_embed, d_gain_first, d_gains, [own_rest, *late_y.sent, *mid_y.terms[1:]]
     )
     head_sum = tied(head_sum, e_own) / weight_sum
     scalars = jnp.stack([weight_sum, jnp.sum(jnp.square(head_sum)), loss[0, 0]])
@@ -1151,13 +1164,6 @@
     block_grads, small_grad = finish_call(
         grads_kernel, factor, [], own_parts, part, [split, (size, part // 3, width)], [back]
     )
-    head_all = settled(
-        head_parts,
-        [(size, *head_sum.shape)],
-        [(j, (), 0, lambda f, s, j=j: j ^ s) for j in range(size)],
-        [back],
-    )[0].reshape(head.shape)
-
     small_grad = jnp.concatenate([small_grad[:, :, i * 256 : (i + 1) * 256] for i in range(3)], axis=1)
     small_grad = small_grad.reshape(lanes, 256).T
     table_grad = small_grad[: 2 * grid_rows].reshape(2, grid_rows, lanes)
@@ -1166,8 +1172,13 @@
         pos_table, table_grad, pos_first, pos_second, table_rate, decay_rate
     )
     gains_new, gain_first_new, gain_second_new = adam(gains, gain_grad, gain_first, gain_second, gain_rate, 0.0)
-    head_new, head_first_new, head_second_new = adam(
-        head, head_all * factor, head_first, head_second, adam_rate, decay_rate
+    head_shape = (size, *head_sum.shape)
+    head_new, head_first_new, head_second_new = (
+        x.reshape(head.shape)
+        for x in finish_call(
+            classifier_kernel, factor, [x.reshape(head_shape) for x in (head, head_first, head_second)], head_parts,
+            part, [head_shape] * 3, [back],
+        )
     )
     blocks_new = finish_call(
         update_kernel, factor, [blocks.reshape(split)], back_parts, part, [split],

time: 650 us -> 653 us (level)
  waiting for transfers between devices: 65.6 us -> 76.5 us
    ppermute x44, waiting for transfers between devices: 65.4 us -> 76.4 us  [swap(): lax.ppermute(x, axis, [(i, i ^ bits) for i in range(lax.axis_size(axis))])]
  transfers between devices with their start and end apart: 49 -> 49, of which waited for: 19 -> 19; matrix products, arithmetic and copies ran while one was open for 8% -> 7% of each run, Pallas kernels for 64% -> 63%
where the time goes in v6:
time: 653 us; the launch traced here: 648 us
  Pallas kernels  439 us (67%)
  waiting for transfers between devices  76.5 us (12%)
  starting transfers between devices  51.6 us (8%)
  other arithmetic  30.7 us (5%)
  local copies, waits for them, and re-layouts  28.6 us (4%)
  between operations  21.6 us (3%)
    pallas_call x2, Pallas kernels, attend_back_call(): pl.pallas_call(beside(attend_back_kernel, 12, len(first)), grid_spec=pltp...  107 us
    ppermute x44, waiting for transfers between devices, swap(): lax.ppermute(x, axis, [(i, i ^ bits) for i in range(lax.axis_size(axis))])  76.4 us
    pallas_call x1, Pallas kernels, backward_call(): pl.pallas_call(backward_kernel, grid_spec=pltpu.PrefetchScalarGridSpec(nu...  52.4 us
    pallas_call x1, Pallas kernels, attend_call(): pl.pallas_call(attend_kernel, grid_spec=pltpu.PrefetchScalarGridSpec(num_...  52.1 us
    pallas_call x1, Pallas kernels, forward_call(): pl.pallas_call(forward_kernel, grid_spec=pltpu.PrefetchScalarGridSpec(num...  51 us
    ppermute x44, starting transfers between devices, swap(): lax.ppermute(x, axis, [(i, i ^ bits) for i in range(lax.axis_size(axis))])  42.3 us
    pallas_call x1, Pallas kernels, weight_call(): pl.pallas_call(weight_kernel, grid=(9,), in_specs=[spec(one, lambda i: (j...  42.3 us
    pallas_call x2, Pallas kernels, one_weight_call(): pl.pallas_call(beside(functools.partial(one_weight_kernel, groups=[len(gr...  24.3 us
  transfers between devices with their start and end apart: 49, of which 19 were waited for; matrix products, arithmetic and copies ran while one was open for 7% of the time, Pallas kernels for 63%

profile of v6, /device:TPU:0, one launch (start us, length us, event | category | flops | bytes accessed | tf_op | source)
XLA Modules:
  0.0 647.7 jit_solution(2574892597469793174)
XLA Ops:
  38.5 5.8 collective-permute-done.1
  46.3 4.6 collective-permute-done.2
  52.6 8.6 %collective-permute-done.5.refs_3_ = bf16[8,24,1024]{2,1,0:T(8,128)(2,1)S(1)} collective-permute-done((bf16[8,24,1024]{2,1,0:T(8,128)(2,1)S(1)}, bf16[8,24,1024]{2,1,0:T(8,128)(2,1)S(1)}, u32[]{:S(2)}, u32[]{:S(2)}) %collective-permute-start.5) | collective-permute-done | bytes 393248 | tf_op jit(solution)/shard_map/ppermute | solution.py:702
  70.9 11.8 %shard_map.316 = (f32[2,1408,768]{2,1,0:T(8,128)}, bf16[2,1408,768]{2,1,0:T(8,128)(2,1)}) custom-call(bf16[2,1,1536,768]{3,2,1,0:T(8,128)(2,1)} %refs_1_.2, bf16[2,1408,128]{2,1,0:T(8,128)(2,1)} %add_convert_fusion.hot_ref.refs_2_, bf16[768,1024]{1,0:T(8,128)(2,1)} %bitcast.191, f32[8,768]{1,0:T(8,128)} %slice_convert_fusion.1.gain_ref.refs_10_.refs_9_), custom_call_target="tpu_custom_call" | custom-call | flops 3875536896 | bytes 20000000 | tf_op jit(solution)/shard_map/pallas_call | solution.py:89
  82.7 5.9 collective-permute-done.8.refs_3_
  91.2 4.3 shard_map.317
  95.5 22.7 %shard_map.318 = (bf16[2,1408,768]{2,1,0:T(8,128)(2,1)}, bf16[2,1408,768]{2,1,0:T(8,128)(2,1)}, bf16[2,1408,768]{2,1,0:T(8,128)(2,1)}, bf16[2,1408,768]{2,1,0:T(...) custom-call(bf16[2,1408,768]{2,1,0:T(8,128)(2,1)} %get-tuple-element.114.fi, ...), custom_call_target="tpu_custom_call" | custom-call | flops 9965666304 | bytes 30000000 | tf_op jit(solution)/shard_map/pallas_call | solution.py:135
  118.2 52.1 %shard_map.319 = (bf16[2,1408,768]{2,1,0:T(8,128)(2,1)}, f32[2,1408,128]{2,1,0:T(8,128)}) custom-call(s32[2,2]{1,0:T(2,128)} %bitcast.230, bf16[2,1408,768]{2,1,0:T(8,128)(2,1)} %get-tuple-element.116.q_ref.refs_1_, bf16[2,1408,768]{2,1,0:T(8,128)(2,1)} %get-tuple-element.117.k_ref.refs_2_, bf16[2,1408,768]{2,1,0:T(8,128)(2,1)} %get-tuple-element.118.v_ref.refs_3_), custom_call_target="tpu_custom_call" | custom-call | flops 34225520640 | bytes 17301504 | tf_op jit(solution)/shard_map/pallas_call | solution.py:197
  170.3 51.0 %shard_map.320 = (bf16[2,1408,768]{2,1,0:T(8,128)(2,1)}, bf16[4,2,1408,768]{3,2,1,0:T(8,128)(2,1)}, bf16[4,2,1408,768]{3,2,1,0:T(8,128)(2,1)}, bf16[2,1408,768]{...) custom-call(s32[2,2]{1,0:T(2,128)} %bitcast.231, ...), custom_call_target="tpu_custom_call" | custom-call | flops 29896998912 | bytes 80000000 | tf_op jit(solution)/shard_map/pallas_call | solution.py:261
  221.3 4.4 shard_map.321
  225.8 52.4 %shard_map.322 = (bf16[2,1408,768]{2,1,0:T(8,128)(2,1)}, bf16[4,2,1408,768]{3,2,1,0:T(8,128)(2,1)}, bf16[2,1408,768]{2,1,0:T(8,128)(2,1)}, bf16[2,1408,768]{2,1,...) custom-call(s32[2,2]{1,0:T(2,128)} %bitcast.232, f32[2,8,768]{2,1,0:T(8,128)} %bitcast.241, ...), custom_call_target="tpu_custom_call" | custom-call | flops 29896998912 | bytes 70000000 | tf_op jit(solution)/shard_map/pallas_call | solution.py:364
  278.1 42.3 %shard_map.323.refs_12_ = bf16[32,9,24,768]{3,2,1,0:T(8,128)(2,1)} custom-call(bf16[4,2,1408,768]{3,2,1,0:T(8,128)(2,1)} %get-tuple-element.136.act_ref, bf16[2,1408,768]{2,1,0:T(8,128)(2,1)} %get-tuple-element.137.dm_ref, bf16[2,1408,768]{2,1,0:T(8,128)(2,1)} %get-tuple-element.138.second_ref, bf16[4,2,1408,768]{3,2,1,0:T(8,128)(2,1)} %get-tuple-element.139.dup_ref, ...), custom_call_target="tpu_custom_call" | custom-call | flops 29896998912 | bytes 70000000 | tf_op jit(solution)/shard_map/pallas_call | solution.py:568
  323.8 70.4 %shard_map.324 = (bf16[2,1408,512]{2,1,0:T(8,128)(2,1)}, bf16[2,1408,512]{2,1,0:T(8,128)(2,1)}, bf16[2,1408,512]{2,1,0:T(8,128)(2,1)}, f32[4,8,128]{2,1,0:T(8,128)}) custom-call(s32[2,2]{1,0:T(2,128)} %bitcast.233, bf16[2,1408,768]{2,1,0:T(8,128)(2,1)} %get-tuple-element.116.q_ref.refs_1_, bf16[2,1408,768]{2,1,0:T(8,128)(2,1)} %get-tuple-element.117.k_ref.refs_2_, ...), custom_call_target="tpu_custom_call" | custom-call | flops 57042534400 | bytes 25952256 | tf_op jit(solution)/shard_map/pallas_call | solution.py:462
  394.2 13.4 %shard_map.325 = (bf16[2,2,4,1,24,1536]{5,4,3,2,1,0:T(8,128)(2,1)}, bf16[2,2,4,1,24,1536]{5,4,3,2,1,0:T(8,128)(2,1)}) custom-call(s32[1]{0:T(128)} %bitcast.38.refs_0_, bf16[2,1408,768]{2,1,0:T(8,128)(2,1)} %get-tuple-element.114.first_ref.refs_1_, bf16[2,1408,512]{2,1,0:T(8,128)(2,1)} %get-tuple-element.141.refs_2_.refs_0_, ...), custom_call_target="tpu_custom_call" | custom-call | flops 6643777536 | bytes 12000000 | tf_op jit(solution)/shard_map/pallas_call | solution.py:621
  414.7 36.9 %shard_map.326 = (bf16[2,1408,256]{2,1,0:T(8,128)(2,1)}, bf16[2,1408,256]{2,1,0:T(8,128)(2,1)}, bf16[2,1408,256]{2,1,0:T(8,128)(2,1)}, f32[2,8,128]{2,1,0:T(8,128)}) custom-call(s32[2,2]{1,0:T(2,128)} %bitcast.234, bf16[2,1408,768]{2,1,0:T(8,128)(2,1)} %get-tuple-element.116.q_ref.refs_1_, bf16[2,1408,768]{2,1,0:T(8,128)(2,1)} %get-tuple-element.117.k_ref.refs_2_, ...), custom_call_target="tpu_custom_call" | custom-call | flops 28521267200 | bytes 12976128 | tf_op jit(solution)/shard_map/pallas_call | solution.py:462
  452.5 11.0 %shard_map.327 = (bf16[2,2,4,1,24,768]{5,4,3,2,1,0:T(8,128)(2,1)}, bf16[2,2,4,1,24,768]{5,4,3,2,1,0:T(8,128)(2,1)}) custom-call(s32[1]{0:T(128)} %bitcast.38.refs_0_, bf16[2,1408,768]{2,1,0:T(8,128)(2,1)} %get-tuple-element.114.first_ref.refs_1_, bf16[2,1408,256]{2,1,0:T(8,128)(2,1)} %get-tuple-element.146.refs_2_.refs_3_, ...), custom_call_target="tpu_custom_call" | custom-call | flops 3321888768 | bytes 12000000 | tf_op jit(solution)/shard_map/pallas_call | solution.py:621
  469.1 21.4 %shard_map.328 = (bf16[2,1408,768]{2,1,0:T(8,128)(2,1)}, f32[8,768]{1,0:T(8,128)}) custom-call(bf16[2,1408,512]{2,1,0:T(8,128)(2,1)} %get-tuple-element.141.refs_2_.refs_0_, bf16[2,1408,512]{2,1,0:T(8,128)(2,1)} %get-tuple-element.142.refs_3_.refs_1_, bf16[2,1408,512]{2,1,0:T(8,128)(2,1)} %get-tuple-element.143.refs_4_.refs_2_, ...), custom_call_target="tpu_custom_call" | custom-call | flops 9965666304 | bytes 32000000 | tf_op jit(solution)/shard_map/pallas_call | solution.py:507
  492.1 9.6 %shard_map.329 = (bf16[2,2,4,1,24,1024]{5,4,3,2,1,0:T(8,128)(2,1)}, bf16[2,2,4,1,24,1024]{5,4,3,2,1,0:T(8,128)(2,1)}) custom-call(s32[1]{0:T(128)} %bitcast.38.refs_0_, bf16[2,1,1536,768]{3,2,1,0:T(8,128)(2,1)} %refs_1_.2, bf16[2,1408,128]{2,1,0:T(8,128)(2,1)} %add_convert_fusion.hot_ref.refs_2_, bf16[2,1408,768]{2,1,0:T(8,128)(2,1)} %get-tuple-element.152.refs_3_, ...), custom_call_target="tpu_custom_call" | custom-call | flops 3875536896 | bytes 12000000 | tf_op jit(solution)/shard_map/pallas_call | solution.py:671
  557.0 10.7 %collective-permute-done.33.refs_2_ = bf16[8,56,768]{2,1,0:T(8,128)(2,1)S(1)} collective-permute-done((bf16[8,56,768]{2,1,0:T(8,128)(2,1)S(1)}, bf16[8,56,768]{2,1,0:T(8,128)(2,1)S(1)}, u32[]{:S(2)}, u32[]{:S(2)}) %collective-permute-start.33) | collective-permute-done | bytes 688160 | tf_op jit(solution)/shard_map/ppermute | solution.py:702
  570.7 5.8 shard_map.332
  576.6 8.7 %all-to-all-start = ((bf16[8,2,24,768]{3,2,1,0:T(8,128)(2,1)}), bf16[8,2,24,768]{3,2,1,0:T(8,128)(2,1)S(1)}, u32[]{:S(2)}, u32[]{:S(2)}) async-start(bf16[8,2,24,768]{3,2,1,0:T(8,128)(2,1)} %get-tuple-element.176), calls=%async_computation.2 | async-start | bytes 1179648 | tf_op jit(solution)/shard_map/all_to_all | solution.py:1157
  586.1 12.3 %collective-permute-done.35.refs_4_ = bf16[320,768]{1,0:T(8,128)(2,1)S(1)} collective-permute-done((bf16[320,768]{1,0:T(8,128)(2,1)S(1)}, bf16[320,768]{1,0:T(8,128)(2,1)S(1)}, u32[]{:S(2)}, u32[]{:S(2)}) %collective-permute-start.35) | collective-permute-done | bytes 491552 | tf_op jit(solution)/shard_map/ppermute | solution.py:702
  612.4 8.4 %shard_map.335 = (f32[2,768,768]{2,1,0:T(8,128)}, f32[2,768,768]{2,1,0:T(8,128)}) custom-call(f32[1]{0:T(128)} %bitcast.91.refs_1_.refs_0_, bf16[2,768,768]{2,1,0:T(8,128)(2,1)} %get-tuple-element.178.refs_1_, f32[2,768,768]{2,1,0:T(8,128)} %refs_2_.1, f32[2,768,768]{2,1,0:T(8,128)} %refs_3_.1), custom_call_target="tpu_custom_call" | custom-call | flops 3623878656 | bytes 20000000 | tf_op jit(solution)/shard_map/pallas_call | solution.py:979
  633.4 5.3 shard_map.337
  (289 shorter events, 146.2 us)
Async XLA Ops:
  7.2 163.1 %all-gather.3.cloned.1.call-start = ((), (), s32[]{:S(2)}) async-start(), calls=%async_computation.3 | async-start | bytes 10948608 | tf_op jit(solution)/shard_map/all_gather | solution.py:1089
  20.7 25.6 %collective-permute-start.3 = (bf16[2,24,3328]{2,1,0:T(8,128)(2,1)S(1)}, bf16[2,24,3328]{2,1,0:T(8,128)(2,1)S(1)}, u32[]{:S(2)}, u32[]{:S(2)}) collective-permute-start(bf16[2,24,3328]{2,1,0:T(8,128)(2,1)S(1)} %pad_maximum_fusion.1), channel_id=1, source_target_pairs={{0,6},{1,7},{2,4},{3,5},{4,2},{5,3},{6,0},{7,1},{8,14},{9,15},{10,... | collective-permute-start | bytes 958472 | tf_op jit(solution)/shard_map/ppermute | solution.py:702
  24.6 26.4 %collective-permute-start.2 = (bf16[2,24,3328]{2,1,0:T(8,128)(2,1)S(1)}, bf16[2,24,3328]{2,1,0:T(8,128)(2,1)S(1)}, u32[]{:S(2)}, u32[]{:S(2)}) collective-permute-start(bf16[2,24,3328]{2,1,0:T(8,128)(2,1)S(1)} %pad_maximum_fusion.1), channel_id=1, source_target_pairs={{0,4},{1,5},{2,6},{3,7},{4,0},{5,1},{6,2},{7,3},{8,12},{9,13},{10,... | collective-permute-start | bytes 958472 | tf_op jit(solution)/shard_map/ppermute | solution.py:702
  24.6 19.7 %collective-permute-start.1 = (bf16[2,24,3328]{2,1,0:T(8,128)(2,1)S(1)}, bf16[2,24,3328]{2,1,0:T(8,128)(2,1)S(1)}, u32[]{:S(2)}, u32[]{:S(2)}) collective-permute-start(bf16[2,24,3328]{2,1,0:T(8,128)(2,1)S(1)} %pad_maximum_fusion.1), channel_id=1, source_target_pairs={{0,2},{1,3},{2,0},{3,1},{4,6},{5,7},{6,4},{7,5},{8,10},{9,11},{10,... | collective-permute-start | bytes 958472 | tf_op jit(solution)/shard_map/ppermute | solution.py:702
  63.8 157.5 %all-gather.5.cloned.1.call-start = ((), (), s32[]{:S(2)}) async-start(), calls=%async_computation.4 | async-start | bytes 1622016 | tf_op jit(solution)/shard_map/all_gather | solution.py:1090
  64.3 24.4 %collective-permute-start.8 = (bf16[8,24,2304]{2,1,0:T(8,128)(2,1)S(1)}, bf16[8,24,2304]{2,1,0:T(8,128)(2,1)S(1)}, u32[]{:S(2)}, u32[]{:S(2)}) collective-permute-start(bf16[8,24,2304]{2,1,0:T(8,128)(2,1)S(1)} %bitcast.186), channel_id=1, source_target_pairs={{0,16},{8,24},{16,0},{24,8},{1,17},{9,25},{17,1},{25,9},{2,18},{10... | collective-permute-start | bytes 2654216 | tf_op jit(solution)/shard_map/ppermute | solution.py:702
  66.5 22.5 %collective-permute-start.7 = (bf16[8,24,2304]{2,1,0:T(8,128)(2,1)S(1)}, bf16[8,24,2304]{2,1,0:T(8,128)(2,1)S(1)}, u32[]{:S(2)}, u32[]{:S(2)}) collective-permute-start(bf16[8,24,2304]{2,1,0:T(8,128)(2,1)S(1)} %bitcast.187), channel_id=1, source_target_pairs={{0,8},{8,0},{16,24},{24,16},{1,9},{9,1},{17,25},{25,17},{2,10},{10... | collective-permute-start | bytes 2654216 | tf_op jit(solution)/shard_map/ppermute | solution.py:702
  88.7 305.6 %reduce-scatter.3.cloned.1.call-start = ((), (), s32[]{:S(2)}) async-start(), calls=%async_computation.5 | async-start | bytes 3244032 | tf_op jit(solution)/shard_map/reduce_scatter | solution.py:1101
  225.7 265.6 %reduce-scatter.5.cloned.1.call-start = ((), (), s32[]{:S(2)}) async-start(), calls=%async_computation.6 | async-start | bytes 10948608 | tf_op jit(solution)/shard_map/reduce_scatter | solution.py:1107
  413.0 38.6 %collective-permute-start.11 = (bf16[2,4,1,24,1536]{4,3,1,2,0:T(8,128)(2,1)S(1)}, bf16[2,4,1,24,1536]{4,3,1,2,0:T(8,128)(2,1)S(1)}, u32[]{:S(2)}, u32[]{:S(2)}) collective-permute-start(bf16[2,4,1,24,1536]{4,3,1,2,0:T(8,128)(2,1)S(1)} %get-tuple-element.196), channel_id=1, source_target_pairs={{0,16},{8,24},{16,0},{24,8},{1,17},{9,25},{17,1},{25,9},{2,18},{10... | collective-permute-start | bytes 1769480 | tf_op jit(solution)/shard_map/ppermute | solution.py:702
  465.0 26.3 %collective-permute-start.14 = (bf16[4,1,24,1536]{3,2,1,0:T(8,128)(2,1)S(1)}, bf16[4,1,24,1536]{3,2,1,0:T(8,128)(2,1)S(1)}, u32[]{:S(2)}, u32[]{:S(2)}) collective-permute-start(bf16[4,1,24,1536]{3,2,1,0:T(8,128)(2,1)S(1)} %copy-done.18), channel_id=1, source_target_pairs={{0,1},{1,0},{2,3},{3,2},{4,5},{5,4},{6,7},{7,6},{8,9},{9,8},{10,11... | collective-permute-start | bytes 884744 | tf_op jit(solution)/shard_map/ppermute | solution.py:702
  468.4 22.2 %collective-permute-start.13 = (bf16[2,4,1,24,768]{4,3,1,2,0:T(8,128)(2,1)S(1)}, bf16[2,4,1,24,768]{4,3,1,2,0:T(8,128)(2,1)S(1)}, u32[]{:S(2)}, u32[]{:S(2)}) collective-permute-start(bf16[2,4,1,24,768]{4,3,1,2,0:T(8,128)(2,1)S(1)} %get-tuple-element.205), channel_id=1, source_target_pairs={{0,16},{8,24},{16,0},{24,8},{1,17},{9,25},{17,1},{25,9},{2,18},{10... | collective-permute-start | bytes 884744 | tf_op jit(solution)/shard_map/ppermute | solution.py:702
  505.5 11.2 %collective-permute-start.16 = (bf16[2,4,1,24,1024]{4,3,1,2,0:T(8,128)(2,1)S(1)}, bf16[2,4,1,24,1024]{4,3,1,2,0:T(8,128)(2,1)S(1)}, u32[]{:S(2)}, u32[]{:S(2)}) collective-permute-start(bf16[2,4,1,24,1024]{4,3,1,2,0:T(8,128)(2,1)S(1)} %get-tuple-element.201), channel_id=1, source_target_pairs={{0,16},{8,24},{16,0},{24,8},{1,17},{9,25},{17,1},{25,9},{2,18},{10... | collective-permute-start | bytes 1179656 | tf_op jit(solution)/shard_map/ppermute | solution.py:702
  542.6 10.5 %collective-permute-start.28 = (bf16[56,768]{1,0:T(8,128)(2,1)}, bf16[56,768]{1,0:T(8,128)(2,1)S(1)}, u32[]{:S(2)}, u32[]{:S(2)}) collective-permute-start(bf16[56,768]{1,0:T(8,128)(2,1)} %get-tuple-element.171), channel_id=1, source_target_pairs={{0,4},{1,5},{2,6},{3,7},{4,0},{5,1},{6,2},{7,3},{8,12},{9,13},{10,... | collective-permute-start | bytes 258056 | tf_op jit(solution)/shard_map/ppermute | solution.py:702
  543.6 12.3 %collective-permute-start.29 = (bf16[56,768]{1,0:T(8,128)(2,1)}, bf16[56,768]{1,0:T(8,128)(2,1)S(1)}, u32[]{:S(2)}, u32[]{:S(2)}) collective-permute-start(bf16[56,768]{1,0:T(8,128)(2,1)} %get-tuple-element.172), channel_id=1, source_target_pairs={{0,5},{1,4},{2,7},{3,6},{4,1},{5,0},{6,3},{7,2},{8,13},{9,12},{10,... | collective-permute-start | bytes 258056 | tf_op jit(solution)/shard_map/ppermute | solution.py:702
  545.1 10.7 %collective-permute-start.30 = (bf16[56,768]{1,0:T(8,128)(2,1)}, bf16[56,768]{1,0:T(8,128)(2,1)S(1)}, u32[]{:S(2)}, u32[]{:S(2)}) collective-permute-start(bf16[56,768]{1,0:T(8,128)(2,1)} %get-tuple-element.173), channel_id=1, source_target_pairs={{0,6},{1,7},{2,4},{3,5},{4,2},{5,3},{6,0},{7,1},{8,14},{9,15},{10,... | collective-permute-start | bytes 258056 | tf_op jit(solution)/shard_map/ppermute | solution.py:702
  555.9 11.8 %collective-permute-start.33 = (bf16[8,56,768]{2,1,0:T(8,128)(2,1)S(1)}, bf16[8,56,768]{2,1,0:T(8,128)(2,1)S(1)}, u32[]{:S(2)}, u32[]{:S(2)}) collective-permute-start(bf16[8,56,768]{2,1,0:T(8,128)(2,1)S(1)} %bitcast_dynamic-update-slice_fusion.refs_0_), channel_id=1, source_target_pairs={{0,16},{8,24},{16,0},{24,8},{1,17},{9,25},{17,1},{25,9},{2,18},{10... | collective-permute-start | bytes 2064392 | tf_op jit(solution)/shard_map/ppermute | solution.py:702
  557.0 10.7 %collective-permute-start.32 = (bf16[8,56,768]{2,1,0:T(8,128)(2,1)S(1)}, bf16[8,56,768]{2,1,0:T(8,128)(2,1)S(1)}, u32[]{:S(2)}, u32[]{:S(2)}) collective-permute-start(bf16[8,56,768]{2,1,0:T(8,128)(2,1)S(1)} %bitcast_dynamic-update-slice_fusion.refs_0_), channel_id=1, source_target_pairs={{0,8},{8,0},{16,24},{24,16},{1,9},{9,1},{17,25},{25,17},{2,10},{10... | collective-permute-start | bytes 2064392 | tf_op jit(solution)/shard_map/ppermute | solution.py:702
  576.6 31.6 %all-to-all-start = ((bf16[8,2,24,768]{3,2,1,0:T(8,128)(2,1)}), bf16[8,2,24,768]{3,2,1,0:T(8,128)(2,1)S(1)}, u32[]{:S(2)}, u32[]{:S(2)}) async-start(bf16[8,2,24,768]{3,2,1,0:T(8,128)(2,1)} %get-tuple-element.176), calls=%async_computation.2 | async-start | bytes 1179648 | tf_op jit(solution)/shard_map/all_to_all | solution.py:1157
  585.3 13.0 %collective-permute-start.35 = (bf16[320,768]{1,0:T(8,128)(2,1)S(1)}, bf16[320,768]{1,0:T(8,128)(2,1)S(1)}, u32[]{:S(2)}, u32[]{:S(2)}) collective-permute-start(bf16[320,768]{1,0:T(8,128)(2,1)S(1)} %copy-done.9), channel_id=1, source_target_pairs={{0,16},{8,24},{16,0},{24,8},{1,17},{9,25},{17,1},{25,9},{2,18},{10... | collective-permute-start | bytes 1474568 | tf_op jit(solution)/shard_map/ppermute | solution.py:702
  598.4 22.8 %collective-permute-start.42 = (bf16[320,768]{1,0:T(8,128)(2,1)S(1)}, bf16[320,768]{1,0:T(8,128)(2,1)S(1)}, u32[]{:S(2)}, u32[]{:S(2)}) collective-permute-start(bf16[320,768]{1,0:T(8,128)(2,1)S(1)} %copy-done.9), channel_id=1, source_target_pairs={{0,8},{8,0},{16,24},{24,16},{1,9},{9,1},{17,25},{25,17},{2,10},{10... | collective-permute-start | bytes 1474568 | tf_op jit(solution)/shard_map/ppermute | solution.py:702
  599.6 27.4 %collective-permute-start.43 = (f32[24,1000]{1,0:T(8,128)S(1)}, f32[24,1000]{1,0:T(8,128)S(1)}, u32[]{:S(2)}, u32[]{:S(2)}) collective-permute-start(f32[24,1000]{1,0:T(8,128)S(1)} %get-tuple-element.180.refs_5_), channel_id=1, source_target_pairs={{0,8},{8,0},{16,24},{24,16},{1,9},{9,1},{17,25},{25,17},{2,10},{10... | collective-permute-start | bytes 288008 | tf_op jit(solution)/shard_map/ppermute | solution.py:702
  611.8 14.6 %collective-permute-start.40 = (bf16[312,768]{1,0:T(8,128)(2,1)}, bf16[312,768]{1,0:T(8,128)(2,1)S(1)}, u32[]{:S(2)}, u32[]{:S(2)}) collective-permute-start(bf16[312,768]{1,0:T(8,128)(2,1)} %shard_map.333.refs_6_.refs_9_.refs_3_), channel_id=1, source_target_pairs={{0,16},{8,24},{16,0},{24,8},{1,17},{9,25},{17,1},{25,9},{2,18},{10... | collective-permute-start | bytes 1437704 | tf_op jit(solution)/shard_map/ppermute | solution.py:702
  620.9 11.6 %collective-permute-start.39 = (bf16[312,768]{1,0:T(8,128)(2,1)S(1)}, bf16[312,768]{1,0:T(8,128)(2,1)S(1)}, u32[]{:S(2)}, u32[]{:S(2)}) collective-permute-start(bf16[312,768]{1,0:T(8,128)(2,1)S(1)} %copy-done), channel_id=1, source_target_pairs={{0,8},{8,0},{16,24},{24,16},{1,9},{9,1},{17,25},{25,17},{2,10},{10... | collective-permute-start | bytes 1437704 | tf_op jit(solution)/shard_map/ppermute | solution.py:702
  (71 other events, 536.2 us)
Sparse Core Ops, SparseCore 0:
  63.9 88.2 all-gather.2
  155.7 53.3 all-gather.4
  225.8 100.6 reduce-scatter.2
  332.5 149.7 reduce-scatter.4
